TPU v7x, 128 devices: a whole 4x4x4 slice. The times are simulated.
128 devices in a mesh: dp: 16 (over x, z_hi, core), tensor: 8 (over z_lo, y).
Axes of the slice: x: 4, y: 4, z: 4 (z_hi: 2, z_lo: 2; z = z_hi * 2 + z_lo), core: 2. Of those that a mesh axis runs over, the one named last changes fastest.
Arguments:
- hidden_in: bfloat16 [16384, 4096], P(('dp', 'tensor')), may hold values from -6 to 6
- block_output_gradient: bfloat16 [16384, 4096], P(('dp', 'tensor')), may hold values from -6 to 6
- rms_norm_gain: float32 [4096], replicated, may hold values from 0.25 to 1.75
- routes: int32 [16384, 1], P(('dp', 'tensor')), may hold values from 0 to 31; in each aligned block of 128 rows (0 to 127, 128 to 255, ...) at most 6 rows name the same one
- route_weights: bfloat16 [16384, 1], P(('dp', 'tensor')), may hold values from 0.099609375 to 1
- w_gate: bfloat16 [32, 1536, 4096], P('dp', 'tensor'), may hold values from -0.09375 to 0.09375
- w_up: bfloat16 [32, 1536, 4096], P('dp', 'tensor'), may hold values from -0.09375 to 0.09375
- w_down: bfloat16 [32, 1536, 4096], P('dp', 'tensor'), may hold values from -0.15625 to 0.15625
Outputs:
- block_input_gradient: bfloat16 [16384, 4096], P(('dp', 'tensor'))
- norm_gain_gradient: float32 [4096], replicated
- grad_routes: float32 [16384, 1], P(('dp', 'tensor'))
- grad_gate: bfloat16 [32, 1536, 4096], P('dp', 'tensor')
- grad_up: bfloat16 [32, 1536, 4096], P('dp', 'tensor')
- grad_down: bfloat16 [32, 1536, 4096], P('dp', 'tensor')
Inputs may be any that keep to these rules, and one draw needn't show every extreme that they name: Each row names one expert. In each aligned block of 128 rows (the rows of one device) no expert is named by more than 6 routes, a bound that some block reaches.
All inputs are finite; a program needn't handle non-finite values.
Results may differ from a plain program's by a relative error of at most 0.0075.
Values may be sent and summed in bfloat16 or wider, within the bound.
No kernel may reach another device: no remote copies, remote signals or barrier semaphores. Data moves between devices by JAX's collectives and lax.ppermute only.
A program may use at most 192 MiB of HBM per device.

v0:
```python
import jax
import jax.numpy as jnp
from jax import lax
from jax.sharding import PartitionSpec as P

EPS = 1e-06


def place(blocks, cap, count):
    nb = blocks.shape[0]
    onehot = (blocks[..., None] == jnp.arange(count, dtype=jnp.int32)).astype(jnp.int32)
    before = jnp.sum((jnp.cumsum(onehot, axis=1) - onehot) * onehot, axis=-1)
    return blocks * (nb * cap) + jnp.arange(nb, dtype=jnp.int32)[:, None] * cap + before


def fill_slots(flat, total, rows_h, rows_dy, rows_w, per_token):
    width = rows_h.shape[1]
    token_of = jnp.arange(flat.shape[0], dtype=jnp.int32) // per_token
    hbuf = jnp.zeros((total, width), jnp.bfloat16).at[flat].set(rows_h[token_of])
    dybuf = jnp.zeros((total, width), jnp.bfloat16).at[flat].set(rows_dy[token_of])
    wbuf = jnp.zeros((total,), jnp.bfloat16).at[flat].set(rows_w.reshape(-1))
    return (hbuf, dybuf, wbuf)


def expert_backward(rows_h, rows_dy, rows_w, w_gate, w_up, w_down):
    gate = jnp.einsum("erd,efd->erf", rows_h, w_gate, preferred_element_type=jnp.float32)
    up = jnp.einsum("erd,efd->erf", rows_h, w_up, preferred_element_type=jnp.float32)
    back = jnp.einsum("erd,efd->erf", rows_dy, w_down, preferred_element_type=jnp.float32)
    sig = jax.nn.sigmoid(gate)
    silu = gate * sig
    act = silu * up
    weight = rows_w.astype(jnp.float32)[..., None]
    dact = weight * back
    dgate = (dact * up * sig * (1.0 + gate * (1.0 - sig))).astype(jnp.bfloat16)
    dup = (dact * silu).astype(jnp.bfloat16)
    actw = (weight * act).astype(jnp.bfloat16)
    part_w = jnp.sum(act * back, axis=-1).astype(jnp.bfloat16)
    part_h = jnp.einsum("erf,efd->erd", dgate, w_gate, preferred_element_type=jnp.float32)
    part_h = part_h + jnp.einsum("erf,efd->erd", dup, w_up, preferred_element_type=jnp.float32)
    part_h = part_h.astype(jnp.bfloat16)
    grad_g = jnp.einsum("erf,erd->efd", dgate, rows_h, preferred_element_type=jnp.float32)
    grad_u = jnp.einsum("erf,erd->efd", dup, rows_h, preferred_element_type=jnp.float32)
    grad_d = jnp.einsum("erf,erd->efd", actw, rows_dy, preferred_element_type=jnp.float32)
    return (
        part_h,
        part_w,
        grad_g.astype(jnp.bfloat16),
        grad_u.astype(jnp.bfloat16),
        grad_d.astype(jnp.bfloat16),
    )


def copies(buffer, n_data, n_slices, exp_dev, cap):
    tail = buffer.shape[1:]
    shaped = buffer.reshape((n_data, 1, exp_dev, cap) + tail)
    spread = jnp.broadcast_to(shaped, (n_data, n_slices, exp_dev, cap) + tail)
    return spread.reshape((n_data * n_slices, exp_dev, cap) + tail)


def body(
    hidden_in, block_output_gradient, rms_norm_gain, routes, route_weights, w_gate, w_up, w_down
):
    tok_count = hidden_in.shape[0]
    per_token = routes.shape[1]
    width = hidden_in.shape[1]
    n_data = lax.axis_size("dp")
    n_slices = lax.axis_size("tensor")
    exp_dev = w_gate.shape[0]
    experts = exp_dev * n_data
    cap = tok_count * per_token * 3 // (2 * experts)
    expert_values = hidden_in.astype(jnp.float32)
    inverse_rms_scale = lax.rsqrt(
        jnp.mean(expert_values * expert_values, axis=-1, keepdims=True) + EPS
    )
    unit_scaled_input = expert_values * inverse_rms_scale
    normalized_input = (unit_scaled_input * rms_norm_gain).astype(jnp.bfloat16)
    flat = place(routes.reshape(1, tok_count * per_token), cap, experts).reshape(-1)
    hbuf, dybuf, wbuf = fill_slots(
        flat, experts * cap, normalized_input, block_output_gradient, route_weights, per_token
    )
    send_h = copies(hbuf, n_data, n_slices, exp_dev, cap)
    send_dy = copies(dybuf, n_data, n_slices, exp_dev, cap)
    send_w = copies(wbuf, n_data, n_slices, exp_dev, cap)
    got_h, got_dy, got_w = (
        lax.all_to_all(send_h, ("dp", "tensor"), split_axis=0, concat_axis=2, tiled=True),
        lax.all_to_all(send_dy, ("dp", "tensor"), split_axis=0, concat_axis=2, tiled=True),
        lax.all_to_all(send_w, ("dp", "tensor"), split_axis=0, concat_axis=2, tiled=True),
    )
    rows_h = got_h.reshape(exp_dev, -1, width)
    rows_dy = got_dy.reshape(exp_dev, -1, width)
    rows_w = got_w.reshape(exp_dev, -1)
    part_h, part_w, grad_g, grad_u, grad_d = expert_backward(
        rows_h, rows_dy, rows_w, w_gate, w_up, w_down
    )
    back_h, back_w = (
        lax.all_to_all(
            part_h.reshape(1, exp_dev, -1, width),
            ("dp", "tensor"),
            split_axis=2,
            concat_axis=0,
            tiled=True,
        ),
        lax.all_to_all(
            part_w.reshape(1, exp_dev, -1),
            ("dp", "tensor"),
            split_axis=2,
            concat_axis=0,
            tiled=True,
        ),
    )
    summed_h = jnp.sum(
        back_h.reshape(n_data, n_slices, exp_dev, cap, width), axis=1, dtype=jnp.float32
    )
    summed_w = jnp.sum(back_w.reshape(n_data, n_slices, exp_dev, cap), axis=1, dtype=jnp.float32)
    slot_h = summed_h.reshape(experts * cap, width)[flat]
    normalized_input_gradient = jnp.sum(slot_h.reshape(tok_count, per_token, width), axis=1)
    grad_routes = summed_w.reshape(-1)[flat].reshape(tok_count, per_token)
    norm_gain_gradient = lax.psum(
        jnp.sum(normalized_input_gradient * unit_scaled_input, axis=0), ("dp", "tensor")
    )
    unit_input_gradient = normalized_input_gradient * rms_norm_gain
    expert_mixture = jnp.mean(unit_input_gradient * unit_scaled_input, axis=-1, keepdims=True)
    block_input_gradient = (
        block_output_gradient.astype(jnp.float32)
        + inverse_rms_scale * (unit_input_gradient - unit_scaled_input * expert_mixture)
    ).astype(jnp.bfloat16)
    return (block_input_gradient, norm_gain_gradient, grad_routes, grad_g, grad_u, grad_d)


def solution(mesh):
    in_specs = (
        P(("dp", "tensor"), None),
        P(("dp", "tensor"), None),
        P(),
        P(("dp", "tensor"), None),
        P(("dp", "tensor"), None),
        P("dp", "tensor", None),
        P("dp", "tensor", None),
        P("dp", "tensor", None),
    )
    out_specs = (
        P(("dp", "tensor"), None),
        P(),
        P(("dp", "tensor"), None),
        P("dp", "tensor", None),
        P("dp", "tensor", None),
        P("dp", "tensor", None),
    )
    return jax.shard_map(body, mesh=mesh, in_specs=in_specs, out_specs=out_specs, check_vma=False)
```

profile of v0, /device:TPU:1, one launch (start us, length us, event | category | flops | bytes accessed | tf_op | source)
XLA Modules:
  0.0 791.9 jit_solution(8960347083708593748)
XLA Ops:
  5.5 11.5 %all-to-all-start = ((bf16[128,2,6]{2,1,0:T(2,128)(2,1)}), bf16[128,2,6]{2,1,0:T(2,128)(2,1)S(1)}, u32[]{:S(2)}, u32[]{:S(2)}) async-start(bf16[128,2,6]{2,1,0:T(2,128)(2,1)} %bitcast.4), calls=%async_computation | async-start | bytes 131072 | tf_op jit(solution)/shard_map/all_to_all | solution.py:87
  21.6 6.4 scatter_custom_fusion.2
  28.0 3.5 broadcast_in_dim.19
  31.4 4.4 copy.54
  35.8 13.9 %broadcast_in_dim.20 = bf16[16,8,2,6,4096]{4,2,3,1,0:T(2,128)(2,1)} broadcast(bf16[16,2,6,4096]{3,1,2,0:T(2,128)(2,1)} %copy.54), dimensions={0,2,3,4} | broadcast | bytes 14155776 | tf_op jit(solution)/shard_map/broadcast_in_dim | solution.py:56
  49.7 10.8 %all-to-all-start.2 = ((bf16[128,2,6,4096]{3,1,2,0:T(2,128)(2,1)}), bf16[128,2,6,4096]{3,1,2,0:T(2,128)(2,1)}, u32[]{:S(2)}, u32[]{:S(2)}) async-start(bf16[128,2,6,4096]{3,1,2,0:T(2,128)(2,1)} %bitcast.57), calls=%async_computation.2 | async-start | bytes 25165824 | tf_op jit(solution)/shard_map/all_to_all | solution.py:85
  60.5 6.3 scatter_custom_fusion.1
  66.8 3.5 broadcast_in_dim.17
  70.3 4.4 copy.52
  74.7 152.8 %all-to-all-done.2 = bf16[128,2,6,4096]{3,1,2,0:T(2,128)(2,1)} async-done(((bf16[128,2,6,4096]{3,1,2,0:T(2,128)(2,1)}), bf16[128,2,6,4096]{3,1,2,0:T(2,128)(2,1)}, u32[]{:S(2)}, u32[]{:S(2)}) %all-to-all-start.2) | async-done | bytes 12582944 | tf_op jit(solution)/shard_map/all_to_all | solution.py:85
  227.5 13.8 %broadcast_in_dim.18 = bf16[16,8,2,6,4096]{4,2,3,1,0:T(2,128)(2,1)} broadcast(bf16[16,2,6,4096]{3,1,2,0:T(2,128)(2,1)} %copy.52), dimensions={0,2,3,4} | broadcast | bytes 14155776 | tf_op jit(solution)/shard_map/broadcast_in_dim | solution.py:56
  241.3 12.0 %all-to-all-start.1 = ((bf16[128,2,6,4096]{3,1,2,0:T(2,128)(2,1)}), bf16[128,2,6,4096]{3,1,2,0:T(2,128)(2,1)}, u32[]{:S(2)}, u32[]{:S(2)}) async-start(bf16[128,2,6,4096]{3,1,2,0:T(2,128)(2,1)} %bitcast.56), calls=%async_computation.1 | async-start | bytes 25165824 | tf_op jit(solution)/shard_map/all_to_all | solution.py:86
  253.6 20.6 %fusion.9 = f32[2,768,192]{1,2,0:T(8,128)} fusion(bf16[2,192,4096]{2,1,0:T(8,128)(2,1)S(1)} %copy-done, bf16[2,768,4096]{2,0,1:T(2,128)(2,1)} %bitcast.14), kind=kOutput, calls=%fused_computation.17 | convolution fusion | flops 2415919104 | bytes 16908288 | tf_op jit(solution)/shard_map/erd,efd->erf/dot_general | solution.py:26
  274.2 21.8 %fusion.11 = f32[2,768,192]{1,2,0:T(8,128)} fusion(bf16[2,192,4096]{2,1,0:T(8,128)(2,1)} %param.14, bf16[2,768,4096]{2,0,1:T(2,128)(2,1)} %bitcast.14), kind=kOutput, calls=%fused_computation.19 | convolution fusion | flops 2415919104 | bytes 16908288 | tf_op jit(solution)/shard_map/erd,efd->erf/dot_general | solution.py:27
  296.0 122.7 %all-to-all-done.1 = bf16[128,2,6,4096]{3,1,2,0:T(2,128)(2,1)} async-done(((bf16[128,2,6,4096]{3,1,2,0:T(2,128)(2,1)}), bf16[128,2,6,4096]{3,1,2,0:T(2,128)(2,1)}, u32[]{:S(2)}, u32[]{:S(2)}) %all-to-all-start.1) | async-done | bytes 12582944 | tf_op jit(solution)/shard_map/all_to_all | solution.py:86
  418.7 22.7 %multiply_reduce_fusion = (bf16[2,768]{1,0:T(2,128)(2,1)S(1)}, bf16[2,768,192]{1,2,0:T(8,128)(2,1)}, bf16[2,768,192]{1,2,0:T(8,128)(2,1)}) fusion(f32[2,768,192]{1,2,0:T(8,128)} %fusion.11, f32[2,768,192]{1,2,0:T(8,128)} %fusion.9, f32[2,768]{1,0:T(2,128)S(1)} %reshape.212, bf16[2,192,4096]{2,1,0:T(8,128)(2,1)} %param.15, bf16[2,768,4096]{2,0,1:T(2,128)(2,1)} %bitcast.10), kind=kOutput, calls=%fused_computation.39 | convolution fusion | flops 2420931072 | bytes 19276800 | tf_op jit(solution)/shard_map/erd,efd->erf/dot_general | solution.py:28
  442.5 11.7 %all-to-all-start.4 = ((bf16[1,2,768]{1,0,2:T(2,128)(2,1)}), bf16[1,2,768]{1,0,2:T(2,128)(2,1)S(1)}, u32[]{:S(2)}, u32[]{:S(2)}) async-start(bf16[1,2,768]{1,0,2:T(2,128)(2,1)} %copy.59), calls=%async_computation.4 | async-start | bytes 786432 | tf_op jit(solution)/shard_map/all_to_all | solution.py:103
  454.2 11.2 %fusion.48 = f32[2,768,4096]{2,1,0:T(8,128)} fusion(bf16[2,768,192]{1,2,0:T(8,128)(2,1)} %get-tuple-element.9, bf16[2,192,4096]{2,1,0:T(8,128)(2,1)S(1)} %copy-done), kind=kOutput, calls=%fused_computation.67 | convolution fusion | flops 2415919104 | bytes 28901376 | tf_op jit(solution)/shard_map/erf,efd->erd/dot_general | solution.py:38
  465.4 16.1 %fusion = bf16[1,2,768,4096]{3,2,1,0:T(8,128)(2,1)} fusion(f32[2,768,4096]{2,1,0:T(8,128)} %fusion.48, bf16[2,768,192]{1,2,0:T(8,128)(2,1)} %get-tuple-element.10, bf16[2,192,4096]{2,1,0:T(8,128)(2,1)} %param.14), kind=kOutput, calls=%fused_computation.8 | convolution fusion | flops 2428502016 | bytes 41484288 | tf_op jit(solution)/shard_map/erf,efd->erd/dot_general | solution.py:39
  481.4 23.7 %copy.57 = bf16[1,2,768,4096]{3,1,0,2:T(2,128)(2,1)} copy(bf16[1,2,768,4096]{3,2,1,0:T(8,128)(2,1)} %fusion) | data formatting | bytes 25165824 | tf_op jit(solution)/shard_map/reshape | solution.py:97
  505.1 10.6 %all-to-all-start.3 = ((bf16[1,2,768,4096]{3,1,0,2:T(2,128)(2,1)}), bf16[1,2,768,4096]{3,1,0,2:T(2,128)(2,1)}, u32[]{:S(2)}, u32[]{:S(2)}) async-start(bf16[1,2,768,4096]{3,1,0,2:T(2,128)(2,1)} %copy.57), calls=%async_computation.3 | async-start | bytes 25165824 | tf_op jit(solution)/shard_map/all_to_all | solution.py:96
  515.8 20.9 %fusion.13 = bf16[2,192,4096]{2,1,0:T(8,128)(2,1)} fusion(bf16[2,768,192]{1,2,0:T(8,128)(2,1)S(1)} %copy-done.2, bf16[2,768,4096]{2,0,1:T(2,128)(2,1)} %bitcast.14), kind=kOutput, calls=%fused_computation.21 | convolution fusion | flops 2417491968 | bytes 16318464 | tf_op jit(solution)/shard_map/erf,erd->efd/dot_general | solution.py:41
  536.7 21.1 %fusion.16 = bf16[2,192,4096]{2,1,0:T(8,128)(2,1)} fusion(bf16[2,768,192]{1,2,0:T(8,128)(2,1)S(1)} %copy-done.3, bf16[2,768,4096]{2,0,1:T(2,128)(2,1)} %bitcast.14), kind=kOutput, calls=%fused_computation.22 | convolution fusion | flops 2417491968 | bytes 16318464 | tf_op jit(solution)/shard_map/erf,erd->efd/dot_general | solution.py:42
  557.8 21.3 %fusion.19 = bf16[2,192,4096]{2,1,0:T(8,128)(2,1)} fusion(bf16[2,768,4096]{2,0,1:T(2,128)(2,1)} %bitcast.10, f32[2,768]{1,0:T(2,128)S(1)} %reshape.212, f32[2,768,192]{1,2,0:T(8,128)S(1)} %copy-done.8, f32[2,768,192]{1,2,0:T(8,128)S(1)} %copy-done.7), kind=kOutput, calls=%fused_computation.23 | convolution fusion | flops 2419556352 | bytes 18094080 | tf_op jit(solution)/shard_map/erf,erd->efd/dot_general | solution.py:43
  581.5 99.4 %all-to-all-done.3 = bf16[1,2,768,4096]{3,1,0,2:T(2,128)(2,1)} async-done(((bf16[1,2,768,4096]{3,1,0,2:T(2,128)(2,1)}), bf16[1,2,768,4096]{3,1,0,2:T(2,128)(2,1)}, u32[]{:S(2)}, u32[]{:S(2)}) %all-to-all-start.3) | async-done | bytes 12582944 | tf_op jit(solution)/shard_map/all_to_all | solution.py:96
  680.8 13.5 %convert.10 = f32[1,2,128,6,4096]{4,1,3,2,0:T(2,128)} convert(bf16[1,2,128,6,4096]{4,1,3,2,0:T(2,128)(2,1)} %bitcast.28) | non-fusion elementwise | flops 6291456 | bytes 37748736 | tf_op jit(solution)/shard_map/convert_element_type | solution.py:111
  694.3 12.8 %reduce_sum.72 = f32[16,2,6,4096]{3,1,2,0:T(2,128)S(1)} reduce(f32[16,8,2,6,4096]{4,2,3,1,0:T(2,128)} %bitcast.55, f32[]{:T(128)} %constant.15.clone.1), dimensions={1}, to_apply=%region_6.7 | reduce | flops 5505024 | bytes 28311556 | tf_op jit(solution)/shard_map/reduce_sum | solution.py:111
  707.0 4.2 copy.58
  711.2 3.0 reshape.209
  714.3 2.6 gather_fusion
  719.4 68.3 %psum.7 = f32[4096]{0:T(1024)} all-reduce(f32[4096]{0:T(1024)S(1)} %get-tuple-element.6), channel_id=1, replica_groups=mesh['dp'=16,'tensor'=8] {'dp','tensor'}, use_global_device_ids=true, to_apply=%region_9.10 | all-reduce | flops 4096 | bytes 32768 | tf_op jit(solution)/shard_map/psum | solution.py:118
  787.7 4.0 fusion.31
  (45 shorter events, 15.6 us)
Async XLA Ops:
  0.6 252.9 %copy-start = (bf16[2,192,4096]{2,1,0:T(8,128)(2,1)S(1)}, bf16[2,192,4096]{2,1,0:T(8,128)(2,1)}, u32[]{:S(2)}) copy-start(bf16[2,192,4096]{2,1,0:T(8,128)(2,1)} %param.13) | copy-start | bytes 9437188
  5.5 30.3 %all-to-all-start = ((bf16[128,2,6]{2,1,0:T(2,128)(2,1)}), bf16[128,2,6]{2,1,0:T(2,128)(2,1)S(1)}, u32[]{:S(2)}, u32[]{:S(2)}) async-start(bf16[128,2,6]{2,1,0:T(2,128)(2,1)} %bitcast.4), calls=%async_computation | async-start | bytes 131072 | tf_op jit(solution)/shard_map/all_to_all | solution.py:87
  18.5 0.5 copy-start.5
  49.7 177.8 %all-to-all-start.2 = ((bf16[128,2,6,4096]{3,1,2,0:T(2,128)(2,1)}), bf16[128,2,6,4096]{3,1,2,0:T(2,128)(2,1)}, u32[]{:S(2)}, u32[]{:S(2)}) async-start(bf16[128,2,6,4096]{3,1,2,0:T(2,128)(2,1)} %bitcast.57), calls=%async_computation.2 | async-start | bytes 25165824 | tf_op jit(solution)/shard_map/all_to_all | solution.py:85
  241.3 177.3 %all-to-all-start.1 = ((bf16[128,2,6,4096]{3,1,2,0:T(2,128)(2,1)}), bf16[128,2,6,4096]{3,1,2,0:T(2,128)(2,1)}, u32[]{:S(2)}, u32[]{:S(2)}) async-start(bf16[128,2,6,4096]{3,1,2,0:T(2,128)(2,1)} %bitcast.56), calls=%async_computation.1 | async-start | bytes 25165824 | tf_op jit(solution)/shard_map/all_to_all | solution.py:86
  442.5 62.7 %all-to-all-start.4 = ((bf16[1,2,768]{1,0,2:T(2,128)(2,1)}), bf16[1,2,768]{1,0,2:T(2,128)(2,1)S(1)}, u32[]{:S(2)}, u32[]{:S(2)}) async-start(bf16[1,2,768]{1,0,2:T(2,128)(2,1)} %copy.59), calls=%async_computation.4 | async-start | bytes 786432 | tf_op jit(solution)/shard_map/all_to_all | solution.py:103
  505.1 10.6 %copy-start.2 = (bf16[2,768,192]{1,2,0:T(8,128)(2,1)S(1)}, bf16[2,768,192]{1,2,0:T(8,128)(2,1)}, u32[]{:S(2)}) copy-start(bf16[2,768,192]{1,2,0:T(8,128)(2,1)} %get-tuple-element.9) | copy-start | bytes 1769476
  505.1 175.7 %all-to-all-start.3 = ((bf16[1,2,768,4096]{3,1,0,2:T(2,128)(2,1)}), bf16[1,2,768,4096]{3,1,0,2:T(2,128)(2,1)}, u32[]{:S(2)}, u32[]{:S(2)}) async-start(bf16[1,2,768,4096]{3,1,0,2:T(2,128)(2,1)} %copy.57), calls=%async_computation.3 | async-start | bytes 25165824 | tf_op jit(solution)/shard_map/all_to_all | solution.py:96
  515.7 21.0 %copy-start.3 = (bf16[2,768,192]{1,2,0:T(8,128)(2,1)S(1)}, bf16[2,768,192]{1,2,0:T(8,128)(2,1)}, u32[]{:S(2)}) copy-start(bf16[2,768,192]{1,2,0:T(8,128)(2,1)} %get-tuple-element.10) | copy-start | bytes 1769476
  536.7 21.1 %copy-start.7 = (f32[2,768,192]{1,2,0:T(8,128)S(1)}, f32[2,768,192]{1,2,0:T(8,128)}, u32[]{:S(2)}) copy-start(f32[2,768,192]{1,2,0:T(8,128)} %fusion.9) | copy-start | bytes 3538948
  536.7 21.1 %copy-start.8 = (f32[2,768,192]{1,2,0:T(8,128)S(1)}, f32[2,768,192]{1,2,0:T(8,128)}, u32[]{:S(2)}) copy-start(f32[2,768,192]{1,2,0:T(8,128)} %fusion.11) | copy-start | bytes 3538948
  714.2 2.6 copy-start.4
  714.2 2.6 copy-start.6
  787.6 4.0 copy-start.1
where the time goes:
time: 800 us; the launch traced here: 792 us
  waiting for transfers between devices  375 us (47%)
  matrix products  156 us (20%)
  local copies, waits for them, and re-layouts  96 us (12%)
  blocking collectives  68.3 us (9%)
  starting transfers between devices  56.6 us (7%)
  other arithmetic  39.5 us (5%)
    all_to_all x1, waiting for transfers between devices, body(): lax.all_to_all(send_h, ('dp', 'tensor'), split_axis=0, concat_axis=2, til...  153 us
    all_to_all x1, waiting for transfers between devices, body(): lax.all_to_all(send_dy, ('dp', 'tensor'), split_axis=0, concat_axis=2, ti...  123 us
    all_to_all x1, waiting for transfers between devices, body(): lax.all_to_all(part_h.reshape(1, exp_dev, -1, width), ('dp', 'tensor'), s...  99.4 us
    psum x1, blocking collectives, body(): lax.psum(jnp.sum(normalized_input_gradient * unit_scaled_input, axis=0),...  68.3 us
    broadcast_in_dim x8, local copies, waits for them, and re-layouts, copies(): spread = jnp.broadcast_to(shaped, (n_data, n_slices, exp_dev, cap) + tail)  44.2 us
    reshape x1, local copies, waits for them, and re-layouts, body(): part_h.reshape(1, exp_dev, -1, width)  23.7 us
    dot_general x1, matrix products, expert_backward(): jnp.einsum('erd,efd->erf', rows_dy, w_down, preferred_element_type=jnp.fl...  22.7 us
    dot_general x1, matrix products, expert_backward(): jnp.einsum('erd,efd->erf', rows_h, w_up, preferred_element_type=jnp.float32)  21.8 us
  transfers between devices with their start and end apart: 5, of which 3 were waited for; matrix products, arithmetic and copies ran while one was open for 24% of the time, Pallas kernels for 0%

commit v1 on v0

v1 whole, which is shorter than its diff:
```python
import jax
import jax.numpy as jnp
import numpy as np
from jax import lax
from jax.experimental import pallas as pl
from jax.experimental.pallas import tpu as pltpu
from jax.sharding import PartitionSpec as P

EPS = 1e-06
TOK = 128
D = 4096
CAP = 6
N_DP = 16
SLICE = 192
ROWS = N_DP * CAP
ALL = 8 * ROWS
WIDE_A = 2304
WIDE_B = D - WIDE_A
EXTRA = 256
CHUNK = 256
STEP = 1024
VMEM = 56 * 1024 * 1024
F32 = jnp.float32
BF16 = jnp.bfloat16


def params():
    return pltpu.CompilerParams(vmem_limit_bytes=VMEM)


def whole(shape):
    return pl.BlockSpec(shape, lambda *_: (0,) * len(shape))


def dot(a, b):
    return jnp.dot(a, b, preferred_element_type=F32)


def dot_nt(a, b):
    return lax.dot_general(a, b, (((1,), (1,)), ((), ())), preferred_element_type=F32)


def iota(shape, dim):
    return lax.broadcasted_iota(jnp.int32, shape, dim)


def dispatch_kernel(h_ref, c_ref, gain_ref, rcol_ref, rrow_ref, w_ref, out_ref, scale_ref, pick_ref):
    @pl.when(pl.program_id(0) == 0)
    def _():
        x = h_ref[...].astype(F32)
        scale_ref[...] = lax.rsqrt(jnp.mean(x * x, axis=-1, keepdims=True) + EPS)
        same = rcol_ref[...] == rrow_ref[...]
        earlier = iota((TOK, TOK), 0) < iota((TOK, TOK), 1)
        rank = jnp.sum(jnp.where(same & earlier, 1, 0), axis=0, keepdims=True)
        expert = rrow_ref[...]
        slot = (expert >> 1) * (4 * CAP) + (expert & 1) * CAP + rank
        rows = iota((N_DP * 4 * CAP, TOK), 0)
        pick_ref[:, :TOK] = jnp.where(rows == slot, 1.0, 0.0).astype(BF16)
        pick_ref[:, TOK:] = jnp.where(rows == slot + 2 * CAP, 1.0, 0.0).astype(BF16)

    cols = pl.ds(pl.multiple_of(pl.program_id(0) * 512, 512), 512)
    v = (h_ref[:, cols].astype(F32) * scale_ref[...] * gain_ref[...]).astype(BF16)
    c = (c_ref[:, cols].astype(F32) * w_ref[...].astype(F32)).astype(BF16)
    out_ref[...] = dot(pick_ref[...], jnp.concatenate([v, c], axis=0)).astype(BF16)


def dispatch(h, c, gain, rcol, rrow, w):
    rows = N_DP * 4 * CAP
    return pl.pallas_call(
        dispatch_kernel,
        grid=(D // 512,),
        in_specs=[
            whole((TOK, D)),
            whole((TOK, D)),
            pl.BlockSpec((1, 512), lambda j: (0, j)),
            whole((TOK, 1)),
            whole((1, TOK)),
            whole((TOK, 1)),
        ],
        out_specs=pl.BlockSpec((rows, 512), lambda j: (0, j)),
        out_shape=jax.ShapeDtypeStruct((rows, D), BF16),
        scratch_shapes=[pltpu.VMEM((TOK, 1), F32), pltpu.VMEM((rows, 2 * TOK), BF16)],
        compiler_params=params(),
        name="dispatch",
    )(h, c, gain, rcol, rrow, w)


def sort_matrix():
    out = np.zeros((4 * ROWS, 4 * ROWS), np.float32)
    for kind in range(4):
        for src in range(N_DP):
            for k in range(CAP):
                out[kind * ROWS + src * CAP + k, src * 4 * CAP + kind * CAP + k] = 1.0
    return out


def sort_kernel(m_ref, x_ref, *outs):
    for kind, out in enumerate(outs):
        rows = m_ref[kind * ROWS : (kind + 1) * ROWS, :]
        out[...] = dot(rows, x_ref[...]).astype(BF16)


def sort_rows(x):
    n = 4 * ROWS
    return pl.pallas_call(
        sort_kernel,
        grid=(D // 512,),
        in_specs=[whole((n, n)), pl.BlockSpec((n, 512), lambda j: (0, j))],
        out_specs=[pl.BlockSpec((ROWS, 512), lambda j: (0, j))] * 4,
        out_shape=[jax.ShapeDtypeStruct((ROWS, D), BF16)] * 4,
        compiler_params=params(),
        name="sort_rows",
    )(jnp.asarray(sort_matrix(), BF16), x)


def up(x):
    return lax.ppermute(x, "tensor", [(t, t // 4 * 4 + (t + 1) % 4) for t in range(8)])


def down(x):
    return lax.ppermute(x, "tensor", [(t, t // 4 * 4 + (t + 3) % 4) for t in range(8)])


def over(x):
    return lax.ppermute(x, "tensor", [(t, (t + 4) % 8) for t in range(8)])


def gather_z_first(h):
    hz = over(h)
    h1, h3 = up(h), down(h)
    z1, z3 = up(hz), down(hz)
    return [h, h1, up(h1), h3, hz, z1, down(z3), z3]


def gather_y_first(c, mirror):
    c1, c3 = up(c), down(c)
    c2 = down(c3) if mirror else up(c1)
    near = [c, c1, c2, c3]
    return near + [over(x) for x in near]


def add(a, b):
    return (a.astype(F32) + b.astype(F32)).astype(BF16)


def reduce_y(q, mirror):
    if mirror:
        return q[0], down(add(q[1], down(q[2]))), up(q[3])
    return q[0], up(add(q[3], up(q[2]))), down(q[1])


def reduce_y_first(p):
    near = reduce_y(p[:4], False)
    a, b, c = reduce_y(p[4:], True)
    far = (a.astype(F32) + b.astype(F32) + c.astype(F32)).astype(BF16)
    return near + (over(far),)


def reduce_z_first(p, mirror):
    return reduce_y([add(p[k], over(p[4 + k])) for k in range(4)], mirror)


def rows_kernel(*refs):
    hs, cs = refs[:8], refs[8:16]
    gate_ref, up_ref, down_ref, gate2_ref, up2_ref = refs[16:21]
    outs_a, outs_b = refs[21:29], refs[29:37]
    dgu_t_ref, act_t_ref = refs[37:39]
    acc_g, acc_u, acc_b, dgu_ref, pw_ref = refs[39:]
    s = pl.program_id(0)
    first = D // STEP
    n_a = WIDE_A // CHUNK
    n_b = WIDE_B // CHUNK

    @pl.when(s < first)
    def _():
        h = jnp.concatenate([r[...] for r in hs], axis=0)
        c = jnp.concatenate([r[...] for r in cs], axis=0)
        g = dot_nt(h, gate_ref[0])
        u = dot_nt(h, up_ref[0])
        b = dot_nt(c, down_ref[0])

        @pl.when(s == 0)
        def _():
            acc_g[...] = g
            acc_u[...] = u
            acc_b[...] = b

        @pl.when(s > 0)
        def _():
            acc_g[...] += g
            acc_u[...] += u
            acc_b[...] += b

    @pl.when(s == first - 1)
    def _():
        gate, upp, back = acc_g[...], acc_u[...], acc_b[...]
        sig = jax.nn.sigmoid(gate)
        silu = gate * sig
        act = silu * upp
        dgate = back * upp * sig * (1.0 + gate * (1.0 - sig))
        dup = back * silu
        dgu_ref[:, :SLICE] = dgate.astype(BF16)
        dgu_ref[:, SLICE:] = dup.astype(BF16)
        dgu_t_ref[:SLICE, :] = dgate.T.astype(BF16)
        dgu_t_ref[SLICE:, :] = dup.T.astype(BF16)
        act_t_ref[...] = act.T.astype(BF16)
        pw_ref[...] = jnp.sum(act * back, axis=-1, keepdims=True)

    def part():
        w = jnp.concatenate([gate2_ref[0], up2_ref[0]], axis=0)
        return dot(dgu_ref[...], w).astype(BF16)

    def put(outs, value):
        for k, out in enumerate(outs):
            out[...] = value[k * ROWS : (k + 1) * ROWS]

    @pl.when((s >= first) & (s < first + n_a))
    def _():
        put(outs_a, part())

    @pl.when((s >= first + n_a) & (s < first + n_a + n_b))
    def _():
        put(outs_b, part())

    @pl.when(s == first + n_a + n_b)
    def _():
        pw = pw_ref[...]
        high = pw.astype(BF16).astype(F32)
        lane = iota((ALL, EXTRA), 1)
        value = jnp.where(lane == 0, high, jnp.where(lane == 1, pw - high, 0.0))
        put(outs_b, value.astype(BF16))


def expert_rows(e, hs, cs, w_gate, w_up, w_down):
    first = D // STEP
    n_a = WIDE_A // CHUNK
    n_b = WIDE_B // CHUNK
    n = n_a + n_b
    head = lambda s: jnp.minimum(s, first - 1)
    tail = lambda s: jnp.clip(s - first, 0, n - 1)
    rows = pl.BlockSpec((ROWS, STEP), lambda s: (0, head(s)))
    weight = pl.BlockSpec((1, SLICE, STEP), lambda s: (e, 0, head(s)))
    again = pl.BlockSpec((1, SLICE, CHUNK), lambda s: (e, 0, tail(s)))
    out_a = pl.BlockSpec((ROWS, CHUNK), lambda s: (0, jnp.clip(s - first, 0, n_a - 1)))
    out_b = pl.BlockSpec((ROWS, CHUNK), lambda s: (0, jnp.clip(s - first - n_a, 0, n_b)))
    out = pl.pallas_call(
        rows_kernel,
        grid=(first + n + 1,),
        in_specs=[rows] * 16 + [weight] * 3 + [again] * 2,
        out_specs=[out_a] * 8 + [out_b] * 8 + [whole((2 * SLICE, ALL)), whole((SLICE, ALL))],
        out_shape=[jax.ShapeDtypeStruct((ROWS, WIDE_A), BF16)] * 8
        + [jax.ShapeDtypeStruct((ROWS, WIDE_B + EXTRA), BF16)] * 8
        + [jax.ShapeDtypeStruct((2 * SLICE, ALL), BF16), jax.ShapeDtypeStruct((SLICE, ALL), BF16)],
        scratch_shapes=[
            pltpu.VMEM((ALL, SLICE), F32),
            pltpu.VMEM((ALL, SLICE), F32),
            pltpu.VMEM((ALL, SLICE), F32),
            pltpu.VMEM((ALL, 2 * SLICE), BF16),
            pltpu.VMEM((ALL, 1), F32),
        ],
        compiler_params=params(),
        cost_estimate=pl.CostEstimate(
            flops=2 * ALL * SLICE * D * 5, bytes_accessed=26 << 20, transcendentals=ALL * SLICE
        ),
        name="expert_rows",
    )(*hs, *cs, w_gate, w_up, w_down, w_gate, w_up)
    return out[:8], out[8:16], out[16], out[17]


def weights_kernel(*refs):
    hs, cs = refs[:8], refs[8:16]
    dgu_t_ref, act_t_ref, gate_ref, up_ref = refs[16:20]
    gg_ref, gu_ref, gd_ref, norm_ref = refs[-4:]
    h = jnp.concatenate([r[...] for r in hs], axis=0)
    c = jnp.concatenate([r[...] for r in cs], axis=0)
    gu = dot(dgu_t_ref[...], h)
    gg_ref[0] = gu[:SLICE].astype(BF16)
    gu_ref[0] = gu[SLICE:].astype(BF16)
    gd_ref[0] = dot(act_t_ref[...], c).astype(BF16)
    norm = gu[:SLICE] * gate_ref[0].astype(F32) + gu[SLICE:] * up_ref[0].astype(F32)
    norm_ref[...] = jnp.sum(norm, axis=0, keepdims=True)


def expert_weights(e, hs, cs, dgu_t, act_t, w_gate, w_up, before):
    rows = pl.BlockSpec((ROWS, 512), lambda j: (0, j))
    weight = pl.BlockSpec((1, SLICE, 512), lambda j: (e, 0, j))
    grad = jax.ShapeDtypeStruct((2, SLICE, D), BF16)
    return pl.pallas_call(
        weights_kernel,
        grid=(D // 512,),
        in_specs=[rows] * 16
        + [whole((2 * SLICE, ALL)), whole((SLICE, ALL)), weight, weight]
        + [pl.BlockSpec(memory_space=pl.ANY)] * len(before),
        out_specs=[weight] * 3 + [pl.BlockSpec((1, 512), lambda j: (0, j))],
        out_shape=[grad] * 3 + [jax.ShapeDtypeStruct((1, D), F32)],
        input_output_aliases={20 + k: k for k in range(len(before))},
        compiler_params=params(),
        cost_estimate=pl.CostEstimate(
            flops=2 * ALL * SLICE * D * 3, bytes_accessed=18 << 20, transcendentals=0
        ),
        name="expert_weights",
    )(*hs, *cs, dgu_t, act_t, w_gate, w_up, *before)


def pack_matrices():
    rows = np.zeros((N_DP * 16, 2 * ROWS), np.float32)
    lanes = np.zeros((2 * ROWS, 128), np.float32)
    high = np.zeros((N_DP * 16, 2 * ROWS), np.float32)
    low = np.zeros((N_DP * 16, 2 * ROWS), np.float32)
    for e in range(2):
        for src in range(N_DP):
            for k in range(CAP):
                s = e * ROWS + src * CAP + k
                rows[src * 16 + e * CAP + k, s] = 1.0
                lanes[s, e * CAP + k] = 1.0
                high[src * 16 + 2 * CAP, s] = 1.0
                low[src * 16 + 2 * CAP + 1, s] = 1.0
    return rows, lanes, high, low


def pack_kernel(*refs):
    rows_ref, lanes_ref, high_ref, low_ref = refs[:4]
    a0, a1, b0, b1 = refs[4:8], refs[8:12], refs[12:15], refs[15:18]
    out_ref = refs[18]

    def total(parts, cols):
        value = parts[0][:, cols].astype(F32)
        for p in parts[1:]:
            value = value + p[:, cols].astype(F32)
        return value

    def both(first, second, cols):
        return jnp.concatenate([total(first, cols), total(second, cols)], axis=0)

    rows = rows_ref[...]
    for j in range(WIDE_A // CHUNK):
        cols = slice(j * CHUNK, (j + 1) * CHUNK)
        out_ref[:, cols] = dot(rows, both(a0, a1, cols).astype(BF16)).astype(BF16)
    for j in range(WIDE_B // CHUNK):
        cols = slice(j * CHUNK, (j + 1) * CHUNK)
        value = dot(rows, both(b0, b1, cols).astype(BF16)).astype(BF16)
        out_ref[:, WIDE_A + j * CHUNK : WIDE_A + (j + 1) * CHUNK] = value
    pw = both(b0, b1, slice(WIDE_B, WIDE_B + 128))
    pw = pw[:, 0:1] + pw[:, 1:2]
    top = pw.astype(BF16).astype(F32)
    spread = lanes_ref[...].astype(F32)
    value = dot(high_ref[...], (top * spread).astype(BF16))
    value = value + dot(low_ref[...], ((pw - top) * spread).astype(BF16))
    out_ref[:, :128] = (out_ref[:, :128].astype(F32) + value).astype(BF16)


def pack(a0, a1, b0, b1):
    mats = [jnp.asarray(m, BF16) for m in pack_matrices()]
    return pl.pallas_call(
        pack_kernel,
        out_shape=jax.ShapeDtypeStruct((N_DP * 16, D), BF16),
        compiler_params=params(),
        name="pack_rows",
    )(*mats, *a0, *a1, *b0, *b1)


def combine_kernel(r_ref, h_ref, c_ref, gain_ref, rcol_ref, rrow_ref, w_ref, out_ref, routes_ref):
    same = rcol_ref[...] == rrow_ref[...]
    earlier = iota((TOK, TOK), 1) < iota((TOK, TOK), 0)
    rank = jnp.sum(jnp.where(same & earlier, 1, 0), axis=1, keepdims=True)
    expert = rcol_ref[...]
    place = (expert & 1) * CAP + rank
    base = (expert >> 1) * 16
    cols = iota((TOK, N_DP * 16), 1)

    def choose(index):
        return jnp.where(cols == index, 1.0, 0.0).astype(BF16)

    pw = dot(choose(base + 2 * CAP), r_ref[:, :128]) + dot(choose(base + 2 * CAP + 1), r_ref[:, :128])
    pw = jnp.sum(jnp.where(iota((TOK, 128), 1) == place, pw, 0.0), axis=1, keepdims=True)
    routes_ref[...] = pw / w_ref[...].astype(F32)
    g = dot(choose(base + place), r_ref[...])
    x = h_ref[...].astype(F32)
    scale = lax.rsqrt(jnp.mean(x * x, axis=-1, keepdims=True) + EPS)
    x = x * scale
    dx = g * gain_ref[...]
    mix = jnp.mean(dx * x, axis=-1, keepdims=True)
    out_ref[...] = (c_ref[...].astype(F32) + scale * (dx - x * mix)).astype(BF16)


def combine(r, h, c, gain, rcol, rrow, w):
    return pl.pallas_call(
        combine_kernel,
        out_shape=[
            jax.ShapeDtypeStruct((TOK, D), BF16),
            jax.ShapeDtypeStruct((TOK, 1), F32),
        ],
        compiler_params=params(),
        name="combine",
    )(r, h, c, gain, rcol, rrow, w)


def body(h, c, gain, routes, w, w_gate, w_up, w_down):
    gain = gain.reshape(1, D)
    rrow = routes.reshape(1, TOK)
    slots = dispatch(h, c, gain, routes, rrow, w)
    got = lax.all_to_all(
        slots.reshape(N_DP, 4 * CAP, D), "dp", split_axis=0, concat_axis=0, tiled=True
    )
    h0, h1, c0, c1 = sort_rows(got.reshape(4 * ROWS, D))
    hs0, cs0 = gather_z_first(h0), gather_y_first(c0, False)
    hs1, cs1 = gather_z_first(h1), gather_y_first(c1, True)
    pa0, pb0, dgu0, act0 = expert_rows(0, hs0, cs0, w_gate, w_up, w_down)
    pa1, pb1, dgu1, act1 = expert_rows(1, hs1, cs1, w_gate, w_up, w_down)
    a0, b0 = reduce_y_first(pa0), reduce_z_first(pb0, False)
    a1, b1 = reduce_y_first(pa1), reduce_z_first(pb1, True)
    *grads, norm0 = expert_weights(0, hs0, cs0, dgu0, act0, w_gate, w_up, ())
    gg, gu, gd, norm1 = expert_weights(1, hs1, cs1, dgu1, act1, w_gate, w_up, grads)
    norm = lax.psum(((norm0 + norm1) / gain).reshape(D), ("dp", "tensor"))
    packed = pack(a0, a1, b0, b1)
    back = lax.all_to_all(packed.reshape(N_DP, 16, D), "dp", split_axis=0, concat_axis=0, tiled=True)
    out, grad_routes = combine(back.reshape(N_DP * 16, D), h, c, gain, routes, rrow, w)
    return out, norm, grad_routes, gg, gu, gd


def solution(mesh):
    tokens = P(("dp", "tensor"), None)
    weights = P("dp", "tensor", None)
    return jax.shard_map(
        body,
        mesh=mesh,
        in_specs=(tokens, tokens, P(), tokens, tokens, weights, weights, weights),
        out_specs=(tokens, P(), tokens, weights, weights, weights),
        check_vma=False,
    )
```

time: 800 us -> 515 us (0.64)
  waiting for transfers between devices: 375 us -> 204 us
  matrix products: 156 us -> 0 us
  Pallas kernels: 0 us -> 96.6 us
  local copies, waits for them, and re-layouts: 96 us -> 7.38 us
  blocking collectives: 68.3 us -> 114 us
  other arithmetic: 39.5 us -> 3.88 us
  starting transfers between devices: 56.6 us -> 86.7 us
    all_to_all x5 -> x1, waiting for transfers between devices: 375 us -> 0.01 us  [body(): lax.all_to_all(packed.reshape(N_DP, 16, D), 'dp', split_axis=0, concat_ax...]
    ppermute x0 -> x56, waiting for transfers between devices: none -> 204 us  [the longest x18 130 us: up(): lax.ppermute(x, 'tensor', [(t, t // 4 * 4 + (t + 1) % 4) for t in range(8)])]
    dot_general x8 -> x0, matrix products: 156 us -> none  [the longest x1 22.7 us: expert_backward(): jnp.einsum('erd,efd->erf', rows_dy, w_down, preferred_element_type=jnp.fl...]
    pallas_call x0 -> x8, Pallas kernels: none -> 96.6 us  [the longest x2 48.6 us: expert_rows(): pl.pallas_call(rows_kernel, grid=(first + n + 1,), in_specs=[rows] * 16 +...]
    ppermute x0 -> x56, starting transfers between devices: none -> 63.8 us  [the longest x18 37.4 us: down(): lax.ppermute(x, 'tensor', [(t, t // 4 * 4 + (t + 3) % 4) for t in range(8)])]
    all_to_all x0 -> x1, blocking collectives: none -> 48.5 us  [body(): lax.all_to_all(slots.reshape(N_DP, 4 * CAP, D), 'dp', split_axis=0, conca...]
    broadcast_in_dim x8 -> x0, local copies, waits for them, and re-layouts: 44.2 us -> none  [copies(): spread = jnp.broadcast_to(shaped, (n_data, n_slices, exp_dev, cap) + tail)]
    all_to_all x5 -> x1, starting transfers between devices: 56.6 us -> 22.9 us  [body(): lax.all_to_all(packed.reshape(N_DP, 16, D), 'dp', split_axis=0, concat_ax...]
  transfers between devices with their start and end apart: 5 -> 57, of which waited for: 3 -> 25; matrix products, arithmetic and copies ran while one was open for 24% -> 1% of each run, Pallas kernels for 0% -> 14%
where the time goes in v1:
time: 515 us; the launch traced here: 513 us
  waiting for transfers between devices  204 us (40%)
  blocking collectives  114 us (22%)
  Pallas kernels  96.6 us (19%)
  starting transfers between devices  86.7 us (17%)
  local copies, waits for them, and re-layouts  7.38 us (1%)
    ppermute x18, waiting for transfers between devices, up(): lax.ppermute(x, 'tensor', [(t, t // 4 * 4 + (t + 1) % 4) for t in range(8)])  130 us
    psum x1, blocking collectives, body(): norm = lax.psum(((norm0 + norm1) / gain).reshape(D), ('dp', 'tensor'))  65.2 us
    pallas_call x2, Pallas kernels, expert_rows(): pl.pallas_call(rows_kernel, grid=(first + n + 1,), in_specs=[rows] * 16 +...  48.6 us
    all_to_all x1, blocking collectives, body(): lax.all_to_all(slots.reshape(N_DP, 4 * CAP, D), 'dp', split_axis=0, conca...  48.5 us
    ppermute x20, waiting for transfers between devices, over(): return lax.ppermute(x, 'tensor', [(t, (t + 4) % 8) for t in range(8)])  38.8 us
    ppermute x18, starting transfers between devices, down(): lax.ppermute(x, 'tensor', [(t, t // 4 * 4 + (t + 3) % 4) for t in range(8)])  37.4 us
    ppermute x18, waiting for transfers between devices, down(): lax.ppermute(x, 'tensor', [(t, t // 4 * 4 + (t + 3) % 4) for t in range(8)])  34.9 us
    pallas_call x2, Pallas kernels, expert_weights(): pl.pallas_call(weights_kernel, grid=(D // 512,), in_specs=[rows] * 16 + [...  23.3 us
  transfers between devices with their start and end apart: 57, of which 25 were waited for; matrix products, arithmetic and copies ran while one was open for 1% of the time, Pallas kernels for 14%

profile of v1, /device:TPU:1, one launch (start us, length us, event | category | flops | bytes accessed | tf_op | source)
XLA Modules:
  0.0 513.1 jit_solution(1660386043810557189)
XLA Ops:
  3.4 7.0 %dispatch.1 = bf16[384,4096]{1,0:T(8,128)(2,1)} custom-call(bf16[128,4096]{1,0:T(8,128)(2,1)} %h_ref.3, bf16[128,4096]{1,0:T(8,128)(2,1)} %c_ref.3, f32[1,4096]{1,0:T(1,128)} %bitcast.11, s32[128,1]{1,0:T(8,128)} %copy.22.rcol_ref, s32[1,128]{1,0:T(1,128)} %bitcast.15, bf16[128,1]{1,0:T(8,128)(2,1)} %copy.23.w_ref), custom_call_target="tpu_custom_call" | custom-call | tf_op jit(solution)/shard_map/dispatch/pallas_call | solution.py:69
  10.4 48.5 %all_to_all.10 = bf16[16,24,4096]{2,1,0:T(8,128)(2,1)} all-to-all(bf16[16,24,4096]{2,1,0:T(8,128)(2,1)} %bitcast.8), channel_id=1, replica_groups=mesh['dp'=16,'tensor'=8] {'dp'}, dimensions={0} | all-to-all | bytes 6291456 | tf_op jit(solution)/shard_map/all_to_all | solution.py:402
  58.9 7.3 %sort_rows.1 = (bf16[96,4096]{1,0:T(8,128)(2,1)}, bf16[96,4096]{1,0:T(8,128)(2,1)}, bf16[96,4096]{1,0:T(8,128)(2,1)}, bf16[96,4096]{1,0:T(8,128)(2,1)}) custom-call(bf16[384,384]{1,0:T(8,128)(2,1)} %constant.10.clone.m_ref, bf16[384,4096]{1,0:T(8,128)(2,1)} %bitcast.7), custom_call_target="tpu_custom_call" | custom-call | tf_op jit(solution)/shard_map/sort_rows/pallas_call | solution.py:105
  72.3 13.0 %collective-permute-done.refs_1_ = bf16[96,4096]{1,0:T(8,128)(2,1)S(1)} collective-permute-done((bf16[96,4096]{1,0:T(8,128)(2,1)}, bf16[96,4096]{1,0:T(8,128)(2,1)S(1)}, u32[]{:S(2)}, u32[]{:S(2)}) %collective-permute-start) | collective-permute-done | bytes 786464 | tf_op jit(solution)/shard_map/ppermute | solution.py:117
  88.8 13.4 %collective-permute-done.7.refs_9_ = bf16[96,4096]{1,0:T(8,128)(2,1)S(1)} collective-permute-done((bf16[96,4096]{1,0:T(8,128)(2,1)}, bf16[96,4096]{1,0:T(8,128)(2,1)S(1)}, u32[]{:S(2)}, u32[]{:S(2)}) %collective-permute-start.7) | collective-permute-done | bytes 786464 | tf_op jit(solution)/shard_map/ppermute | solution.py:117
  105.7 13.4 %collective-permute-done.21.refs_1_ = bf16[96,4096]{1,0:T(8,128)(2,1)S(1)} collective-permute-done((bf16[96,4096]{1,0:T(8,128)(2,1)}, bf16[96,4096]{1,0:T(8,128)(2,1)S(1)}, u32[]{:S(2)}, u32[]{:S(2)}) %collective-permute-start.21) | collective-permute-done | bytes 786464 | tf_op jit(solution)/shard_map/ppermute | solution.py:117
  121.2 14.8 %collective-permute-done.28.refs_9_ = bf16[96,4096]{1,0:T(8,128)(2,1)} collective-permute-done((bf16[96,4096]{1,0:T(8,128)(2,1)}, bf16[96,4096]{1,0:T(8,128)(2,1)}, u32[]{:S(2)}, u32[]{:S(2)}) %collective-permute-start.28) | collective-permute-done | bytes 786464 | tf_op jit(solution)/shard_map/ppermute | solution.py:117
  138.3 14.5 %collective-permute-done.1.refs_2_ = bf16[96,4096]{1,0:T(8,128)(2,1)S(1)} collective-permute-done((bf16[96,4096]{1,0:T(8,128)(2,1)S(1)}, bf16[96,4096]{1,0:T(8,128)(2,1)S(1)}, u32[]{:S(2)}, u32[]{:S(2)}) %collective-permute-start.1) | collective-permute-done | bytes 786464 | tf_op jit(solution)/shard_map/ppermute | solution.py:117
  153.5 16.1 %collective-permute-done.4.refs_5_ = bf16[96,4096]{1,0:T(8,128)(2,1)S(1)} collective-permute-done((bf16[96,4096]{1,0:T(8,128)(2,1)S(1)}, bf16[96,4096]{1,0:T(8,128)(2,1)S(1)}, u32[]{:S(2)}, u32[]{:S(2)}) %collective-permute-start.4) | collective-permute-done | bytes 786464 | tf_op jit(solution)/shard_map/ppermute | solution.py:117
  172.3 14.2 %collective-permute-done.8.refs_10_ = bf16[96,4096]{1,0:T(8,128)(2,1)S(1)} collective-permute-done((bf16[96,4096]{1,0:T(8,128)(2,1)S(1)}, bf16[96,4096]{1,0:T(8,128)(2,1)S(1)}, u32[]{:S(2)}, u32[]{:S(2)}) %collective-permute-start.8) | collective-permute-done | bytes 786464 | tf_op jit(solution)/shard_map/ppermute | solution.py:117
  189.2 14.1 %collective-permute-done.22.refs_2_ = bf16[96,4096]{1,0:T(8,128)(2,1)S(1)} collective-permute-done((bf16[96,4096]{1,0:T(8,128)(2,1)S(1)}, bf16[96,4096]{1,0:T(8,128)(2,1)S(1)}, u32[]{:S(2)}, u32[]{:S(2)}) %collective-permute-start.22) | collective-permute-done | bytes 786464 | tf_op jit(solution)/shard_map/ppermute | solution.py:117
  204.9 15.3 %collective-permute-done.6.refs_6_ = bf16[96,4096]{1,0:T(8,128)(2,1)S(1)} collective-permute-done((bf16[96,4096]{1,0:T(8,128)(2,1)S(1)}, bf16[96,4096]{1,0:T(8,128)(2,1)S(1)}, u32[]{:S(2)}, u32[]{:S(2)}) %collective-permute-start.6) | collective-permute-done | bytes 786464 | tf_op jit(solution)/shard_map/ppermute | solution.py:121
  225.5 24.3 %expert_rows.2 = (bf16[96,2304]{1,0:T(8,128)(2,1)}, bf16[96,2304]{1,0:T(8,128)(2,1)}, bf16[96,2304]{1,0:T(8,128)(2,1)}, bf16[96,2304]{1,0:T(8,128)(2,1)}, bf16[9...) custom-call(bf16[96,4096]{1,0:T(8,128)(2,1)} %get-tuple-element.56.r, ...), custom_call_target="tpu_custom_call" | custom-call | flops 6039797760 | bytes 27262976 | tf_op jit(solution)/shard_map/expert_rows/pallas_call | solution.py:246
  257.9 24.3 %expert_rows.3 = (bf16[96,2304]{1,0:T(8,128)(2,1)}, bf16[96,2304]{1,0:T(8,128)(2,1)}, bf16[96,2304]{1,0:T(8,128)(2,1)}, bf16[96,2304]{1,0:T(8,128)(2,1)}, bf16[9...) custom-call(bf16[96,4096]{1,0:T(8,128)(2,1)} %get-tuple-element.66.r, ...), custom_call_target="tpu_custom_call" | custom-call | flops 6039797760 | bytes 27262976 | tf_op jit(solution)/shard_map/expert_rows/pallas_call | solution.py:246
  284.0 5.0 collective-permute-done.44
  289.9 7.6 %collective-permute-done.47 = bf16[96,2048]{1,0:T(8,128)(2,1)S(1)} collective-permute-done((bf16[96,2048]{1,0:T(8,128)(2,1)S(1)}, bf16[96,2048]{1,0:T(8,128)(2,1)S(1)}, u32[]{:S(2)}, u32[]{:S(2)}) %collective-permute-start.47) | collective-permute-done | bytes 393248 | tf_op jit(solution)/shard_map/ppermute | solution.py:125
  298.4 8.7 %collective-permute-done.51 = bf16[96,2048]{1,0:T(8,128)(2,1)S(1)} collective-permute-done((bf16[96,2048]{1,0:T(8,128)(2,1)}, bf16[96,2048]{1,0:T(8,128)(2,1)S(1)}, u32[]{:S(2)}, u32[]{:S(2)}) %collective-permute-start.51) | collective-permute-done | bytes 393248 | tf_op jit(solution)/shard_map/ppermute | solution.py:125
  308.1 9.8 %collective-permute-done.54 = bf16[96,2048]{1,0:T(8,128)(2,1)S(1)} collective-permute-done((bf16[96,2048]{1,0:T(8,128)(2,1)S(1)}, bf16[96,2048]{1,0:T(8,128)(2,1)S(1)}, u32[]{:S(2)}, u32[]{:S(2)}) %collective-permute-start.54) | collective-permute-done | bytes 393248 | tf_op jit(solution)/shard_map/ppermute | solution.py:125
  321.1 5.1 collective-permute-done.35
  327.3 3.9 collective-permute-done.38
  334.1 5.7 %collective-permute-done.45 = bf16[96,2048]{1,0:T(8,128)(2,1)S(1)} collective-permute-done((bf16[96,2048]{1,0:T(8,128)(2,1)S(1)}, bf16[96,2048]{1,0:T(8,128)(2,1)S(1)}, u32[]{:S(2)}, u32[]{:S(2)}) %collective-permute-start.45) | collective-permute-done | bytes 393248 | tf_op jit(solution)/shard_map/ppermute | solution.py:117
  343.2 3.5 collective-permute-done.52
  350.6 4.0 collective-permute-done.18
  359.5 5.4 %collective-permute-done.39 = bf16[96,2304]{1,0:T(8,128)(2,1)S(1)} collective-permute-done((bf16[96,2304]{1,0:T(8,128)(2,1)S(1)}, bf16[96,2304]{1,0:T(8,128)(2,1)S(1)}, u32[]{:S(2)}, u32[]{:S(2)}) %collective-permute-start.39) | collective-permute-done | bytes 442400 | tf_op jit(solution)/shard_map/ppermute | solution.py:121
  378.3 4.7 collective-permute-done.46.refs_13_
  383.0 4.0 collective-permute-done.41.refs_11_
  387.8 5.5 %pack_rows.1 = bf16[256,4096]{1,0:T(8,128)(2,1)} custom-call(bf16[256,192]{1,0:T(8,128)(2,1)} %constant.11.clone.refs_0_, bf16[192,128]{1,0:T(8,128)(2,1)} %constant.12.clone.refs_1_, bf16[256,192]{1,0:T(8,128)(2,1)} %constant.13.clone.refs_2_, bf16[256,192]{1,0:T(8,128)(2,1)} %constant.14.clone.refs_3_, bf16[96,2304]{1,0:T(8,128)(2,1)} %get-tuple-element.58.refs_4_, ...), custom_call_target="tpu_custom_call" | custom-call | tf_op jit(solution)/shard_map/pack_rows/pallas_call | solution.py:354
  393.2 22.9 %all-to-all-start.1 = ((bf16[16,16,4096]{2,1,0:T(8,128)(2,1)}), bf16[16,16,4096]{2,1,0:T(8,128)(2,1)S(1)}, u32[]{:S(2)}, u32[]{:S(2)}) async-start(bf16[16,16,4096]{2,1,0:T(8,128)(2,1)} %bitcast.10), calls=%async_computation.1 | async-start | bytes 4194304 | tf_op jit(solution)/shard_map/all_to_all | solution.py:416
  416.1 11.6 %expert_weights.2 = (bf16[2,192,4096]{2,1,0:T(8,128)(2,1)}, bf16[2,192,4096]{2,1,0:T(8,128)(2,1)}, bf16[2,192,4096]{2,1,0:T(8,128)(2,1)}, f32[1,4096]{1,0:T(1,128)}) custom-call(bf16[96,4096]{1,0:T(8,128)(2,1)} %get-tuple-element.56.refs_0_, bf16[96,4096]{1,0:T(8,128)(2,1)} %copy-done.1, bf16[96,4096]{1,0:T(8,128)(2,1)} %copy-done.7, ...), custom_call_target="tpu_custom_call" | custom-call | flops 3623878656 | bytes 18874368 | tf_op jit(solution)/shard_map/expert_weights/pallas_call | solution.py:288
  427.8 11.7 %expert_weights.3 = (bf16[2,192,4096]{2,1,0:T(8,128)(2,1)}, bf16[2,192,4096]{2,1,0:T(8,128)(2,1)}, bf16[2,192,4096]{2,1,0:T(8,128)(2,1)}, f32[1,4096]{1,0:T(1,128)}) custom-call(bf16[96,4096]{1,0:T(8,128)(2,1)} %get-tuple-element.66.refs_0_, bf16[96,4096]{1,0:T(8,128)(2,1)} %copy-done.15, ...), custom_call_target="tpu_custom_call", output_to_operand_aliasing={{0}: (20, {}), {1}: (21, {}), {2}: (22, {})} | custom-call | flops 3623878656 | bytes 18874368 | tf_op jit(solution)/shard_map/expert_weights/pallas_call | solution.py:288
  440.2 65.2 %psum.7 = f32[4096]{0:T(1024)} all-reduce(f32[4096]{0:T(1024)S(1)} %bitcast.14), channel_id=1, replica_groups=mesh['dp'=16,'tensor'=8] {'dp','tensor'}, use_global_device_ids=true, to_apply=%region_0.0 | all-reduce | flops 4096 | bytes 32768 | tf_op jit(solution)/shard_map/psum | solution.py:414
  506.8 4.9 combine.1
  (216 shorter events, 82.7 us)
Async XLA Ops:
  66.2 19.2 %collective-permute-start = (bf16[96,4096]{1,0:T(8,128)(2,1)}, bf16[96,4096]{1,0:T(8,128)(2,1)S(1)}, u32[]{:S(2)}, u32[]{:S(2)}) collective-permute-start(bf16[96,4096]{1,0:T(8,128)(2,1)} %get-tuple-element.56.refs_0_), channel_id=1, source_target_pairs={{0,1},{1,2},{2,3},{3,0},{4,5},{5,6},{6,7},{7,4},{8,9},{9,10},{10,1... | collective-permute-start | bytes 2359304 | tf_op jit(solution)/shard_map/ppermute | solution.py:117
  67.5 18.7 %collective-permute-start.2 = (bf16[96,4096]{1,0:T(8,128)(2,1)}, bf16[96,4096]{1,0:T(8,128)(2,1)S(1)}, u32[]{:S(2)}, u32[]{:S(2)}) collective-permute-start(bf16[96,4096]{1,0:T(8,128)(2,1)} %get-tuple-element.56.refs_0_), channel_id=1, source_target_pairs={{0,3},{1,0},{2,1},{3,2},{4,7},{5,4},{6,5},{7,6},{8,11},{9,8},{10,9... | collective-permute-start | bytes 2359304 | tf_op jit(solution)/shard_map/ppermute | solution.py:121
  69.7 32.5 %collective-permute-start.7 = (bf16[96,4096]{1,0:T(8,128)(2,1)}, bf16[96,4096]{1,0:T(8,128)(2,1)S(1)}, u32[]{:S(2)}, u32[]{:S(2)}) collective-permute-start(bf16[96,4096]{1,0:T(8,128)(2,1)} %get-tuple-element.57.refs_8_), channel_id=1, source_target_pairs={{0,1},{1,2},{2,3},{3,0},{4,5},{5,6},{6,7},{7,4},{8,9},{9,10},{10,1... | collective-permute-start | bytes 2359304 | tf_op jit(solution)/shard_map/ppermute | solution.py:117
  69.7 33.3 %collective-permute-start.9 = (bf16[96,4096]{1,0:T(8,128)(2,1)}, bf16[96,4096]{1,0:T(8,128)(2,1)S(1)}, u32[]{:S(2)}, u32[]{:S(2)}) collective-permute-start(bf16[96,4096]{1,0:T(8,128)(2,1)} %get-tuple-element.57.refs_8_), channel_id=1, source_target_pairs={{0,3},{1,0},{2,1},{3,2},{4,7},{5,4},{6,5},{7,6},{8,11},{9,8},{10,9... | collective-permute-start | bytes 2359304 | tf_op jit(solution)/shard_map/ppermute | solution.py:121
  86.1 32.9 %collective-permute-start.21 = (bf16[96,4096]{1,0:T(8,128)(2,1)}, bf16[96,4096]{1,0:T(8,128)(2,1)S(1)}, u32[]{:S(2)}, u32[]{:S(2)}) collective-permute-start(bf16[96,4096]{1,0:T(8,128)(2,1)} %get-tuple-element.66.refs_0_), channel_id=1, source_target_pairs={{0,1},{1,2},{2,3},{3,0},{4,5},{5,6},{6,7},{7,4},{8,9},{9,10},{10,1... | collective-permute-start | bytes 2359304 | tf_op jit(solution)/shard_map/ppermute | solution.py:117
  86.4 33.5 %collective-permute-start.23 = (bf16[96,4096]{1,0:T(8,128)(2,1)}, bf16[96,4096]{1,0:T(8,128)(2,1)}, u32[]{:S(2)}, u32[]{:S(2)}) collective-permute-start(bf16[96,4096]{1,0:T(8,128)(2,1)} %get-tuple-element.66.refs_0_), channel_id=1, source_target_pairs={{0,3},{1,0},{2,1},{3,2},{4,7},{5,4},{6,5},{7,6},{8,11},{9,8},{10,9... | collective-permute-start | bytes 2359304 | tf_op jit(solution)/shard_map/ppermute | solution.py:121
  102.2 18.0 %collective-permute-start.24 = (bf16[96,4096]{1,0:T(8,128)(2,1)}, bf16[96,4096]{1,0:T(8,128)(2,1)}, u32[]{:S(2)}, u32[]{:S(2)}) collective-permute-start(bf16[96,4096]{1,0:T(8,128)(2,1)} %get-tuple-element.66.refs_0_), channel_id=1, source_target_pairs={{0,4},{1,5},{2,6},{3,7},{4,0},{5,1},{6,2},{7,3},{8,12},{9,13},{10,... | collective-permute-start | bytes 2359304 | tf_op jit(solution)/shard_map/ppermute | solution.py:125
  103.0 33.0 %collective-permute-start.28 = (bf16[96,4096]{1,0:T(8,128)(2,1)}, bf16[96,4096]{1,0:T(8,128)(2,1)}, u32[]{:S(2)}, u32[]{:S(2)}) collective-permute-start(bf16[96,4096]{1,0:T(8,128)(2,1)} %get-tuple-element.67.refs_8_), channel_id=1, source_target_pairs={{0,1},{1,2},{2,3},{3,0},{4,5},{5,6},{6,7},{7,4},{8,9},{9,10},{10,1... | collective-permute-start | bytes 2359304 | tf_op jit(solution)/shard_map/ppermute | solution.py:117
  103.2 34.2 %collective-permute-start.29 = (bf16[96,4096]{1,0:T(8,128)(2,1)}, bf16[96,4096]{1,0:T(8,128)(2,1)}, u32[]{:S(2)}, u32[]{:S(2)}) collective-permute-start(bf16[96,4096]{1,0:T(8,128)(2,1)} %get-tuple-element.67.refs_8_), channel_id=1, source_target_pairs={{0,3},{1,0},{2,1},{3,2},{4,7},{5,4},{6,5},{7,6},{8,11},{9,8},{10,9... | collective-permute-start | bytes 2359304 | tf_op jit(solution)/shard_map/ppermute | solution.py:121
  119.0 18.4 %collective-permute-start.31 = (bf16[96,4096]{1,0:T(8,128)(2,1)}, bf16[96,4096]{1,0:T(8,128)(2,1)}, u32[]{:S(2)}, u32[]{:S(2)}) collective-permute-start(bf16[96,4096]{1,0:T(8,128)(2,1)} %get-tuple-element.67.refs_8_), channel_id=1, source_target_pairs={{0,4},{1,5},{2,6},{3,7},{4,0},{5,1},{6,2},{7,3},{8,12},{9,13},{10,... | collective-permute-start | bytes 2359304 | tf_op jit(solution)/shard_map/ppermute | solution.py:125
  119.8 32.9 %collective-permute-start.1 = (bf16[96,4096]{1,0:T(8,128)(2,1)S(1)}, bf16[96,4096]{1,0:T(8,128)(2,1)S(1)}, u32[]{:S(2)}, u32[]{:S(2)}) collective-permute-start(bf16[96,4096]{1,0:T(8,128)(2,1)S(1)} %collective-permute-done.refs_1_), channel_id=1, source_target_pairs={{0,1},{1,2},{2,3},{3,0},{4,5},{5,6},{6,7},{7,4},{8,9},{9,10},{10,1... | collective-permute-start | bytes 2359304 | tf_op jit(solution)/shard_map/ppermute | solution.py:117
  120.2 49.4 %collective-permute-start.4 = (bf16[96,4096]{1,0:T(8,128)(2,1)S(1)}, bf16[96,4096]{1,0:T(8,128)(2,1)S(1)}, u32[]{:S(2)}, u32[]{:S(2)}) collective-permute-start(bf16[96,4096]{1,0:T(8,128)(2,1)S(1)} %collective-permute-done.3.refs_4_), channel_id=1, source_target_pairs={{0,1},{1,2},{2,3},{3,0},{4,5},{5,6},{6,7},{7,4},{8,9},{9,10},{10,1... | collective-permute-start | bytes 2359304 | tf_op jit(solution)/shard_map/ppermute | solution.py:117
  136.0 33.6 %collective-permute-start.5 = (bf16[96,4096]{1,0:T(8,128)(2,1)S(1)}, bf16[96,4096]{1,0:T(8,128)(2,1)S(1)}, u32[]{:S(2)}, u32[]{:S(2)}) collective-permute-start(bf16[96,4096]{1,0:T(8,128)(2,1)S(1)} %collective-permute-done.3.refs_4_), channel_id=1, source_target_pairs={{0,3},{1,0},{2,1},{3,2},{4,7},{5,4},{6,5},{7,6},{8,11},{9,8},{10,9... | collective-permute-start | bytes 2359304 | tf_op jit(solution)/shard_map/ppermute | solution.py:121
  137.4 49.0 %collective-permute-start.8 = (bf16[96,4096]{1,0:T(8,128)(2,1)S(1)}, bf16[96,4096]{1,0:T(8,128)(2,1)S(1)}, u32[]{:S(2)}, u32[]{:S(2)}) collective-permute-start(bf16[96,4096]{1,0:T(8,128)(2,1)S(1)} %collective-permute-done.7.refs_9_), channel_id=1, source_target_pairs={{0,1},{1,2},{2,3},{3,0},{4,5},{5,6},{6,7},{7,4},{8,9},{9,10},{10,1... | collective-permute-start | bytes 2359304 | tf_op jit(solution)/shard_map/ppermute | solution.py:117
  137.5 50.5 %collective-permute-start.11 = (bf16[96,4096]{1,0:T(8,128)(2,1)S(1)}, bf16[96,4096]{1,0:T(8,128)(2,1)S(1)}, u32[]{:S(2)}, u32[]{:S(2)}) collective-permute-start(bf16[96,4096]{1,0:T(8,128)(2,1)S(1)} %collective-permute-done.7.refs_9_), channel_id=1, source_target_pairs={{0,4},{1,5},{2,6},{3,7},{4,0},{5,1},{6,2},{7,3},{8,12},{9,13},{10,... | collective-permute-start | bytes 2359304 | tf_op jit(solution)/shard_map/ppermute | solution.py:125
  152.7 35.7 %collective-permute-start.13 = (bf16[96,4096]{1,0:T(8,128)(2,1)S(1)}, bf16[96,4096]{1,0:T(8,128)(2,1)S(1)}, u32[]{:S(2)}, u32[]{:S(2)}) collective-permute-start(bf16[96,4096]{1,0:T(8,128)(2,1)S(1)} %collective-permute-done.9.refs_11_), channel_id=1, source_target_pairs={{0,4},{1,5},{2,6},{3,7},{4,0},{5,1},{6,2},{7,3},{8,12},{9,13},{10,... | collective-permute-start | bytes 2359304 | tf_op jit(solution)/shard_map/ppermute | solution.py:125
  169.6 33.7 %collective-permute-start.22 = (bf16[96,4096]{1,0:T(8,128)(2,1)S(1)}, bf16[96,4096]{1,0:T(8,128)(2,1)S(1)}, u32[]{:S(2)}, u32[]{:S(2)}) collective-permute-start(bf16[96,4096]{1,0:T(8,128)(2,1)S(1)} %collective-permute-done.21.refs_1_), channel_id=1, source_target_pairs={{0,1},{1,2},{2,3},{3,0},{4,5},{5,6},{6,7},{7,4},{8,9},{9,10},{10,1... | collective-permute-start | bytes 2359304 | tf_op jit(solution)/shard_map/ppermute | solution.py:117
  169.6 33.8 %collective-permute-start.26 = (bf16[96,4096]{1,0:T(8,128)(2,1)}, bf16[96,4096]{1,0:T(8,128)(2,1)}, u32[]{:S(2)}, u32[]{:S(2)}) collective-permute-start(bf16[96,4096]{1,0:T(8,128)(2,1)} %collective-permute-done.24.refs_4_), channel_id=1, source_target_pairs={{0,3},{1,0},{2,1},{3,2},{4,7},{5,4},{6,5},{7,6},{8,11},{9,8},{10,9... | collective-permute-start | bytes 2359304 | tf_op jit(solution)/shard_map/ppermute | solution.py:121
  188.0 32.2 %collective-permute-start.6 = (bf16[96,4096]{1,0:T(8,128)(2,1)S(1)}, bf16[96,4096]{1,0:T(8,128)(2,1)S(1)}, u32[]{:S(2)}, u32[]{:S(2)}) collective-permute-start(bf16[96,4096]{1,0:T(8,128)(2,1)S(1)} %collective-permute-done.5.refs_7_), channel_id=1, source_target_pairs={{0,3},{1,0},{2,1},{3,2},{4,7},{5,4},{6,5},{7,6},{8,11},{9,8},{10,9... | collective-permute-start | bytes 2359304 | tf_op jit(solution)/shard_map/ppermute | solution.py:121
  188.5 35.1 %collective-permute-start.12 = (bf16[96,4096]{1,0:T(8,128)(2,1)S(1)}, bf16[96,4096]{1,0:T(8,128)(2,1)S(1)}, u32[]{:S(2)}, u32[]{:S(2)}) collective-permute-start(bf16[96,4096]{1,0:T(8,128)(2,1)S(1)} %collective-permute-done.8.refs_10_), channel_id=1, source_target_pairs={{0,4},{1,5},{2,6},{3,7},{4,0},{5,1},{6,2},{7,3},{8,12},{9,13},{10,... | collective-permute-start | bytes 2359304 | tf_op jit(solution)/shard_map/ppermute | solution.py:125
  203.3 46.5 %collective-permute-start.25 = (bf16[96,4096]{1,0:T(8,128)(2,1)}, bf16[96,4096]{1,0:T(8,128)(2,1)}, u32[]{:S(2)}, u32[]{:S(2)}) collective-permute-start(bf16[96,4096]{1,0:T(8,128)(2,1)} %collective-permute-done.24.refs_4_), channel_id=1, source_target_pairs={{0,1},{1,2},{2,3},{3,0},{4,5},{5,6},{6,7},{7,4},{8,9},{9,10},{10,1... | collective-permute-start | bytes 2359304 | tf_op jit(solution)/shard_map/ppermute | solution.py:117
  203.4 46.4 %collective-permute-start.32 = (bf16[96,4096]{1,0:T(8,128)(2,1)}, bf16[96,4096]{1,0:T(8,128)(2,1)}, u32[]{:S(2)}, u32[]{:S(2)}) collective-permute-start(bf16[96,4096]{1,0:T(8,128)(2,1)} %collective-permute-done.28.refs_9_), channel_id=1, source_target_pairs={{0,4},{1,5},{2,6},{3,7},{4,0},{5,1},{6,2},{7,3},{8,12},{9,13},{10,... | collective-permute-start | bytes 2359304 | tf_op jit(solution)/shard_map/ppermute | solution.py:125
  204.2 48.4 %collective-permute-start.34 = (bf16[96,4096]{1,0:T(8,128)(2,1)}, bf16[96,4096]{1,0:T(8,128)(2,1)}, u32[]{:S(2)}, u32[]{:S(2)}) collective-permute-start(bf16[96,4096]{1,0:T(8,128)(2,1)} %collective-permute-done.29.refs_11_), channel_id=1, source_target_pairs={{0,4},{1,5},{2,6},{3,7},{4,0},{5,1},{6,2},{7,3},{8,12},{9,13},{10,... | collective-permute-start | bytes 2359304 | tf_op jit(solution)/shard_map/ppermute | solution.py:125
  220.2 32.4 %collective-permute-start.27 = (bf16[96,4096]{1,0:T(8,128)(2,1)}, bf16[96,4096]{1,0:T(8,128)(2,1)}, u32[]{:S(2)}, u32[]{:S(2)}) collective-permute-start(bf16[96,4096]{1,0:T(8,128)(2,1)} %collective-permute-done.26.refs_7_), channel_id=1, source_target_pairs={{0,3},{1,0},{2,1},{3,2},{4,7},{5,4},{6,5},{7,6},{8,11},{9,8},{10,9... | collective-permute-start | bytes 2359304 | tf_op jit(solution)/shard_map/ppermute | solution.py:121
  224.6 32.5 %collective-permute-start.33 = (bf16[96,4096]{1,0:T(8,128)(2,1)}, bf16[96,4096]{1,0:T(8,128)(2,1)}, u32[]{:S(2)}, u32[]{:S(2)}) collective-permute-start(bf16[96,4096]{1,0:T(8,128)(2,1)} %collective-permute-done.30.refs_10_), channel_id=1, source_target_pairs={{0,4},{1,5},{2,6},{3,7},{4,0},{5,1},{6,2},{7,3},{8,12},{9,13},{10,... | collective-permute-start | bytes 2359304 | tf_op jit(solution)/shard_map/ppermute | solution.py:125
  249.8 68.2 %collective-permute-start.14 = (bf16[96,2304]{1,0:T(8,128)(2,1)}, bf16[96,2304]{1,0:T(8,128)(2,1)S(1)}, u32[]{:S(2)}, u32[]{:S(2)}) collective-permute-start(bf16[96,2304]{1,0:T(8,128)(2,1)} %get-tuple-element.60), channel_id=1, source_target_pairs={{0,1},{1,2},{2,3},{3,0},{4,5},{5,6},{6,7},{7,4},{8,9},{9,10},{10,1... | collective-permute-start | bytes 1327112 | tf_op jit(solution)/shard_map/ppermute | solution.py:117
  249.9 115.2 %collective-permute-start.16 = (bf16[96,2304]{1,0:T(8,128)(2,1)}, bf16[96,2304]{1,0:T(8,128)(2,1)S(1)}, u32[]{:S(2)}, u32[]{:S(2)}) collective-permute-start(bf16[96,2304]{1,0:T(8,128)(2,1)} %get-tuple-element.61), channel_id=1, source_target_pairs={{0,3},{1,0},{2,1},{3,2},{4,7},{5,4},{6,5},{7,6},{8,11},{9,8},{10,9... | collective-permute-start | bytes 1327112 | tf_op jit(solution)/shard_map/ppermute | solution.py:121
  252.5 97.0 %collective-permute-start.19 = (bf16[96,2304]{1,0:T(8,128)(2,1)}, bf16[96,2304]{1,0:T(8,128)(2,1)S(1)}, u32[]{:S(2)}, u32[]{:S(2)}) collective-permute-start(bf16[96,2304]{1,0:T(8,128)(2,1)} %get-tuple-element.65), channel_id=1, source_target_pairs={{0,1},{1,2},{2,3},{3,0},{4,5},{5,6},{6,7},{7,4},{8,9},{9,10},{10,1... | collective-permute-start | bytes 1327112 | tf_op jit(solution)/shard_map/ppermute | solution.py:117
  252.5 68.3 %collective-permute-start.17 = (bf16[96,2304]{1,0:T(8,128)(2,1)}, bf16[96,2304]{1,0:T(8,128)(2,1)S(1)}, u32[]{:S(2)}, u32[]{:S(2)}) collective-permute-start(bf16[96,2304]{1,0:T(8,128)(2,1)} %get-tuple-element.64), channel_id=1, source_target_pairs={{0,3},{1,0},{2,1},{3,2},{4,7},{5,4},{6,5},{7,6},{8,11},{9,8},{10,9... | collective-permute-start | bytes 1327112 | tf_op jit(solution)/shard_map/ppermute | solution.py:121
  257.1 25.2 %collective-permute-start.42 = (bf16[96,2048]{1,0:T(8,128)(2,1)}, bf16[96,2048]{1,0:T(8,128)(2,1)S(1)}, u32[]{:S(2)}, u32[]{:S(2)}) collective-permute-start(bf16[96,2048]{1,0:T(8,128)(2,1)} %get-tuple-element.77), channel_id=1, source_target_pairs={{0,4},{1,5},{2,6},{3,7},{4,0},{5,1},{6,2},{7,3},{8,12},{9,13},{10,... | collective-permute-start | bytes 1179656 | tf_op jit(solution)/shard_map/ppermute | solution.py:125
  318.0 48.0 %collective-permute-start.37 = (bf16[96,2304]{1,0:T(8,128)(2,1)S(1)}, bf16[96,2304]{1,0:T(8,128)(2,1)S(1)}, u32[]{:S(2)}, u32[]{:S(2)}) collective-permute-start(bf16[96,2304]{1,0:T(8,128)(2,1)S(1)} %copy-done.43), channel_id=1, source_target_pairs={{0,3},{1,0},{2,1},{3,2},{4,7},{5,4},{6,5},{7,6},{8,11},{9,8},{10,9... | collective-permute-start | bytes 1327112 | tf_op jit(solution)/shard_map/ppermute | solution.py:121
  393.2 112.2 %all-to-all-start.1 = ((bf16[16,16,4096]{2,1,0:T(8,128)(2,1)}), bf16[16,16,4096]{2,1,0:T(8,128)(2,1)S(1)}, u32[]{:S(2)}, u32[]{:S(2)}) async-start(bf16[16,16,4096]{2,1,0:T(8,128)(2,1)} %bitcast.10), calls=%async_computation.1 | async-start | bytes 4194304 | tf_op jit(solution)/shard_map/all_to_all | solution.py:416
  (78 other events, 2365.8 us)

commit v2 on v0

v2 whole, which is shorter than its diff:
```python
import functools

import jax
import jax.numpy as jnp
import numpy as np
from jax import lax
from jax.experimental import pallas as pl
from jax.experimental.pallas import tpu as pltpu
from jax.sharding import PartitionSpec as P

EPS = 1e-06
TOK = 128
D = 4096
HALF = D // 2
QUART = D // 4
CAP = 6
N_DP = 16
SLICE = 192
ROWS = N_DP * CAP
PART = 4 * ROWS
EXTRA = 128
VMEM = 56 * 1024 * 1024
F32 = jnp.float32
BF16 = jnp.bfloat16


def params():
    return pltpu.CompilerParams(vmem_limit_bytes=VMEM)


def whole(shape):
    return pl.BlockSpec(shape, lambda *_: (0,) * len(shape))


def dot(a, b):
    return jnp.dot(a, b, preferred_element_type=F32)


def dot_nt(a, b):
    return lax.dot_general(a, b, (((1,), (1,)), ((), ())), preferred_element_type=F32)


def iota(shape, dim):
    return lax.broadcasted_iota(jnp.int32, shape, dim)


def stack(refs, cols=slice(None)):
    return jnp.concatenate([r[:, cols] for r in refs], axis=0)


def move(i, kind):
    z, y = divmod(i % 8, 4)
    if kind == "z":
        z = z ^ 1
    elif (kind == "trade") == (i // 8 % 2 == 0):
        y = y ^ 1
    else:
        y = 3 - y
    return i // 8 * 8 + z * 4 + y


AXES = ("dp", "tensor")
PERMS = {k: [(i, move(i, k)) for i in range(128)] for k in ("trade", "y", "z")}


def trade(x):
    return lax.ppermute(x, AXES, PERMS["trade"])


def trade_for(core, x):
    return lax.ppermute(x, "tensor", [(t, move(core * 8 + t, "trade") % 8) for t in range(8)])


def over_y(x):
    return lax.ppermute(x, AXES, PERMS["y"])


def over_z(x):
    return lax.ppermute(x, AXES, PERMS["z"])


def owned():
    y = lax.axis_index("tensor") & 3
    return jnp.where((y == 0) | (y == 3), 1, 0).astype(jnp.int32), y >> 1


def column(row):
    diagonal = iota((TOK, TOK), 0) == iota((TOK, TOK), 1)
    return jnp.sum(jnp.where(diagonal, row, jnp.zeros_like(row)), axis=1, keepdims=True)


def rank_of(rrow, axis):
    same = column(rrow) == rrow
    earlier = iota((TOK, TOK), axis) < iota((TOK, TOK), 1 - axis)
    return jnp.sum(jnp.where(same & earlier, 1, 0), axis=axis, keepdims=True)


def place_of(expert, own_ref):
    dp = expert >> 1
    mine = jnp.where((dp & 1) == 0, own_ref[0], own_ref[1])
    return dp, (expert & 1) ^ mine


def dispatch_kernel(turn, own_ref, h_ref, c_ref, gain_ref, rrow_ref, wrow_ref, *outs):
    rows = 4 * ROWS
    len_out = rows // len(outs)
    x = h_ref[...].astype(F32)
    scale = lax.rsqrt(jnp.mean(x * x, axis=-1, keepdims=True) + EPS)
    weight = column(wrow_ref[...].astype(F32))
    rank = rank_of(rrow_ref[...], 0)
    dp, when = place_of(rrow_ref[...], own_ref)
    if len(outs) == 2:
        dp = (dp >> 1) + (dp & 1) * (N_DP // 2)
    slot = jnp.where(when == turn, dp * (4 * CAP) + rank, -4 * CAP)
    at = iota((rows, TOK), 0)
    pick = [jnp.where(at == slot + k * CAP, 1.0, 0.0).astype(BF16) for k in range(4)]
    pick = jnp.concatenate(pick, axis=1)
    wide = 512
    for j in range(HALF // wide):
        value = []
        for half in range(2):
            cols = slice(half * HALF + j * wide, half * HALF + (j + 1) * wide)
            value.append((x[:, cols] * scale * gain_ref[:, cols]).astype(BF16))
            value.append((c_ref[:, cols].astype(F32) * weight).astype(BF16))
        rows_j = dot(pick, jnp.concatenate(value, axis=0)).astype(BF16)
        for k, out in enumerate(outs):
            out[:, j * wide : (j + 1) * wide] = rows_j[k * len_out : (k + 1) * len_out]


def dispatch(turn, own, h, c, gain, rrow, wrow):
    return pl.pallas_call(
        functools.partial(dispatch_kernel, turn),
        in_specs=[pl.BlockSpec(memory_space=pltpu.SMEM)] + [pl.BlockSpec(memory_space=pltpu.VMEM)] * 5,
        out_shape=[jax.ShapeDtypeStruct((4 * ROWS // (1 + turn), HALF), BF16)] * (1 + turn),
        compiler_params=params(),
        cost_estimate=pl.CostEstimate(flops=2 * 384 * 512 * HALF, bytes_accessed=4 << 20, transcendentals=0),
        name="dispatch",
    )(own, h, c, gain, rrow, wrow)


def sort_matrix():
    out = np.zeros((4 * ROWS, 4 * ROWS), np.float32)
    for block in range(4):
        for src in range(N_DP):
            for k in range(CAP):
                out[block * ROWS + src * CAP + k, src * 4 * CAP + block * CAP + k] = 1.0
    return out


def sort_kernel(m_ref, x_ref, out_ref):
    for half in range(2):
        rows = m_ref[half * 2 * ROWS : (half + 1) * 2 * ROWS, :]
        out_ref[:, half * HALF : (half + 1) * HALF] = dot(rows, x_ref[...]).astype(BF16)


def sort_rows(x):
    return pl.pallas_call(
        sort_kernel,
        out_shape=jax.ShapeDtypeStruct((2 * ROWS, D), BF16),
        compiler_params=params(),
        cost_estimate=pl.CostEstimate(flops=2 * 384 * 384 * HALF, bytes_accessed=4 << 20, transcendentals=0),
        name="sort_rows",
    )(jnp.asarray(sort_matrix(), BF16), x)


def tie(x, *others):
    return barrier(x, *others)[0]


def barrier(*arrays):
    return list(lax.optimization_barrier(arrays))


def pieces(hs, cs, wide):
    specs = [pl.BlockSpec((ROWS, wide), lambda s, own, k=k: (k, s)) for _, k in hs + cs]
    return specs, [x for x, _ in hs + cs]


def slices(count, wide):
    return [pl.BlockSpec((SLICE, wide), lambda s, own, k=k: (k, s)) for k in range(count)]


def add(a, b):
    return (a.astype(F32) + b.astype(F32)).astype(BF16)


def sum_dp(x, bit):
    return x + lax.ppermute(x, "dp", [(i, i ^ bit) for i in range(16)])


def spread(x):
    return jnp.where(iota((8, D), 0) == lax.axis_index("tensor"), x, 0.0)


def forward_kernel(own_ref, *refs):
    hs, cs = refs[:4], refs[4:8]
    gate_ref, up_ref, down_ref, gate2_ref, up2_ref, down2_ref = refs[8:14]
    dgu_ref, dgu_t_ref, act_t_ref, pw_ref = refs[14:18]
    acc_g, acc_u, acc_b = refs[18:]
    s = pl.program_id(0)
    h, c = stack(hs), stack(cs)
    g = dot_nt(h, jnp.concatenate([gate_ref[0], gate2_ref[...]], axis=0))
    u = dot_nt(h, jnp.concatenate([up_ref[0], up2_ref[...]], axis=0))
    b = dot_nt(c, jnp.concatenate([down_ref[0], down2_ref[...]], axis=0))

    @pl.when(s == 0)
    def _():
        acc_g[...] = g
        acc_u[...] = u
        acc_b[...] = b

    @pl.when(s > 0)
    def _():
        acc_g[...] += g
        acc_u[...] += u
        acc_b[...] += b

    @pl.when(s == pl.num_programs(0) - 1)
    def _():
        gate, upp, back = acc_g[...], acc_u[...], acc_b[...]
        sig = jax.nn.sigmoid(gate)
        silu = gate * sig
        act = silu * upp
        dgate = back * upp * sig * (1.0 + gate * (1.0 - sig))
        dup = back * silu
        for part in range(2):
            cols = slice(part * SLICE, (part + 1) * SLICE)
            lo = part * 2 * SLICE
            dgu_ref[:, lo : lo + SLICE] = dgate[:, cols].astype(BF16)
            dgu_ref[:, lo + SLICE : lo + 2 * SLICE] = dup[:, cols].astype(BF16)
        dgate_t, dup_t = dgate.T.astype(BF16), dup.T.astype(BF16)
        for part in range(2):
            rows = slice(part * SLICE, (part + 1) * SLICE)
            lo = part * 2 * SLICE
            dgu_t_ref[lo : lo + SLICE, :] = dgate_t[rows]
            dgu_t_ref[lo + SLICE : lo + 2 * SLICE, :] = dup_t[rows]
        act_t_ref[...] = act.T.astype(BF16)
        pw = jnp.sum(act * back, axis=-1, keepdims=True)
        high = pw.astype(BF16).astype(F32)
        lane = iota((PART, EXTRA), 1)
        value = jnp.where(lane == 0, high, jnp.where(lane == 1, pw - high, 0.0))
        pw_ref[...] = value.astype(BF16)


def forward(own, hs, cs, weights, got_gu, got_d):
    step = 1024
    specs, arrays = pieces(hs, cs, step)
    mine = pl.BlockSpec((1, SLICE, step), lambda s, own: (own[0], 0, s))
    shapes = [(PART, 4 * SLICE), (4 * SLICE, PART), (2 * SLICE, PART), (PART, EXTRA)]
    return pl.pallas_call(
        forward_kernel,
        grid_spec=pltpu.PrefetchScalarGridSpec(
            num_scalar_prefetch=1,
            grid=(D // step,),
            in_specs=specs + [mine] * 3 + slices(2, step) + slices(1, step),
            out_specs=[whole(s) for s in shapes],
            scratch_shapes=[pltpu.VMEM((PART, 2 * SLICE), F32)] * 3,
        ),
        out_shape=[jax.ShapeDtypeStruct(s, BF16) for s in shapes],
        compiler_params=params(),
        cost_estimate=pl.CostEstimate(
            flops=2 * PART * 6 * SLICE * D, bytes_accessed=16 << 20, transcendentals=PART * 384
        ),
        name="expert_forward",
    )(own, *arrays, *weights, got_gu, got_gu, got_d)


def rows_kernel(own_ref, dgu_ref, pw_ref, *refs):
    hs = refs[:4]
    gate_ref, up_ref, gate2_ref, up2_ref = refs[4:8]
    outs, norm_ref = refs[8:12], refs[12]
    s = pl.program_id(0)
    wide = gate_ref.shape[-1]
    w = jnp.concatenate([gate_ref[0], up_ref[0], gate2_ref[...], up2_ref[...]], axis=0)
    value = dot(dgu_ref[...], w)
    norm_ref[...] = jnp.sum(value * stack(hs).astype(F32), axis=0, keepdims=True)
    value = value.astype(BF16)
    cols = pl.ds(pl.multiple_of(s * wide, wide), wide)
    for k, out in enumerate(outs):
        out[:, cols] = value[k * ROWS : (k + 1) * ROWS]

    @pl.when(s == 0)
    def _():
        for k, out in enumerate(outs):
            out[:, D:] = pw_ref[k * ROWS : (k + 1) * ROWS, :]


def expert_rows(own, dgu, pw, hs, weights, got):
    wide = 512
    mine = pl.BlockSpec((1, SLICE, wide), lambda s, own: (own[0], 0, s))
    specs, arrays = pieces(hs, [], wide)
    shape = (ROWS, D + EXTRA)
    return pl.pallas_call(
        rows_kernel,
        grid_spec=pltpu.PrefetchScalarGridSpec(
            num_scalar_prefetch=1,
            grid=(D // wide,),
            in_specs=[whole((PART, 4 * SLICE)), whole((PART, EXTRA))] + specs + [mine, mine] + slices(2, wide),
            out_specs=[whole(shape)] * 4 + [pl.BlockSpec((1, wide), lambda s, own: (0, s))],
        ),
        out_shape=[jax.ShapeDtypeStruct(shape, BF16)] * 4 + [jax.ShapeDtypeStruct((1, D), F32)],
        compiler_params=params(),
        cost_estimate=pl.CostEstimate(
            flops=2 * PART * 4 * SLICE * D, bytes_accessed=10 << 20, transcendentals=0
        ),
        name="expert_rows",
    )(own, dgu, pw, *arrays, weights[0], weights[1], got, got)


def weights_kernel(part, kinds, own_ref, *refs):
    outs = refs[-len(kinds) :]
    hs, cs = refs[:8], refs[8:16]
    if 2 not in kinds:
        lhs, lo, hi, rows = refs[8:10], part * 2 + kinds[0], part * 2 + kinds[-1] + 1, hs
        values = dot(jnp.concatenate([r[lo * SLICE : hi * SLICE] for r in lhs], axis=1), stack(rows))
        values = [values[k * SLICE : (k + 1) * SLICE] for k in range(len(kinds))]
    elif kinds == (2,):
        lhs, rows = refs[8:10], hs
        values = [dot(jnp.concatenate([r[part * SLICE : (part + 1) * SLICE] for r in lhs], axis=1), stack(rows))]
    else:
        lo = part * 2 * SLICE
        lhs = [r[lo : lo + 2 * SLICE] for r in refs[16:18]]
        values = dot(jnp.concatenate(lhs, axis=1), stack(hs))
        values = [values[:SLICE], values[SLICE:]]
        lhs = [r[part * SLICE : (part + 1) * SLICE] for r in refs[18:20]]
        values.append(dot(jnp.concatenate(lhs, axis=1), stack(cs)))
    for out, value in zip(outs, values):
        if part == 0:
            out[0] = value.astype(BF16)
        else:
            out[...] = value.astype(BF16)


def expert_weights(part, kinds, own, hs, cs, dgu_t, act_t, after):
    wide = 512
    hs, dgu_t = (hs, dgu_t) if 0 in kinds or 1 in kinds else ([], ())
    cs, act_t = (cs, act_t) if 2 in kinds else ([], ())
    specs, arrays = pieces(hs, cs, wide)
    if part == 0:
        made = pl.BlockSpec((1, SLICE, wide), lambda j, own: (own[0], 0, j))
        grad = jax.ShapeDtypeStruct((2, SLICE, D), BF16)
    else:
        made = pl.BlockSpec((SLICE, wide), lambda j, own: (0, j))
        grad = jax.ShapeDtypeStruct((SLICE, D), BF16)
    out = pl.pallas_call(
        functools.partial(weights_kernel, part, kinds),
        grid_spec=pltpu.PrefetchScalarGridSpec(
            num_scalar_prefetch=1,
            grid=(D // wide,),
            in_specs=specs
            + [whole((4 * SLICE, PART))] * len(dgu_t)
            + [whole((2 * SLICE, PART))] * len(act_t)
            + [pl.BlockSpec(memory_space=pl.ANY)] * len(after),
            out_specs=[made] * len(kinds),
        ),
        out_shape=[grad] * len(kinds),
        compiler_params=params(),
        cost_estimate=pl.CostEstimate(
            flops=2 * 2 * PART * len(kinds) * SLICE * D, bytes_accessed=len(kinds) * 6 << 20, transcendentals=0
        ),
        name="expert_weights",
    )(own, *arrays, *dgu_t, *act_t, *after)
    return list(out)


def pack_matrix():
    out = np.zeros((4 * ROWS, 4 * ROWS), np.float32)
    for quarter in range(4):
        for src in range(N_DP):
            for k in range(CAP):
                out[src * 4 * CAP + quarter * CAP + k, quarter * ROWS + src * CAP + k] = 1.0
    return out


def pack_kernel(m_ref, p_ref, q_ref, r_ref, out_ref):
    def total(cols):
        return p_ref[:, cols].astype(F32) + q_ref[:, cols].astype(F32) + r_ref[:, cols].astype(F32)

    wide = 512
    for j in range(QUART // wide):
        lo = j * wide
        rows = [total(slice(q * QUART + lo, q * QUART + lo + wide)).astype(BF16) for q in range(4)]
        out_ref[:, lo : lo + wide] = dot(m_ref[...], jnp.concatenate(rows, axis=0)).astype(BF16)
    pw = total(slice(D, D + EXTRA))
    pw = pw[:, 0:1] + pw[:, 1:2]
    high = pw.astype(BF16).astype(F32)
    lane = iota((ROWS, EXTRA), 1)
    value = jnp.where(lane == 0, high, jnp.where(lane == 1, pw - high, 0.0)).astype(BF16)
    out_ref[:, QUART:] = dot(m_ref[:, :ROWS], value).astype(BF16)


def pack(p, q, r):
    return pl.pallas_call(
        pack_kernel,
        out_shape=jax.ShapeDtypeStruct((4 * ROWS, QUART + EXTRA), BF16),
        compiler_params=params(),
        cost_estimate=pl.CostEstimate(flops=2 * 384 * 384 * QUART, bytes_accessed=4 << 20, transcendentals=0),
        name="pack_rows",
    )(jnp.asarray(pack_matrix(), BF16), p, q, r)


def combine_kernel(own_ref, r0_ref, r1_ref, h_ref, c_ref, gain_ref, rrow_ref, wrow_ref, out_ref, routes_ref):
    rank = rank_of(rrow_ref[...], 1)
    dp, when = place_of(column(rrow_ref[...]), own_ref)
    place = dp * (4 * CAP) + rank + when * (4 * ROWS)
    at = iota((TOK, 8 * ROWS), 1)
    r = jnp.concatenate([r0_ref[...], r1_ref[...]], axis=0)
    picks = [jnp.where(at == place + q * CAP, 1.0, 0.0).astype(BF16) for q in range(4)]
    pw = dot(picks[0], r[:, QUART:])
    diagonal = iota((TOK, TOK), 0) == iota((TOK, TOK), 1)
    pw = jnp.sum(jnp.where(diagonal, pw[:, 0:1] + pw[:, 1:2], 0.0), axis=0, keepdims=True)
    routes_ref[...] = pw / wrow_ref[...].astype(F32)
    g = jnp.concatenate([dot(p, r[:, :QUART]) for p in picks], axis=1)
    x = h_ref[...].astype(F32)
    scale = lax.rsqrt(jnp.mean(x * x, axis=-1, keepdims=True) + EPS)
    x = x * scale
    dx = g * gain_ref[...]
    mix = jnp.mean(dx * x, axis=-1, keepdims=True)
    out_ref[...] = (c_ref[...].astype(F32) + scale * (dx - x * mix)).astype(BF16)


def combine(own, r0, r1, h, c, gain, rrow, wrow):
    return pl.pallas_call(
        combine_kernel,
        in_specs=[pl.BlockSpec(memory_space=pltpu.SMEM)] + [pl.BlockSpec(memory_space=pltpu.VMEM)] * 7,
        out_shape=[
            jax.ShapeDtypeStruct((TOK, D), BF16),
            jax.ShapeDtypeStruct((1, TOK), F32),
        ],
        compiler_params=params(),
        cost_estimate=pl.CostEstimate(flops=2 * 128 * 768 * D, bytes_accessed=5 << 20, transcendentals=0),
        name="combine",
    )(own, r0, r1, h, c, gain, rrow, wrow)


def exchange(x):
    shaped = x.reshape((N_DP, -1) + x.shape[1:])
    got = lax.all_to_all(shaped, "dp", split_axis=0, concat_axis=0, tiled=True)
    return got.reshape(x.shape)


def body(h, c, gain, routes, w, w_gate, w_up, w_down):
    gain = gain.reshape(1, D)
    rrow, wrow = routes.reshape(1, TOK), w.reshape(1, TOK)
    own0, own1 = owned()
    owns = jnp.stack([own0, own1])
    mine = jnp.where((lax.axis_index("dp") & 1) == 0, own0, own1)
    own = mine.reshape(1)
    weights = (w_gate, w_up, w_down)

    slots_a = dispatch(1, owns, h, c, gain, rrow, wrow)
    slots_a = [trade_for(core, x).reshape(N_DP // 2, -1, HALF) for core, x in enumerate(slots_a)]
    (slots_b,) = dispatch(0, owns, h, c, gain, rrow, wrow)
    leave = [lax.dynamic_index_in_dim(x, 1 - mine, 0, keepdims=False) for x in weights]
    leave_gu = jnp.concatenate(leave[:2], axis=0)
    *slots_a, slots_b, leave_gu = barrier(*slots_a, slots_b, leave_gu)
    got_a = exchange(jnp.stack(slots_a, axis=1).reshape(4 * ROWS, HALF))
    got_gu = trade(leave_gu)
    got_a, leave_d = barrier(got_a, leave[2])
    got_b = exchange(slots_b)
    a = sort_rows(got_a)
    got_d = trade(leave_d)
    az, ay = over_z(a), over_y(a)
    az, ay, got_b, got_gu = barrier(az, ay, got_b, got_gu)
    b = sort_rows(got_b)
    ao, bz, by = over_y(az), over_z(b), over_y(b)
    piece_a = (a, ay, az, ao)
    hs_a, cs_a = [(x, 0) for x in piece_a], [(x, 1) for x in piece_a]
    dgu_a, dgu_ta, act_ta, pw_a = forward(own, hs_a, cs_a, weights, got_gu, got_d)
    bz, by, dgu_a = barrier(bz, by, dgu_a)
    bo = over_y(bz)
    *pa, norm = expert_rows(own, dgu_a, pw_a, hs_a, weights, got_gu)
    za, ya = over_z(pa[3]), over_z(pa[2])

    piece_b = (b, by, bz, bo)
    hs_b, cs_b = [(x, 0) for x in piece_b], [(x, 1) for x in piece_b]
    dgu_b, dgu_tb, act_tb, pw_b = forward(own, hs_b, cs_b, weights, got_gu, got_d)
    dgu_b, za = barrier(dgu_b, za)
    fa = over_y(add(pa[1], za))
    *pb, norm_b = expert_rows(own, dgu_b, pw_b, hs_b, weights, got_gu)
    norm = (norm + norm_b) / gain
    hs, cs, dgu_t, act_t = hs_a + hs_b, cs_a + cs_b, (dgu_ta, dgu_tb), (act_ta, act_tb)
    grads = functools.partial(expert_weights, own=own, hs=hs, cs=cs, dgu_t=dgu_t, act_t=act_t)
    zb, yb = over_z(pb[3]), over_z(pb[2])
    packed_a = pack(tie(pa[0], pb[0]), ya, fa)
    (give_g,) = grads(1, (0,), after=(packed_a,))
    packed_a, give_g, norm = barrier(trade(packed_a), give_g, sum_dp(norm, 1))
    r_a = exchange(packed_a)
    (give_u,) = grads(1, (1,), after=(packed_a,))
    zb, give_u, norm = barrier(zb, give_u, sum_dp(norm, 2))
    far = add(pb[1], zb)
    fb = over_y(far)
    mine_gud = grads(0, (0, 1, 2), after=(far,))
    take_g, norm, mine_gud[0] = barrier(trade(give_g), sum_dp(norm, 4), mine_gud[0])
    (give_d,) = grads(1, (2,), after=(take_g,))
    yb, fb, norm, give_d = barrier(yb, fb, sum_dp(norm, 8), give_d)
    packed_b = pack(pb[0], yb, fb)
    norm = spread(norm)
    r_a, packed_b, take_u, norm = barrier(r_a, packed_b, trade(give_u), norm + over_z(norm))
    r_b = exchange(packed_b)
    take_d = trade(give_d)
    norm = norm + over_y(norm)
    norm = jnp.sum(norm + trade(norm), axis=0)
    out, grad_routes = combine(owns, r_b, r_a, h, c, gain, rrow, wrow)
    grad_routes = grad_routes.reshape(TOK, 1)
    grads = [
        lax.dynamic_update_index_in_dim(x, t, 1 - mine, 0)
        for x, t in zip(mine_gud, (take_g, take_u, take_d))
    ]
    return out, norm, grad_routes, *grads


def solution(mesh):
    tokens = P(("dp", "tensor"), None)
    weights = P("dp", "tensor", None)
    return jax.shard_map(
        body,
        mesh=mesh,
        in_specs=(tokens, tokens, P(), tokens, tokens, weights, weights, weights),
        out_specs=(tokens, P(), tokens, weights, weights, weights),
        check_vma=False,
    )
```

time: 800 us -> 330 us (0.41)
  waiting for transfers between devices: 375 us -> 130 us
  matrix products: 156 us -> 0 us
  Pallas kernels: 0 us -> 105 us
  local copies, waits for them, and re-layouts: 96 us -> 20.5 us
  blocking collectives: 68.3 us -> 0 us
  other arithmetic: 39.5 us -> 5.44 us
  starting transfers between devices: 56.6 us -> 65.6 us
    all_to_all x5 -> x4, waiting for transfers between devices: 375 us -> 85.8 us  [exchange(): got = lax.all_to_all(shaped, 'dp', split_axis=0, concat_axis=0, tiled=True)]
    dot_general x8 -> x0, matrix products: 156 us -> none  [the longest x1 22.7 us: expert_backward(): jnp.einsum('erd,efd->erf', rows_dy, w_down, preferred_element_type=jnp.fl...]
    pallas_call x0 -> x15, Pallas kernels: none -> 105 us  [the longest x4 35.7 us: expert_weights(): pl.pallas_call(functools.partial(weights_kernel, part, kinds), grid_spec=...]
    psum x1 -> x0, blocking collectives: 68.3 us -> none  [body(): lax.psum(jnp.sum(normalized_input_gradient * unit_scaled_input, axis=0),...]
    broadcast_in_dim x8 -> x0, local copies, waits for them, and re-layouts: 44.2 us -> none  [copies(): spread = jnp.broadcast_to(shaped, (n_data, n_slices, exp_dev, cap) + tail)]
    ppermute x0 -> x27, waiting for transfers between devices: none -> 44.1 us  [the longest x7 20.5 us: over_y(): return lax.ppermute(x, AXES, PERMS['y'])]
    ppermute x0 -> x27, starting transfers between devices: none -> 37.8 us  [the longest x7 16.5 us: trade(): return lax.ppermute(x, AXES, PERMS['trade'])]
    all_to_all x5 -> x4, starting transfers between devices: 56.6 us -> 27.8 us  [exchange(): got = lax.all_to_all(shaped, 'dp', split_axis=0, concat_axis=0, tiled=True)]
  transfers between devices with their start and end apart: 5 -> 31, of which waited for: 3 -> 13; matrix products, arithmetic and copies ran while one was open for 24% -> 5% of each run, Pallas kernels for 0% -> 31%
where the time goes in v2:
time: 330 us; the launch traced here: 328 us
  waiting for transfers between devices  130 us (39%)
  Pallas kernels  105 us (32%)
  starting transfers between devices  65.6 us (20%)
  local copies, waits for them, and re-layouts  20.5 us (6%)
  other arithmetic  5.44 us (2%)
    all_to_all x4, waiting for transfers between devices, exchange(): got = lax.all_to_all(shaped, 'dp', split_axis=0, concat_axis=0, tiled=True)  85.8 us
    pallas_call x4, Pallas kernels, expert_weights(): pl.pallas_call(functools.partial(weights_kernel, part, kinds), grid_spec=...  35.7 us
    all_to_all x4, starting transfers between devices, exchange(): got = lax.all_to_all(shaped, 'dp', split_axis=0, concat_axis=0, tiled=True)  27.8 us
    pallas_call x2, Pallas kernels, forward(): pl.pallas_call(forward_kernel, grid_spec=pltpu.PrefetchScalarGridSpec(num...  22 us
    ppermute x7, waiting for transfers between devices, over_y(): return lax.ppermute(x, AXES, PERMS['y'])  20.5 us
    pallas_call x2, Pallas kernels, expert_rows(): pl.pallas_call(rows_kernel, grid_spec=pltpu.PrefetchScalarGridSpec(num_sc...  20 us
    ppermute x7, starting transfers between devices, trade(): return lax.ppermute(x, AXES, PERMS['trade'])  16.5 us
    ppermute x7, waiting for transfers between devices, over_z(): return lax.ppermute(x, AXES, PERMS['z'])  10.9 us
  transfers between devices with their start and end apart: 31, of which 13 were waited for; matrix products, arithmetic and copies ran while one was open for 5% of the time, Pallas kernels for 31%

profile of v2, /device:TPU:1, one launch (start us, length us, event | category | flops | bytes accessed | tf_op | source)
XLA Modules:
  0.0 327.6 jit_solution(17264332514176301372)
XLA Ops:
  1.2 4.0 %dispatch.2 = (bf16[192,2048]{1,0:T(8,128)(2,1)}, bf16[192,2048]{1,0:T(8,128)(2,1)}) custom-call(s32[2]{0:T(128)} %pad_add_fusion.own_ref, bf16[128,4096]{1,0:T(8,128)(2,1)} %h_ref.5, bf16[128,4096]{1,0:T(8,128)(2,1)} %c_ref.5, f32[1,4096]{1,0:T(1,128)} %bitcast.38, s32[1,128]{1,0:T(1,128)} %bitcast.44, bf16[1,128]{1,0:T(2,128)(2,1)} %bitcast.47), custom_call_target="tpu_custom_call" | custom-call | flops 805306368 | bytes 4194304 | tf_op jit(solution)/shard_map/dispatch/pallas_call | solution.py:131
  11.5 4.1 %dispatch.3 = bf16[384,2048]{1,0:T(8,128)(2,1)} custom-call(s32[2]{0:T(128)} %pad_add_fusion.own_ref, bf16[128,4096]{1,0:T(8,128)(2,1)} %h_ref.5, bf16[128,4096]{1,0:T(8,128)(2,1)} %c_ref.5, f32[1,4096]{1,0:T(1,128)} %bitcast.39, s32[1,128]{1,0:T(1,128)} %bitcast.45, bf16[1,128]{1,0:T(2,128)(2,1)} %bitcast.48), custom_call_target="tpu_custom_call" | custom-call | flops 805306368 | bytes 4194304 | tf_op jit(solution)/shard_map/dispatch/pallas_call | solution.py:131
  17.6 6.8 %collective-permute-done = bf16[192,2048]{1,0:T(8,128)(2,1)S(1)} collective-permute-done((bf16[192,2048]{1,0:T(8,128)(2,1)}, bf16[192,2048]{1,0:T(8,128)(2,1)S(1)}, u32[]{:S(2)}, u32[]{:S(2)}) %collective-permute-start) | collective-permute-done | bytes 786464 | tf_op jit(solution)/shard_map/ppermute | solution.py:71
  32.5 7.7 %all-to-all-start = ((bf16[16,24,2048]{2,1,0:T(8,128)(2,1)}), bf16[16,24,2048]{2,1,0:T(8,128)(2,1)}, u32[]{:S(2)}, u32[]{:S(2)}) async-start(bf16[16,24,2048]{2,1,0:T(8,128)(2,1)} %bitcast.33), calls=%async_computation | async-start | bytes 3145728 | tf_op jit(solution)/shard_map/all_to_all | solution.py:438
  40.2 2.7 dynamic-slice_bitcast_fusion
  42.9 20.2 %all-to-all-done = bf16[16,24,2048]{2,1,0:T(8,128)(2,1)} async-done(((bf16[16,24,2048]{2,1,0:T(8,128)(2,1)}), bf16[16,24,2048]{2,1,0:T(8,128)(2,1)}, u32[]{:S(2)}, u32[]{:S(2)}) %all-to-all-start) | async-done | bytes 1572896 | tf_op jit(solution)/shard_map/all_to_all | solution.py:438
  63.1 3.7 %sort_rows.2.refs_0_.refs_4_.refs_8_ = bf16[192,4096]{1,0:T(8,128)(2,1)} custom-call(bf16[384,384]{1,0:T(8,128)(2,1)} %constant.38.clone.m_ref, bf16[384,2048]{1,0:T(8,128)(2,1)} %bitcast.13.x_ref), custom_call_target="tpu_custom_call" | custom-call | flops 603979776 | bytes 4194304 | tf_op jit(solution)/shard_map/sort_rows/pallas_call | solution.py:157
  69.2 6.2 %all-to-all-start.1 = ((bf16[16,24,2048]{2,1,0:T(8,128)(2,1)}), bf16[16,24,2048]{2,1,0:T(8,128)(2,1)}, u32[]{:S(2)}, u32[]{:S(2)}) async-start(bf16[16,24,2048]{2,1,0:T(8,128)(2,1)} %bitcast.32), calls=%async_computation.1 | async-start | bytes 3145728 | tf_op jit(solution)/shard_map/all_to_all | solution.py:438
  76.4 45.1 %all-to-all-done.1 = bf16[16,24,2048]{2,1,0:T(8,128)(2,1)} async-done(((bf16[16,24,2048]{2,1,0:T(8,128)(2,1)}), bf16[16,24,2048]{2,1,0:T(8,128)(2,1)}, u32[]{:S(2)}, u32[]{:S(2)}) %all-to-all-start.1) | async-done | bytes 1572896 | tf_op jit(solution)/shard_map/all_to_all | solution.py:438
  123.2 3.7 %sort_rows.3.refs_0_.refs_4_.refs_12_ = bf16[192,4096]{1,0:T(8,128)(2,1)} custom-call(bf16[384,384]{1,0:T(8,128)(2,1)} %constant.38.clone.m_ref, bf16[384,2048]{1,0:T(8,128)(2,1)} %bitcast.16.x_ref), custom_call_target="tpu_custom_call" | custom-call | flops 603979776 | bytes 4194304 | tf_op jit(solution)/shard_map/sort_rows/pallas_call | solution.py:157
  127.9 13.6 %collective-permute-done.7.refs_3_.refs_7_.refs_11_ = bf16[192,4096]{1,0:T(8,128)(2,1)S(1)} collective-permute-done((bf16[192,4096]{1,0:T(8,128)(2,1)}, bf16[192,4096]{1,0:T(8,128)(2,1)S(1)}, u32[]{:S(2)}, u32[]{:S(2)}) %collective-permute-start.7) | collective-permute-done | bytes 1572896 | tf_op jit(solution)/shard_map/ppermute | solution.py:75
  142.7 11.0 %expert_forward.2 = (bf16[384,768]{1,0:T(8,128)(2,1)}, bf16[768,384]{1,0:T(8,128)(2,1)}, bf16[384,384]{1,0:T(8,128)(2,1)}, bf16[384,128]{1,0:T(8,128)(2,1)}) custom-call(s32[1]{0:T(128)} %bitcast.2.own_ref, bf16[192,4096]{1,0:T(8,128)(2,1)} %sort_rows.2.refs_0_.refs_4_.refs_8_, bf16[192,4096]{1,0:T(8,128)(2,1)} %collective-permute-done.3.refs_1_.refs_5_.refs_9_, ...), custom_call_target="tpu_custom_call" | custom-call | flops 3623878656 | bytes 16777216 | tf_op jit(solution)/shard_map/expert_forward/pallas_call | solution.py:250
  153.7 8.8 %collective-permute-done.5.refs_2_.refs_6_.refs_14_ = bf16[192,4096]{1,0:T(8,128)(2,1)S(1)} collective-permute-done((bf16[192,4096]{1,0:T(8,128)(2,1)}, bf16[192,4096]{1,0:T(8,128)(2,1)S(1)}, u32[]{:S(2)}, u32[]{:S(2)}) %collective-permute-start.5) | collective-permute-done | bytes 1572896 | tf_op jit(solution)/shard_map/ppermute | solution.py:79
  163.5 10.0 %expert_rows.2 = (bf16[96,4224]{1,0:T(8,128)(2,1)}, bf16[96,4224]{1,0:T(8,128)(2,1)}, bf16[96,4224]{1,0:T(8,128)(2,1)}, bf16[96,4224]{1,0:T(8,128)(2,1)}, f32[1,4096]{1,0:T(1,128)}) custom-call(s32[1]{0:T(128)} %bitcast.2.own_ref, bf16[384,768]{1,0:T(8,128)(2,1)} %get-tuple-element.77.dgu_ref, bf16[384,128]{1,0:T(8,128)(2,1)} %get-tuple-element.78.pw_ref, ...), custom_call_target="tpu_custom_call" | custom-call | flops 2415919104 | bytes 10485760 | tf_op jit(solution)/shard_map/expert_rows/pallas_call | solution.py:293
  175.1 7.0 %collective-permute-done.9.refs_3_.refs_7_.refs_15_ = bf16[192,4096]{1,0:T(8,128)(2,1)S(1)} collective-permute-done((bf16[192,4096]{1,0:T(8,128)(2,1)S(1)}, bf16[192,4096]{1,0:T(8,128)(2,1)S(1)}, u32[]{:S(2)}, u32[]{:S(2)}) %collective-permute-start.9) | collective-permute-done | bytes 1572896 | tf_op jit(solution)/shard_map/ppermute | solution.py:75
  183.3 11.1 %expert_forward.3 = (bf16[384,768]{1,0:T(8,128)(2,1)}, bf16[768,384]{1,0:T(8,128)(2,1)}, bf16[384,384]{1,0:T(8,128)(2,1)}, bf16[384,128]{1,0:T(8,128)(2,1)}) custom-call(s32[1]{0:T(128)} %bitcast.2.own_ref, bf16[192,4096]{1,0:T(8,128)(2,1)} %sort_rows.3.refs_0_.refs_4_.refs_12_, bf16[192,4096]{1,0:T(8,128)(2,1)} %copy-done.3, bf16[192,4096]{1,0:T(8,128)(2,1)} %copy-done.2, ...), custom_call_target="tpu_custom_call" | custom-call | flops 3623878656 | bytes 16777216 | tf_op jit(solution)/shard_map/expert_forward/pallas_call | solution.py:250
  195.7 10.0 %expert_rows.3 = (bf16[96,4224]{1,0:T(8,128)(2,1)}, bf16[96,4224]{1,0:T(8,128)(2,1)}, bf16[96,4224]{1,0:T(8,128)(2,1)}, bf16[96,4224]{1,0:T(8,128)(2,1)}, f32[1,4096]{1,0:T(1,128)}) custom-call(s32[1]{0:T(128)} %bitcast.2.own_ref, bf16[384,768]{1,0:T(8,128)(2,1)} %get-tuple-element.84.dgu_ref, bf16[384,128]{1,0:T(8,128)(2,1)} %get-tuple-element.85.pw_ref, ...), custom_call_target="tpu_custom_call" | custom-call | flops 2415919104 | bytes 10485760 | tf_op jit(solution)/shard_map/expert_rows/pallas_call | solution.py:293
  210.0 3.3 %pack_rows.2.refs_10_ = bf16[384,1152]{1,0:T(8,128)(2,1)} custom-call(bf16[384,384]{1,0:T(8,128)(2,1)} %constant.39.clone.m_ref, bf16[96,4224]{1,0:T(8,128)(2,1)} %get-tuple-element.87.p_ref, bf16[96,4224]{1,0:T(8,128)(2,1)} %copy-done.12, bf16[96,4224]{1,0:T(8,128)(2,1)} %copy-done.13), custom_call_target="tpu_custom_call" | custom-call | flops 301989888 | bytes 4194304 | tf_op jit(solution)/shard_map/pack_rows/pallas_call | solution.py:393
  213.3 5.0 %collective-permute-start.13 = (bf16[384,1152]{1,0:T(8,128)(2,1)}, bf16[384,1152]{1,0:T(8,128)(2,1)}, u32[]{:S(2)}, u32[]{:S(2)}) collective-permute-start(bf16[384,1152]{1,0:T(8,128)(2,1)} %pack_rows.2.refs_10_), channel_id=1, source_target_pairs={{0,1},{1,0},{2,3},{3,2},{4,5},{5,4},{6,7},{7,6},{8,11},{9,10},{10,... | collective-permute-start | bytes 2654216 | tf_op jit(solution)/shard_map/ppermute | solution.py:67
  221.6 8.3 %expert_weights.4 = bf16[192,4096]{1,0:T(8,128)(2,1)} custom-call(s32[1]{0:T(128)} %bitcast.2.own_ref, bf16[192,4096]{1,0:T(8,128)(2,1)} %sort_rows.2.refs_0_.refs_4_.refs_8_, bf16[192,4096]{1,0:T(8,128)(2,1)} %collective-permute-done.3.refs_1_.refs_5_.refs_9_, bf16[192,4096]{1,0:T(8,128)(2,1)} %collective-permute-done.2.refs_2_.refs_6_.refs_10_, ...), custom_call_target="tpu_custom_call" | custom-call | flops 1207959552 | bytes 6291456 | tf_op jit(solution)/shard_map/expert_weights/pallas_call | solution.py:345
  231.7 8.2 %expert_weights.5 = bf16[192,4096]{1,0:T(8,128)(2,1)} custom-call(s32[1]{0:T(128)} %bitcast.2.own_ref, bf16[192,4096]{1,0:T(8,128)(2,1)} %sort_rows.2.refs_0_.refs_4_.refs_8_, bf16[192,4096]{1,0:T(8,128)(2,1)} %collective-permute-done.3.refs_1_.refs_5_.refs_9_, bf16[192,4096]{1,0:T(8,128)(2,1)} %collective-permute-done.2.refs_2_.refs_6_.refs_10_, ...), custom_call_target="tpu_custom_call" | custom-call | flops 1207959552 | bytes 6291456 | tf_op jit(solution)/shard_map/expert_weights/pallas_call | solution.py:345
  243.6 3.8 %collective-permute-start.22 = (bf16[192,4096]{1,0:T(8,128)(2,1)}, bf16[192,4096]{1,0:T(8,128)(2,1)}, u32[]{:S(2)}, u32[]{:S(2)}) collective-permute-start(bf16[192,4096]{1,0:T(8,128)(2,1)} %expert_weights.5), channel_id=1, source_target_pairs={{0,1},{1,0},{2,3},{3,2},{4,5},{5,4},{6,7},{7,6},{8,11},{9,10},{10,... | collective-permute-start | bytes 4718600 | tf_op jit(solution)/shard_map/ppermute | solution.py:67
  247.5 11.2 %expert_weights.6 = (bf16[2,192,4096]{2,1,0:T(8,128)(2,1)}, bf16[2,192,4096]{2,1,0:T(8,128)(2,1)}, bf16[2,192,4096]{2,1,0:T(8,128)(2,1)}) custom-call(s32[1]{0:T(128)} %bitcast.2.own_ref, bf16[192,4096]{1,0:T(8,128)(2,1)} %sort_rows.2.refs_0_.refs_4_.refs_8_, bf16[192,4096]{1,0:T(8,128)(2,1)} %collective-permute-done.3.refs_1_.refs_5_.refs_9_, ...), custom_call_target="tpu_custom_call" | custom-call | flops 3623878656 | bytes 18874368 | tf_op jit(solution)/shard_map/expert_weights/pallas_call | solution.py:345
  260.6 8.1 %expert_weights.7 = bf16[192,4096]{1,0:T(8,128)(2,1)} custom-call(s32[1]{0:T(128)} %bitcast.2.own_ref, bf16[192,4096]{1,0:T(8,128)(2,1)} %sort_rows.2.refs_0_.refs_4_.refs_8_, bf16[192,4096]{1,0:T(8,128)(2,1)} %collective-permute-done.3.refs_1_.refs_5_.refs_9_, bf16[192,4096]{1,0:T(8,128)(2,1)} %collective-permute-done.2.refs_2_.refs_6_.refs_10_, ...), custom_call_target="tpu_custom_call" | custom-call | flops 1207959552 | bytes 6291456 | tf_op jit(solution)/shard_map/expert_weights/pallas_call | solution.py:345
  270.7 10.0 %all-to-all-start.2 = ((bf16[16,24,1152]{2,1,0:T(8,128)(2,1)}), bf16[16,24,1152]{2,1,0:T(8,128)(2,1)S(1)}, u32[]{:S(2)}, u32[]{:S(2)}) async-start(bf16[16,24,1152]{2,1,0:T(8,128)(2,1)} %bitcast.17), calls=%async_computation.2 | async-start | bytes 1769472 | tf_op jit(solution)/shard_map/all_to_all | solution.py:438
  281.3 3.3 %pack_rows.3 = bf16[384,1152]{1,0:T(8,128)(2,1)} custom-call(bf16[384,384]{1,0:T(8,128)(2,1)} %constant.39.clone.m_ref, bf16[96,4224]{1,0:T(8,128)(2,1)} %get-tuple-element.86.p_ref, bf16[96,4224]{1,0:T(8,128)(2,1)} %copy-done.10, bf16[96,4224]{1,0:T(8,128)(2,1)} %copy-done.11), custom_call_target="tpu_custom_call" | custom-call | flops 301989888 | bytes 4194304 | tf_op jit(solution)/shard_map/pack_rows/pallas_call | solution.py:393
  284.7 11.4 %all-to-all-done.2 = bf16[16,24,1152]{2,1,0:T(8,128)(2,1)S(1)} async-done(((bf16[16,24,1152]{2,1,0:T(8,128)(2,1)}), bf16[16,24,1152]{2,1,0:T(8,128)(2,1)S(1)}, u32[]{:S(2)}, u32[]{:S(2)}) %all-to-all-start.2) | async-done | bytes 884768 | tf_op jit(solution)/shard_map/all_to_all | solution.py:438
  298.8 3.8 %all-to-all-start.3 = ((bf16[16,24,1152]{2,1,0:T(8,128)(2,1)}), bf16[16,24,1152]{2,1,0:T(8,128)(2,1)S(1)}, u32[]{:S(2)}, u32[]{:S(2)}) async-start(bf16[16,24,1152]{2,1,0:T(8,128)(2,1)} %bitcast.20), calls=%async_computation.3 | async-start | bytes 1769472 | tf_op jit(solution)/shard_map/all_to_all | solution.py:438
  302.6 2.5 collective-permute-start.25
  305.1 2.7 bitcast_dynamic-update-slice_fusion.1
  308.8 9.1 %all-to-all-done.3 = bf16[16,24,1152]{2,1,0:T(8,128)(2,1)S(1)} async-done(((bf16[16,24,1152]{2,1,0:T(8,128)(2,1)}), bf16[16,24,1152]{2,1,0:T(8,128)(2,1)S(1)}, u32[]{:S(2)}, u32[]{:S(2)}) %all-to-all-start.3) | async-done | bytes 884768 | tf_op jit(solution)/shard_map/all_to_all | solution.py:438
  318.8 5.5 %combine.1 = (bf16[128,4096]{1,0:T(8,128)(2,1)}, f32[1,128]{1,0:T(1,128)}) custom-call(s32[2]{0:T(128)} %pad_add_fusion.own_ref, bf16[384,1152]{1,0:T(8,128)(2,1)} %bitcast.35, bf16[384,1152]{1,0:T(8,128)(2,1)} %bitcast.34, bf16[128,4096]{1,0:T(8,128)(2,1)} %h_ref.5, bf16[128,4096]{1,0:T(8,128)(2,1)} %c_ref.5, f32[1,4096]{1,0:T(1,128)} %bitcast.40, ...), custom_call_target="tpu_custom_call" | custom-call | flops 805306368 | bytes 5242880 | tf_op jit(solution)/shard_map/combine/pallas_call | solution.py:423
  (114 shorter events, 54.9 us)
Async XLA Ops:
  5.2 19.2 %collective-permute-start = (bf16[192,2048]{1,0:T(8,128)(2,1)}, bf16[192,2048]{1,0:T(8,128)(2,1)S(1)}, u32[]{:S(2)}, u32[]{:S(2)}) collective-permute-start(bf16[192,2048]{1,0:T(8,128)(2,1)} %get-tuple-element.64), channel_id=1, source_target_pairs={{0,1},{1,0},{2,3},{3,2},{4,5},{5,4},{6,7},{7,6},{8,9},{9,8},{10,11... | collective-permute-start | bytes 2359304 | tf_op jit(solution)/shard_map/ppermute | solution.py:71
  7.4 19.5 %collective-permute-start.1 = (bf16[192,2048]{1,0:T(8,128)(2,1)}, bf16[192,2048]{1,0:T(8,128)(2,1)S(1)}, u32[]{:S(2)}, u32[]{:S(2)}) collective-permute-start(bf16[192,2048]{1,0:T(8,128)(2,1)} %get-tuple-element.65), channel_id=1, source_target_pairs={{0,3},{1,2},{2,1},{3,0},{4,7},{5,6},{6,5},{7,4},{8,11},{9,10},{10,... | collective-permute-start | bytes 2359304 | tf_op jit(solution)/shard_map/ppermute | solution.py:71
  27.7 93.7 %collective-permute-start.4 = (bf16[384,4096]{1,0:T(8,128)(2,1)}, bf16[384,4096]{1,0:T(8,128)(2,1)S(1)}, u32[]{:S(2)}, u32[]{:S(2)}) collective-permute-start(bf16[384,4096]{1,0:T(8,128)(2,1)} %pad_maximum_fusion), channel_id=1, source_target_pairs={{0,1},{1,0},{2,3},{3,2},{4,5},{5,4},{6,7},{7,6},{8,11},{9,10},{10,... | collective-permute-start | bytes 9437192 | tf_op jit(solution)/shard_map/ppermute | solution.py:67
  32.5 30.7 %all-to-all-start = ((bf16[16,24,2048]{2,1,0:T(8,128)(2,1)}), bf16[16,24,2048]{2,1,0:T(8,128)(2,1)}, u32[]{:S(2)}, u32[]{:S(2)}) async-start(bf16[16,24,2048]{2,1,0:T(8,128)(2,1)} %bitcast.33), calls=%async_computation | async-start | bytes 3145728 | tf_op jit(solution)/shard_map/all_to_all | solution.py:438
  66.8 54.6 %collective-permute-start.2 = (bf16[192,4096]{1,0:T(8,128)(2,1)}, bf16[192,4096]{1,0:T(8,128)(2,1)}, u32[]{:S(2)}, u32[]{:S(2)}) collective-permute-start(bf16[192,4096]{1,0:T(8,128)(2,1)} %sort_rows.2.refs_0_.refs_4_.refs_8_), channel_id=1, source_target_pairs={{0,4},{1,5},{2,6},{3,7},{4,0},{5,1},{6,2},{7,3},{8,12},{9,13},{10,... | collective-permute-start | bytes 4718600 | tf_op jit(solution)/shard_map/ppermute | solution.py:79
  67.6 53.9 %collective-permute-start.3 = (bf16[192,4096]{1,0:T(8,128)(2,1)}, bf16[192,4096]{1,0:T(8,128)(2,1)}, u32[]{:S(2)}, u32[]{:S(2)}) collective-permute-start(bf16[192,4096]{1,0:T(8,128)(2,1)} %sort_rows.2.refs_0_.refs_4_.refs_8_), channel_id=1, source_target_pairs={{0,3},{1,2},{2,1},{3,0},{4,7},{5,6},{6,5},{7,4},{8,9},{9,8},{10,11... | collective-permute-start | bytes 4718600 | tf_op jit(solution)/shard_map/ppermute | solution.py:75
  69.2 52.3 %all-to-all-start.1 = ((bf16[16,24,2048]{2,1,0:T(8,128)(2,1)}), bf16[16,24,2048]{2,1,0:T(8,128)(2,1)}, u32[]{:S(2)}, u32[]{:S(2)}) async-start(bf16[16,24,2048]{2,1,0:T(8,128)(2,1)} %bitcast.32), calls=%async_computation.1 | async-start | bytes 3145728 | tf_op jit(solution)/shard_map/all_to_all | solution.py:438
  75.4 52.5 %collective-permute-start.8 = (bf16[192,4096]{1,0:T(8,128)(2,1)}, bf16[192,4096]{1,0:T(8,128)(2,1)}, u32[]{:S(2)}, u32[]{:S(2)}) collective-permute-start(bf16[192,4096]{1,0:T(8,128)(2,1)} %dynamic-slice_bitcast_fusion), channel_id=1, source_target_pairs={{0,1},{1,0},{2,3},{3,2},{4,5},{5,4},{6,7},{7,6},{8,11},{9,10},{10,... | collective-permute-start | bytes 4718600 | tf_op jit(solution)/shard_map/ppermute | solution.py:67
  121.5 20.0 %collective-permute-start.7 = (bf16[192,4096]{1,0:T(8,128)(2,1)}, bf16[192,4096]{1,0:T(8,128)(2,1)S(1)}, u32[]{:S(2)}, u32[]{:S(2)}) collective-permute-start(bf16[192,4096]{1,0:T(8,128)(2,1)} %collective-permute-done.2.refs_2_.refs_6_.refs_10_), channel_id=1, source_target_pairs={{0,3},{1,2},{2,1},{3,0},{4,7},{5,6},{6,5},{7,4},{8,9},{9,8},{10,11... | collective-permute-start | bytes 4718600 | tf_op jit(solution)/shard_map/ppermute | solution.py:75
  126.8 35.6 %collective-permute-start.5 = (bf16[192,4096]{1,0:T(8,128)(2,1)}, bf16[192,4096]{1,0:T(8,128)(2,1)S(1)}, u32[]{:S(2)}, u32[]{:S(2)}) collective-permute-start(bf16[192,4096]{1,0:T(8,128)(2,1)} %sort_rows.3.refs_0_.refs_4_.refs_12_), channel_id=1, source_target_pairs={{0,4},{1,5},{2,6},{3,7},{4,0},{5,1},{6,2},{7,3},{8,12},{9,13},{10,... | collective-permute-start | bytes 4718600 | tf_op jit(solution)/shard_map/ppermute | solution.py:79
  126.8 35.6 %collective-permute-start.6 = (bf16[192,4096]{1,0:T(8,128)(2,1)}, bf16[192,4096]{1,0:T(8,128)(2,1)S(1)}, u32[]{:S(2)}, u32[]{:S(2)}) collective-permute-start(bf16[192,4096]{1,0:T(8,128)(2,1)} %sort_rows.3.refs_0_.refs_4_.refs_12_), channel_id=1, source_target_pairs={{0,3},{1,2},{2,1},{3,0},{4,7},{5,6},{6,5},{7,4},{8,9},{9,8},{10,11... | collective-permute-start | bytes 4718600 | tf_op jit(solution)/shard_map/ppermute | solution.py:75
  162.5 19.6 %collective-permute-start.9 = (bf16[192,4096]{1,0:T(8,128)(2,1)S(1)}, bf16[192,4096]{1,0:T(8,128)(2,1)S(1)}, u32[]{:S(2)}, u32[]{:S(2)}) collective-permute-start(bf16[192,4096]{1,0:T(8,128)(2,1)S(1)} %collective-permute-done.5.refs_2_.refs_6_.refs_14_), channel_id=1, source_target_pairs={{0,3},{1,2},{2,1},{3,0},{4,7},{5,6},{6,5},{7,4},{8,9},{9,8},{10,11... | collective-permute-start | bytes 4718600 | tf_op jit(solution)/shard_map/ppermute | solution.py:75
  173.6 20.8 %collective-permute-start.10 = (bf16[96,4224]{1,0:T(8,128)(2,1)}, bf16[96,4224]{1,0:T(8,128)(2,1)S(1)}, u32[]{:S(2)}, u32[]{:S(2)}) collective-permute-start(bf16[96,4224]{1,0:T(8,128)(2,1)} %get-tuple-element.83), channel_id=1, source_target_pairs={{0,4},{1,5},{2,6},{3,7},{4,0},{5,1},{6,2},{7,3},{8,12},{9,13},{10,... | collective-permute-start | bytes 2433032 | tf_op jit(solution)/shard_map/ppermute | solution.py:79
  174.0 20.4 %copy-start.15 = (bf16[96,4224]{1,0:T(8,128)(2,1)S(1)}, bf16[96,4224]{1,0:T(8,128)(2,1)}, u32[]{:S(2)}) copy-start(bf16[96,4224]{1,0:T(8,128)(2,1)} %get-tuple-element.89) | copy-start | bytes 2433028
  174.0 34.2 %collective-permute-start.11 = (bf16[96,4224]{1,0:T(8,128)(2,1)}, bf16[96,4224]{1,0:T(8,128)(2,1)S(1)}, u32[]{:S(2)}, u32[]{:S(2)}) collective-permute-start(bf16[96,4224]{1,0:T(8,128)(2,1)} %get-tuple-element.88), channel_id=1, source_target_pairs={{0,4},{1,5},{2,6},{3,7},{4,0},{5,1},{6,2},{7,3},{8,12},{9,13},{10,... | collective-permute-start | bytes 2433032 | tf_op jit(solution)/shard_map/ppermute | solution.py:79
  194.6 13.6 %collective-permute-start.12 = (bf16[96,4224]{1,0:T(8,128)(2,1)S(1)}, bf16[96,4224]{1,0:T(8,128)(2,1)S(1)}, u32[]{:S(2)}, u32[]{:S(2)}) collective-permute-start(bf16[96,4224]{1,0:T(8,128)(2,1)S(1)} %add_convert_fusion.1), channel_id=1, source_target_pairs={{0,3},{1,2},{2,1},{3,0},{4,7},{5,6},{6,5},{7,4},{8,9},{9,8},{10,11... | collective-permute-start | bytes 2433032 | tf_op jit(solution)/shard_map/ppermute | solution.py:75
  205.7 36.3 %collective-permute-start.16 = (bf16[96,4224]{1,0:T(8,128)(2,1)}, bf16[96,4224]{1,0:T(8,128)(2,1)S(1)}, u32[]{:S(2)}, u32[]{:S(2)}) collective-permute-start(bf16[96,4224]{1,0:T(8,128)(2,1)} %get-tuple-element.98), channel_id=1, source_target_pairs={{0,4},{1,5},{2,6},{3,7},{4,0},{5,1},{6,2},{7,3},{8,12},{9,13},{10,... | collective-permute-start | bytes 2433032 | tf_op jit(solution)/shard_map/ppermute | solution.py:79
  213.3 16.6 %collective-permute-start.13 = (bf16[384,1152]{1,0:T(8,128)(2,1)}, bf16[384,1152]{1,0:T(8,128)(2,1)}, u32[]{:S(2)}, u32[]{:S(2)}) collective-permute-start(bf16[384,1152]{1,0:T(8,128)(2,1)} %pack_rows.2.refs_10_), channel_id=1, source_target_pairs={{0,1},{1,0},{2,3},{3,2},{4,5},{5,4},{6,7},{7,6},{8,11},{9,10},{10,... | collective-permute-start | bytes 2654216 | tf_op jit(solution)/shard_map/ppermute | solution.py:67
  218.3 3.3 collective-permute-start.14
  220.8 48.0 %collective-permute-start.15 = (bf16[96,4224]{1,0:T(8,128)(2,1)S(1)}, bf16[96,4224]{1,0:T(8,128)(2,1)S(1)}, u32[]{:S(2)}, u32[]{:S(2)}) collective-permute-start(bf16[96,4224]{1,0:T(8,128)(2,1)S(1)} %copy-done.23), channel_id=1, source_target_pairs={{0,4},{1,5},{2,6},{3,7},{4,0},{5,1},{6,2},{7,3},{8,12},{9,13},{10,... | collective-permute-start | bytes 2433032 | tf_op jit(solution)/shard_map/ppermute | solution.py:79
  229.9 12.1 %collective-permute-start.17 = (f32[1,4096]{1,0:T(1,128)S(1)}, f32[1,4096]{1,0:T(1,128)S(1)}, u32[]{:S(2)}, u32[]{:S(2)}) collective-permute-start(f32[1,4096]{1,0:T(1,128)S(1)} %add.44), channel_id=1, source_target_pairs={{0,16},{8,24},{16,0},{24,8},{32,48},{40,56},{48,32},{56,40},{64,80... | collective-permute-start | bytes 49160 | tf_op jit(solution)/shard_map/ppermute | solution.py:188
  230.0 28.7 %collective-permute-start.19 = (bf16[192,4096]{1,0:T(8,128)(2,1)}, bf16[192,4096]{1,0:T(8,128)(2,1)S(1)}, u32[]{:S(2)}, u32[]{:S(2)}) collective-permute-start(bf16[192,4096]{1,0:T(8,128)(2,1)} %expert_weights.4), channel_id=1, source_target_pairs={{0,1},{1,0},{2,3},{3,2},{4,5},{5,4},{6,7},{7,6},{8,11},{9,10},{10,... | collective-permute-start | bytes 4718600 | tf_op jit(solution)/shard_map/ppermute | solution.py:67
  242.3 26.5 %collective-permute-start.18 = (bf16[96,4224]{1,0:T(8,128)(2,1)S(1)}, bf16[96,4224]{1,0:T(8,128)(2,1)S(1)}, u32[]{:S(2)}, u32[]{:S(2)}) collective-permute-start(bf16[96,4224]{1,0:T(8,128)(2,1)S(1)} %add_convert_fusion.refs_20_), channel_id=1, source_target_pairs={{0,3},{1,2},{2,1},{3,0},{4,7},{5,6},{6,5},{7,4},{8,9},{9,8},{10,11... | collective-permute-start | bytes 2433032 | tf_op jit(solution)/shard_map/ppermute | solution.py:75
  243.6 15.1 %collective-permute-start.20 = (f32[1,4096]{1,0:T(1,128)S(1)}, f32[1,4096]{1,0:T(1,128)S(1)}, u32[]{:S(2)}, u32[]{:S(2)}) collective-permute-start(f32[1,4096]{1,0:T(1,128)S(1)} %add.45), channel_id=1, source_target_pairs={{0,32},{8,40},{16,48},{24,56},{32,0},{40,8},{48,16},{56,24},{64,96... | collective-permute-start | bytes 49160 | tf_op jit(solution)/shard_map/ppermute | solution.py:188
  243.6 52.5 %collective-permute-start.22 = (bf16[192,4096]{1,0:T(8,128)(2,1)}, bf16[192,4096]{1,0:T(8,128)(2,1)}, u32[]{:S(2)}, u32[]{:S(2)}) collective-permute-start(bf16[192,4096]{1,0:T(8,128)(2,1)} %expert_weights.5), channel_id=1, source_target_pairs={{0,1},{1,0},{2,3},{3,2},{4,5},{5,4},{6,7},{7,6},{8,11},{9,10},{10,... | collective-permute-start | bytes 4718600 | tf_op jit(solution)/shard_map/ppermute | solution.py:67
  258.7 10.0 %collective-permute-start.21 = (f32[1,4096]{1,0:T(1,128)S(1)}, f32[1,4096]{1,0:T(1,128)S(1)}, u32[]{:S(2)}, u32[]{:S(2)}) collective-permute-start(f32[1,4096]{1,0:T(1,128)S(1)} %add.47), channel_id=1, source_target_pairs={{0,64},{8,72},{16,80},{24,88},{32,96},{40,104},{48,112},{56,120},{... | collective-permute-start | bytes 49160 | tf_op jit(solution)/shard_map/ppermute | solution.py:188
  269.8 14.8 %collective-permute-start.23 = (f32[8,4096]{1,0:T(8,128)S(1)}, f32[8,4096]{1,0:T(8,128)S(1)}, u32[]{:S(2)}, u32[]{:S(2)}) collective-permute-start(f32[8,4096]{1,0:T(8,128)S(1)} %broadcast_select_fusion), channel_id=1, source_target_pairs={{0,4},{1,5},{2,6},{3,7},{4,0},{5,1},{6,2},{7,3},{8,12},{9,13},{10,... | collective-permute-start | bytes 393224 | tf_op jit(solution)/shard_map/ppermute | solution.py:79
  270.7 25.3 %all-to-all-start.2 = ((bf16[16,24,1152]{2,1,0:T(8,128)(2,1)}), bf16[16,24,1152]{2,1,0:T(8,128)(2,1)S(1)}, u32[]{:S(2)}, u32[]{:S(2)}) async-start(bf16[16,24,1152]{2,1,0:T(8,128)(2,1)} %bitcast.17), calls=%async_computation.2 | async-start | bytes 1769472 | tf_op jit(solution)/shard_map/all_to_all | solution.py:438
  280.8 43.5 %collective-permute-start.26 = (bf16[192,4096]{1,0:T(8,128)(2,1)}, bf16[192,4096]{1,0:T(8,128)(2,1)}, u32[]{:S(2)}, u32[]{:S(2)}) collective-permute-start(bf16[192,4096]{1,0:T(8,128)(2,1)} %expert_weights.7), channel_id=1, source_target_pairs={{0,1},{1,0},{2,3},{3,2},{4,5},{5,4},{6,7},{7,6},{8,11},{9,10},{10,... | collective-permute-start | bytes 4718600 | tf_op jit(solution)/shard_map/ppermute | solution.py:67
  296.1 6.4 %collective-permute-start.24 = (f32[8,4096]{1,0:T(8,128)S(1)}, f32[8,4096]{1,0:T(8,128)S(1)}, u32[]{:S(2)}, u32[]{:S(2)}) collective-permute-start(f32[8,4096]{1,0:T(8,128)S(1)} %fusion), channel_id=1, source_target_pairs={{0,3},{1,2},{2,1},{3,0},{4,7},{5,6},{6,5},{7,4},{8,9},{9,8},{10,11... | collective-permute-start | bytes 393224 | tf_op jit(solution)/shard_map/ppermute | solution.py:75
  298.8 19.2 %all-to-all-start.3 = ((bf16[16,24,1152]{2,1,0:T(8,128)(2,1)}), bf16[16,24,1152]{2,1,0:T(8,128)(2,1)S(1)}, u32[]{:S(2)}, u32[]{:S(2)}) async-start(bf16[16,24,1152]{2,1,0:T(8,128)(2,1)} %bitcast.20), calls=%async_computation.3 | async-start | bytes 1769472 | tf_op jit(solution)/shard_map/all_to_all | solution.py:438
  302.6 5.6 %collective-permute-start.25 = (f32[8,4096]{1,0:T(8,128)S(1)}, f32[8,4096]{1,0:T(8,128)S(1)}, u32[]{:S(2)}, u32[]{:S(2)}) collective-permute-start(f32[8,4096]{1,0:T(8,128)S(1)} %add.50), channel_id=1, source_target_pairs={{0,1},{1,0},{2,3},{3,2},{4,5},{5,4},{6,7},{7,6},{8,11},{9,10},{10,... | collective-permute-start | bytes 393224 | tf_op jit(solution)/shard_map/ppermute | solution.py:67
  (23 other events, 148.2 us)

commit v3 on v2

--- a/solution.py
+++ b/solution.py
@@ -20,6 +20,7 @@
 PART = 4 * ROWS
 EXTRA = 128
 VMEM = 56 * 1024 * 1024
+F_STEP, W_STEP = 2048, 2048
 F32 = jnp.float32
 BF16 = jnp.bfloat16
 
@@ -82,6 +83,11 @@
 def owned():
     y = lax.axis_index("tensor") & 3
     return jnp.where((y == 0) | (y == 3), 1, 0).astype(jnp.int32), y >> 1
+
+
+def tree_barrier(tree):
+    leaves, shape = jax.tree.flatten(tree)
+    return jax.tree.unflatten(shape, barrier(*leaves))
 
 
 def column(row):
@@ -147,16 +153,18 @@
     return out
 
 
-def sort_kernel(m_ref, x_ref, out_ref):
+def sort_kernel(m_ref, x_ref, *outs):
+    n = 2 * ROWS // len(outs)
     for half in range(2):
-        rows = m_ref[half * 2 * ROWS : (half + 1) * 2 * ROWS, :]
-        out_ref[:, half * HALF : (half + 1) * HALF] = dot(rows, x_ref[...]).astype(BF16)
-
-
-def sort_rows(x):
+        for k, out in enumerate(outs):
+            lo = half * 2 * ROWS + k * n
+            out[:, half * HALF : (half + 1) * HALF] = dot(m_ref[lo : lo + n, :], x_ref[...]).astype(BF16)
+
+
+def sort_rows(x, parts):
     return pl.pallas_call(
         sort_kernel,
-        out_shape=jax.ShapeDtypeStruct((2 * ROWS, D), BF16),
+        out_shape=[jax.ShapeDtypeStruct((2 * ROWS // parts, D), BF16)] * parts,
         compiler_params=params(),
         cost_estimate=pl.CostEstimate(flops=2 * 384 * 384 * HALF, bytes_accessed=4 << 20, transcendentals=0),
         name="sort_rows",
@@ -190,6 +198,16 @@
 
 def spread(x):
     return jnp.where(iota((8, D), 0) == lax.axis_index("tensor"), x, 0.0)
+
+
+def reduce_first(left, right):
+    return (over_z(left[3]), over_z(left[2])), (over_y(right[3]), over_y(right[1]))
+
+
+def reduce_second(left, right, got_l, got_r):
+    sum_l = left[0], got_l[1], over_y(add(left[1], got_l[0]))
+    sum_r = right[0], got_r[1], over_z(add(right[2], got_r[0]))
+    return sum_l, sum_r
 
 
 def forward_kernel(own_ref, *refs):
@@ -242,8 +260,8 @@
         pw_ref[...] = value.astype(BF16)
 
 
-def forward(own, hs, cs, weights, got_gu, got_d):
-    step = 1024
+def forward(own, hs, cs, weights, got):
+    step = F_STEP
     specs, arrays = pieces(hs, cs, step)
     mine = pl.BlockSpec((1, SLICE, step), lambda s, own: (own[0], 0, s))
     shapes = [(PART, 4 * SLICE), (4 * SLICE, PART), (2 * SLICE, PART), (PART, EXTRA)]
@@ -252,7 +270,7 @@
         grid_spec=pltpu.PrefetchScalarGridSpec(
             num_scalar_prefetch=1,
             grid=(D // step,),
-            in_specs=specs + [mine] * 3 + slices(2, step) + slices(1, step),
+            in_specs=specs + [mine] * 3 + slices(1, step) * 3,
             out_specs=[whole(s) for s in shapes],
             scratch_shapes=[pltpu.VMEM((PART, 2 * SLICE), F32)] * 3,
         ),
@@ -262,49 +280,52 @@
             flops=2 * PART * 6 * SLICE * D, bytes_accessed=16 << 20, transcendentals=PART * 384
         ),
         name="expert_forward",
-    )(own, *arrays, *weights, got_gu, got_gu, got_d)
+    )(own, *arrays, *weights, *got)
 
 
 def rows_kernel(own_ref, dgu_ref, pw_ref, *refs):
     hs = refs[:4]
     gate_ref, up_ref, gate2_ref, up2_ref = refs[4:8]
-    outs, norm_ref = refs[8:12], refs[12]
+    left, right, norm_ref = refs[8:12], refs[12:16], refs[16]
     s = pl.program_id(0)
-    wide = gate_ref.shape[-1]
     w = jnp.concatenate([gate_ref[0], up_ref[0], gate2_ref[...], up2_ref[...]], axis=0)
     value = dot(dgu_ref[...], w)
     norm_ref[...] = jnp.sum(value * stack(hs).astype(F32), axis=0, keepdims=True)
     value = value.astype(BF16)
-    cols = pl.ds(pl.multiple_of(s * wide, wide), wide)
-    for k, out in enumerate(outs):
-        out[:, cols] = value[k * ROWS : (k + 1) * ROWS]
 
     @pl.when(s == 0)
     def _():
-        for k, out in enumerate(outs):
-            out[:, D:] = pw_ref[k * ROWS : (k + 1) * ROWS, :]
+        for k, out in enumerate(left):
+            out[...] = value[k * ROWS : (k + 1) * ROWS]
+
+    @pl.when(s == 1)
+    def _():
+        for k, out in enumerate(right):
+            out[:, :HALF] = value[k * ROWS : (k + 1) * ROWS]
+            out[:, HALF:] = pw_ref[k * ROWS : (k + 1) * ROWS, :]
 
 
 def expert_rows(own, dgu, pw, hs, weights, got):
-    wide = 512
+    wide = HALF
     mine = pl.BlockSpec((1, SLICE, wide), lambda s, own: (own[0], 0, s))
     specs, arrays = pieces(hs, [], wide)
-    shape = (ROWS, D + EXTRA)
-    return pl.pallas_call(
+    shapes = [(ROWS, HALF)] * 4 + [(ROWS, HALF + EXTRA)] * 4
+    *out, norm = pl.pallas_call(
         rows_kernel,
         grid_spec=pltpu.PrefetchScalarGridSpec(
             num_scalar_prefetch=1,
             grid=(D // wide,),
-            in_specs=[whole((PART, 4 * SLICE)), whole((PART, EXTRA))] + specs + [mine, mine] + slices(2, wide),
-            out_specs=[whole(shape)] * 4 + [pl.BlockSpec((1, wide), lambda s, own: (0, s))],
+            in_specs=[whole((PART, 4 * SLICE)), whole((PART, EXTRA))] + specs + [mine, mine] + slices(1, wide) * 2,
+            out_specs=[whole(x) for x in shapes] + [pl.BlockSpec((1, wide), lambda s, own: (0, s))],
         ),
-        out_shape=[jax.ShapeDtypeStruct(shape, BF16)] * 4 + [jax.ShapeDtypeStruct((1, D), F32)],
+        out_shape=[jax.ShapeDtypeStruct(x, BF16) for x in shapes] + [jax.ShapeDtypeStruct((1, D), F32)],
         compiler_params=params(),
         cost_estimate=pl.CostEstimate(
             flops=2 * PART * 4 * SLICE * D, bytes_accessed=10 << 20, transcendentals=0
         ),
         name="expert_rows",
-    )(own, dgu, pw, *arrays, weights[0], weights[1], got, got)
+    )(own, dgu, pw, *arrays, weights[0], weights[1], got[0], got[1])
+    return out[:4], out[4:], norm
 
 
 def weights_kernel(part, kinds, own_ref, *refs):
@@ -332,7 +353,7 @@
 
 
 def expert_weights(part, kinds, own, hs, cs, dgu_t, act_t, after):
-    wide = 512
+    wide = W_STEP
     hs, dgu_t = (hs, dgu_t) if 0 in kinds or 1 in kinds else ([], ())
     cs, act_t = (cs, act_t) if 2 in kinds else ([], ())
     specs, arrays = pieces(hs, cs, wide)
@@ -372,16 +393,19 @@
     return out
 
 
-def pack_kernel(m_ref, p_ref, q_ref, r_ref, out_ref):
-    def total(cols):
-        return p_ref[:, cols].astype(F32) + q_ref[:, cols].astype(F32) + r_ref[:, cols].astype(F32)
+def pack_kernel(m_ref, *refs):
+    left, right, out_ref = refs[:3], refs[3:6], refs[6]
+
+    def total(refs, cols):
+        p, q, r = [x[:, cols].astype(F32) for x in refs]
+        return p + q + r
 
     wide = 512
     for j in range(QUART // wide):
         lo = j * wide
-        rows = [total(slice(q * QUART + lo, q * QUART + lo + wide)).astype(BF16) for q in range(4)]
+        rows = [total(x, slice(at, at + wide)).astype(BF16) for x in (left, right) for at in (lo, lo + QUART)]
         out_ref[:, lo : lo + wide] = dot(m_ref[...], jnp.concatenate(rows, axis=0)).astype(BF16)
-    pw = total(slice(D, D + EXTRA))
+    pw = total(right, slice(HALF, HALF + EXTRA))
     pw = pw[:, 0:1] + pw[:, 1:2]
     high = pw.astype(BF16).astype(F32)
     lane = iota((ROWS, EXTRA), 1)
@@ -389,14 +413,14 @@
     out_ref[:, QUART:] = dot(m_ref[:, :ROWS], value).astype(BF16)
 
 
-def pack(p, q, r):
+def pack(left, right):
     return pl.pallas_call(
         pack_kernel,
         out_shape=jax.ShapeDtypeStruct((4 * ROWS, QUART + EXTRA), BF16),
         compiler_params=params(),
         cost_estimate=pl.CostEstimate(flops=2 * 384 * 384 * QUART, bytes_accessed=4 << 20, transcendentals=0),
         name="pack_rows",
-    )(jnp.asarray(pack_matrix(), BF16), p, q, r)
+    )(jnp.asarray(pack_matrix(), BF16), *left, *right)
 
 
 def combine_kernel(own_ref, r0_ref, r1_ref, h_ref, c_ref, gain_ref, rrow_ref, wrow_ref, out_ref, routes_ref):
@@ -449,58 +473,66 @@
     weights = (w_gate, w_up, w_down)
 
     slots_a = dispatch(1, owns, h, c, gain, rrow, wrow)
+    (slots_b,) = dispatch(0, owns, tie(h, *slots_a), c, gain, rrow, wrow)
     slots_a = [trade_for(core, x).reshape(N_DP // 2, -1, HALF) for core, x in enumerate(slots_a)]
-    (slots_b,) = dispatch(0, owns, h, c, gain, rrow, wrow)
+    got_b = exchange(slots_b)
     leave = [lax.dynamic_index_in_dim(x, 1 - mine, 0, keepdims=False) for x in weights]
-    leave_gu = jnp.concatenate(leave[:2], axis=0)
-    *slots_a, slots_b, leave_gu = barrier(*slots_a, slots_b, leave_gu)
+    got_g = trade(leave[0])
+    got_b, got_g, *slots_a, leave_u, leave_d = barrier(got_b, got_g, *slots_a, *leave[1:])
+    got_u = trade(leave_u)
+    bh, bc = sort_rows(got_b, 2)
     got_a = exchange(jnp.stack(slots_a, axis=1).reshape(4 * ROWS, HALF))
-    got_gu = trade(leave_gu)
-    got_a, leave_d = barrier(got_a, leave[2])
-    got_b = exchange(slots_b)
-    a = sort_rows(got_a)
+    got_a, got_u, bh, bc = barrier(got_a, got_u, bh, bc)
     got_d = trade(leave_d)
+    (a,) = sort_rows(got_a, 1)
     az, ay = over_z(a), over_y(a)
-    az, ay, got_b, got_gu = barrier(az, ay, got_b, got_gu)
-    b = sort_rows(got_b)
-    ao, bz, by = over_y(az), over_z(b), over_y(b)
+    az, ay, bh, bc, got_d = barrier(az, ay, bh, bc, got_d)
+    got = got_g, got_u, got_d
+    ao, bzh, bzc, byh, byc = over_y(az), over_z(bh), over_z(bc), over_y(bh), over_y(bc)
     piece_a = (a, ay, az, ao)
     hs_a, cs_a = [(x, 0) for x in piece_a], [(x, 1) for x in piece_a]
-    dgu_a, dgu_ta, act_ta, pw_a = forward(own, hs_a, cs_a, weights, got_gu, got_d)
-    bz, by, dgu_a = barrier(bz, by, dgu_a)
-    bo = over_y(bz)
-    *pa, norm = expert_rows(own, dgu_a, pw_a, hs_a, weights, got_gu)
-    za, ya = over_z(pa[3]), over_z(pa[2])
-
-    piece_b = (b, by, bz, bo)
-    hs_b, cs_b = [(x, 0) for x in piece_b], [(x, 1) for x in piece_b]
-    dgu_b, dgu_tb, act_tb, pw_b = forward(own, hs_b, cs_b, weights, got_gu, got_d)
-    dgu_b, za = barrier(dgu_b, za)
-    fa = over_y(add(pa[1], za))
-    *pb, norm_b = expert_rows(own, dgu_b, pw_b, hs_b, weights, got_gu)
-    norm = (norm + norm_b) / gain
+    dgu_a, dgu_ta, act_ta, pw_a = forward(own, hs_a, cs_a, weights, got)
+    bzh, bzc, byh, byc, dgu_a = barrier(bzh, bzc, byh, byc, dgu_a)
+    boh, boc = over_y(bzh), over_y(bzc)
+    la, ra, norm_a = expert_rows(own, dgu_a, pw_a, hs_a, weights, got)
+    al, ar = reduce_first(la, ra)
+
+    hs_b, cs_b = [(x, 0) for x in (bh, byh, bzh, boh)], [(x, 0) for x in (bc, byc, bzc, boc)]
+    dgu_b, dgu_tb, act_tb, pw_b = forward(own, hs_b, cs_b, weights, got)
+    dgu_b, *al, = barrier(dgu_b, *al)
+    dgu_b, *ar, = barrier(dgu_b, *ar)
+    al, ar = reduce_second(la, ra, al, ar)
+    lb, rb, norm_b = expert_rows(own, dgu_b, pw_b, hs_b, weights, got)
+    norm = (norm_a + norm_b) / gain
     hs, cs, dgu_t, act_t = hs_a + hs_b, cs_a + cs_b, (dgu_ta, dgu_tb), (act_ta, act_tb)
     grads = functools.partial(expert_weights, own=own, hs=hs, cs=cs, dgu_t=dgu_t, act_t=act_t)
-    zb, yb = over_z(pb[3]), over_z(pb[2])
-    packed_a = pack(tie(pa[0], pb[0]), ya, fa)
-    (give_g,) = grads(1, (0,), after=(packed_a,))
-    packed_a, give_g, norm = barrier(trade(packed_a), give_g, sum_dp(norm, 1))
+    lb, rb, al, ar, norm = tree_barrier((lb, rb, al, ar, norm))
+    bl, br = reduce_first(lb, rb)
+    packed_a = pack(al, ar)
+    norm, sent_a = barrier(sum_dp(norm, 1), packed_a)
+    packed_a = trade(packed_a)
+    (give_g,) = grads(1, (0,), after=(lb[0], sent_a, norm))
+    norm, give_g = barrier(sum_dp(norm, 4), give_g)
+    take_g = trade(give_g)
+    (give_u,) = grads(1, (1,), after=(give_g, norm))
+    norm, packed_a, give_u, *far = barrier(sum_dp(norm, 8), packed_a, give_u, *bl, *br)
+    sum_l, sum_r = add(lb[1], far[0]), add(rb[2], far[2])
+    sum_l, sum_r, packed_a, norm, give_u = barrier(sum_l, sum_r, packed_a, norm, give_u)
+    bl, br = (lb[0], far[1], over_y(sum_l)), (rb[0], far[3], over_z(sum_r))
+    take_u = trade(give_u)
     r_a = exchange(packed_a)
-    (give_u,) = grads(1, (1,), after=(packed_a,))
-    zb, give_u, norm = barrier(zb, give_u, sum_dp(norm, 2))
-    far = add(pb[1], zb)
-    fb = over_y(far)
-    mine_gud = grads(0, (0, 1, 2), after=(far,))
-    take_g, norm, mine_gud[0] = barrier(trade(give_g), sum_dp(norm, 4), mine_gud[0])
-    (give_d,) = grads(1, (2,), after=(take_g,))
-    yb, fb, norm, give_d = barrier(yb, fb, sum_dp(norm, 8), give_d)
-    packed_b = pack(pb[0], yb, fb)
-    norm = spread(norm)
-    r_a, packed_b, take_u, norm = barrier(r_a, packed_b, trade(give_u), norm + over_z(norm))
+    mine_gud = grads(0, (0, 1, 2), after=(sum_l, sum_r))
+    norm, mine_gud[0] = barrier(spread(sum_dp(norm, 2)), mine_gud[0])
+    (give_d,) = grads(1, (2,), after=(mine_gud[0], norm))
+    norm, give_d = barrier(norm + over_z(norm), give_d)
+    norm = norm + over_y(norm)
+    norm, *far = barrier(norm, *bl, *br)
+    norm = norm + trade(norm)
+    packed_b, r_a, take_g = barrier(pack(far[:3], far[3:]), r_a, take_g)
     r_b = exchange(packed_b)
     take_d = trade(give_d)
-    norm = norm + over_y(norm)
-    norm = jnp.sum(norm + trade(norm), axis=0)
+    r_b, take_u = barrier(r_b, take_u)
+    norm = jnp.sum(norm, axis=0)
     out, grad_routes = combine(owns, r_b, r_a, h, c, gain, rrow, wrow)
     grad_routes = grad_routes.reshape(TOK, 1)
     grads = [

time: 330 us -> 314 us (0.952)
  Pallas kernels: 105 us -> 88.9 us
  waiting for transfers between devices: 130 us -> 124 us
  starting transfers between devices: 65.6 us -> 69.8 us
    all_to_all x4, waiting for transfers between devices: 85.8 us -> 32.9 us  [exchange(): got = lax.all_to_all(shaped, 'dp', split_axis=0, concat_axis=0, tiled=True)]
    ppermute x7 -> x10, waiting for transfers between devices: 10.9 us -> 42.5 us  [over_z(): return lax.ppermute(x, AXES, PERMS['z'])]
    pallas_call x4, Pallas kernels: 35.7 us -> 24.1 us  [expert_weights(): pl.pallas_call(functools.partial(weights_kernel, part, kinds), grid_spec=...]
    ppermute x7 -> x13, waiting for transfers between devices: 20.5 us -> 30.6 us  [over_y(): return lax.ppermute(x, AXES, PERMS['y'])]
    ppermute x2, waiting for transfers between devices: 9.29 us -> 15.4 us  [trade_for(): lax.ppermute(x, 'tensor', [(t, move(core * 8 + t, 'trade') % 8) for t in...]
    ppermute x4, starting transfers between devices: 4.43 us -> 9.69 us  [sum_dp(): return x + lax.ppermute(x, 'dp', [(i, i ^ bit) for i in range(16)])]
    pallas_call x2, Pallas kernels: 20 us -> 15.8 us  [expert_rows(): pl.pallas_call(rows_kernel, grid_spec=pltpu.PrefetchScalarGridSpec(num_sc...]
    ppermute x7 -> x8, starting transfers between devices: 16.5 us -> 12.9 us  [trade(): return lax.ppermute(x, AXES, PERMS['trade'])]
  transfers between devices with their start and end apart: 31 -> 41, of which waited for: 13 -> 13; matrix products, arithmetic and copies ran while one was open for 5% -> 5% of each run, Pallas kernels for 31% -> 27%
where the time goes in v3:
time: 314 us; the launch traced here: 313 us
  waiting for transfers between devices  124 us (39%)
  Pallas kernels  88.9 us (28%)
  starting transfers between devices  69.8 us (22%)
  local copies, waits for them, and re-layouts  22.8 us (7%)
  other arithmetic  6.49 us (2%)
    ppermute x10, waiting for transfers between devices, over_z(): return lax.ppermute(x, AXES, PERMS['z'])  42.5 us
    all_to_all x4, waiting for transfers between devices, exchange(): got = lax.all_to_all(shaped, 'dp', split_axis=0, concat_axis=0, tiled=True)  32.9 us
    ppermute x13, waiting for transfers between devices, over_y(): return lax.ppermute(x, AXES, PERMS['y'])  30.6 us
    all_to_all x4, starting transfers between devices, exchange(): got = lax.all_to_all(shaped, 'dp', split_axis=0, concat_axis=0, tiled=True)  26.8 us
    pallas_call x4, Pallas kernels, expert_weights(): pl.pallas_call(functools.partial(weights_kernel, part, kinds), grid_spec=...  24.1 us
    pallas_call x2, Pallas kernels, forward(): pl.pallas_call(forward_kernel, grid_spec=pltpu.PrefetchScalarGridSpec(num...  21.3 us
    pallas_call x2, Pallas kernels, expert_rows(): pl.pallas_call(rows_kernel, grid_spec=pltpu.PrefetchScalarGridSpec(num_sc...  15.8 us
    ppermute x2, waiting for transfers between devices, trade_for(): lax.ppermute(x, 'tensor', [(t, move(core * 8 + t, 'trade') % 8) for t in...  15.4 us
  transfers between devices with their start and end apart: 41, of which 13 were waited for; matrix products, arithmetic and copies ran while one was open for 5% of the time, Pallas kernels for 27%

profile of v3, /device:TPU:1, one launch (start us, length us, event | category | flops | bytes accessed | tf_op | source)
XLA Modules:
  0.0 312.6 jit_solution(4238993500478677775)
XLA Ops:
  0.7 2.7 dynamic-slice_bitcast_fusion.2
  3.4 3.6 %collective-permute-start = (bf16[192,4096]{1,0:T(8,128)(2,1)}, bf16[192,4096]{1,0:T(8,128)(2,1)}, u32[]{:S(2)}, u32[]{:S(2)}) collective-permute-start(bf16[192,4096]{1,0:T(8,128)(2,1)} %dynamic-slice_bitcast_fusion.2), channel_id=1, source_target_pairs={{0,1},{1,0},{2,3},{3,2},{4,5},{5,4},{6,7},{7,6},{8,11},{9,10},{10,... | collective-permute-start | bytes 4718600 | tf_op jit(solution)/shard_map/ppermute | solution.py:68
  7.6 4.0 %dispatch.2 = (bf16[192,2048]{1,0:T(8,128)(2,1)}, bf16[192,2048]{1,0:T(8,128)(2,1)}) custom-call(s32[2]{0:T(128)} %pad_add_fusion.own_ref, bf16[128,4096]{1,0:T(8,128)(2,1)} %h_ref.4, bf16[128,4096]{1,0:T(8,128)(2,1)} %c_ref.5, f32[1,4096]{1,0:T(1,128)} %bitcast.38, s32[1,128]{1,0:T(1,128)} %bitcast.43, bf16[1,128]{1,0:T(2,128)(2,1)} %bitcast.46), custom_call_target="tpu_custom_call" | custom-call | flops 805306368 | bytes 4194304 | tf_op jit(solution)/shard_map/dispatch/pallas_call | solution.py:137
  11.6 4.1 %dispatch.3 = bf16[384,2048]{1,0:T(8,128)(2,1)} custom-call(s32[2]{0:T(128)} %pad_add_fusion.own_ref, bf16[128,4096]{1,0:T(8,128)(2,1)} %h_ref.4, bf16[128,4096]{1,0:T(8,128)(2,1)} %c_ref.5, f32[1,4096]{1,0:T(1,128)} %bitcast.39, s32[1,128]{1,0:T(1,128)} %bitcast.44, bf16[1,128]{1,0:T(2,128)(2,1)} %bitcast.47), custom_call_target="tpu_custom_call" | custom-call | flops 805306368 | bytes 4194304 | tf_op jit(solution)/shard_map/dispatch/pallas_call | solution.py:137
  15.7 8.0 %all-to-all-start = ((bf16[16,24,2048]{2,1,0:T(8,128)(2,1)}), bf16[16,24,2048]{2,1,0:T(8,128)(2,1)}, u32[]{:S(2)}, u32[]{:S(2)}) async-start(bf16[16,24,2048]{2,1,0:T(8,128)(2,1)} %bitcast.32), calls=%async_computation | async-start | bytes 3145728 | tf_op jit(solution)/shard_map/all_to_all | solution.py:462
  25.4 3.3 %dynamic-slice_bitcast_fusion = (bf16[192,4096]{1,0:T(8,128)(2,1)}, bf16[192,4096]{1,0:T(8,128)(2,1)}) fusion(bf16[2,192,4096]{2,1,0:T(8,128)(2,1)} %refs_10_.3, s32[]{:T(128)S(6)} %select_n.24, bf16[2,192,4096]{2,1,0:T(8,128)(2,1)S(1)} %copy-done.3), kind=kLoop, calls=%fused_computation.4 | loop fusion | bytes 6291460 | tf_op jit(solution)/shard_map/jit(dynamic_index_in_dim)/squeeze | solution.py:479
  28.7 15.4 %collective-permute-done.2 = bf16[192,2048]{1,0:T(8,128)(2,1)} collective-permute-done((bf16[192,2048]{1,0:T(8,128)(2,1)}, bf16[192,2048]{1,0:T(8,128)(2,1)}, u32[]{:S(2)}, u32[]{:S(2)}) %collective-permute-start.2) | collective-permute-done | bytes 786464 | tf_op jit(solution)/shard_map/ppermute | solution.py:72
  50.7 4.9 %all-to-all-start.1 = ((bf16[16,24,2048]{2,1,0:T(8,128)(2,1)}), bf16[16,24,2048]{2,1,0:T(8,128)(2,1)S(1)}, u32[]{:S(2)}, u32[]{:S(2)}) async-start(bf16[16,24,2048]{2,1,0:T(8,128)(2,1)} %bitcast.15), calls=%async_computation.1 | async-start | bytes 3145728 | tf_op jit(solution)/shard_map/all_to_all | solution.py:462
  56.8 3.7 %sort_rows.2 = (bf16[96,4096]{1,0:T(8,128)(2,1)}, bf16[96,4096]{1,0:T(8,128)(2,1)}) custom-call(bf16[384,384]{1,0:T(8,128)(2,1)} %constant.38.clone.m_ref, bf16[384,2048]{1,0:T(8,128)(2,1)} %bitcast.7.x_ref), custom_call_target="tpu_custom_call" | custom-call | flops 603979776 | bytes 4194304 | tf_op jit(solution)/shard_map/sort_rows/pallas_call | solution.py:165
  60.5 17.8 %all-to-all-done.1 = bf16[16,24,2048]{2,1,0:T(8,128)(2,1)S(1)} async-done(((bf16[16,24,2048]{2,1,0:T(8,128)(2,1)}), bf16[16,24,2048]{2,1,0:T(8,128)(2,1)S(1)}, u32[]{:S(2)}, u32[]{:S(2)}) %all-to-all-start.1) | async-done | bytes 1572896 | tf_op jit(solution)/shard_map/all_to_all | solution.py:462
  80.0 3.8 %sort_rows.3.refs_0_.refs_4_.refs_8_ = bf16[192,4096]{1,0:T(8,128)(2,1)} custom-call(bf16[384,384]{1,0:T(8,128)(2,1)} %constant.38.clone.m_ref, bf16[384,2048]{1,0:T(8,128)(2,1)} %bitcast.33), custom_call_target="tpu_custom_call" | custom-call | flops 603979776 | bytes 4194304 | tf_op jit(solution)/shard_map/sort_rows/pallas_call | solution.py:165
  85.7 33.4 %collective-permute-done.4.refs_2_.refs_6_.refs_10_ = bf16[192,4096]{1,0:T(8,128)(2,1)S(1)} collective-permute-done((bf16[192,4096]{1,0:T(8,128)(2,1)}, bf16[192,4096]{1,0:T(8,128)(2,1)S(1)}, u32[]{:S(2)}, u32[]{:S(2)}) %collective-permute-start.4) | collective-permute-done | bytes 1572896 | tf_op jit(solution)/shard_map/ppermute | solution.py:80
  123.2 15.5 %collective-permute-done.11.refs_3_.refs_7_.refs_11_ = bf16[192,4096]{1,0:T(8,128)(2,1)S(1)} collective-permute-done((bf16[192,4096]{1,0:T(8,128)(2,1)S(1)}, bf16[192,4096]{1,0:T(8,128)(2,1)S(1)}, u32[]{:S(2)}, u32[]{:S(2)}) %collective-permute-start.11) | collective-permute-done | bytes 1572896 | tf_op jit(solution)/shard_map/ppermute | solution.py:76
  139.9 10.7 %expert_forward.2 = (bf16[384,768]{1,0:T(8,128)(2,1)}, bf16[768,384]{1,0:T(8,128)(2,1)}, bf16[384,384]{1,0:T(8,128)(2,1)}, bf16[384,128]{1,0:T(8,128)(2,1)}) custom-call(s32[1]{0:T(128)} %bitcast.2.own_ref, bf16[192,4096]{1,0:T(8,128)(2,1)} %sort_rows.3.refs_0_.refs_4_.refs_8_, bf16[192,4096]{1,0:T(8,128)(2,1)} %copy-done.1, bf16[192,4096]{1,0:T(8,128)(2,1)} %copy-done, ...), custom_call_target="tpu_custom_call" | custom-call | flops 3623878656 | bytes 16777216 | tf_op jit(solution)/shard_map/expert_forward/pallas_call | solution.py:268
  157.2 7.9 %expert_rows.2 = (bf16[96,2048]{1,0:T(8,128)(2,1)}, bf16[96,2048]{1,0:T(8,128)(2,1)}, bf16[96,2048]{1,0:T(8,128)(2,1)}, bf16[96,2048]{1,0:T(8,128)(2,1)}, bf16[9...) custom-call(s32[1]{0:T(128)} %bitcast.2.own_ref, ...), custom_call_target="tpu_custom_call" | custom-call | flops 2415919104 | bytes 10485760 | tf_op jit(solution)/shard_map/expert_rows/pallas_call | solution.py:313
  168.2 7.1 %collective-permute-done.13.refs_7_.refs_15_ = bf16[96,4096]{1,0:T(8,128)(2,1)S(1)} collective-permute-done((bf16[96,4096]{1,0:T(8,128)(2,1)}, bf16[96,4096]{1,0:T(8,128)(2,1)S(1)}, u32[]{:S(2)}, u32[]{:S(2)}) %collective-permute-start.13) | collective-permute-done | bytes 786464 | tf_op jit(solution)/shard_map/ppermute | solution.py:76
  176.2 10.6 %expert_forward.3 = (bf16[384,768]{1,0:T(8,128)(2,1)}, bf16[768,384]{1,0:T(8,128)(2,1)}, bf16[384,384]{1,0:T(8,128)(2,1)}, bf16[384,128]{1,0:T(8,128)(2,1)}) custom-call(s32[1]{0:T(128)} %bitcast.2.own_ref, bf16[96,4096]{1,0:T(8,128)(2,1)} %get-tuple-element.128.refs_0_.refs_4_, bf16[96,4096]{1,0:T(8,128)(2,1)} %copy-done.7, bf16[96,4096]{1,0:T(8,128)(2,1)} %copy-done.6, ...), custom_call_target="tpu_custom_call" | custom-call | flops 3623878656 | bytes 16777216 | tf_op jit(solution)/shard_map/expert_forward/pallas_call | solution.py:268
  189.1 7.9 %expert_rows.3 = (bf16[96,2048]{1,0:T(8,128)(2,1)}, bf16[96,2048]{1,0:T(8,128)(2,1)}, bf16[96,2048]{1,0:T(8,128)(2,1)}, bf16[96,2048]{1,0:T(8,128)(2,1)}, bf16[9...) custom-call(s32[1]{0:T(128)} %bitcast.2.own_ref, ...), custom_call_target="tpu_custom_call" | custom-call | flops 2415919104 | bytes 10485760 | tf_op jit(solution)/shard_map/expert_rows/pallas_call | solution.py:313
  198.7 3.3 %pack_rows.2.refs_11_ = bf16[384,1152]{1,0:T(8,128)(2,1)} custom-call(bf16[384,384]{1,0:T(8,128)(2,1)} %constant.39.clone.m_ref, bf16[96,2048]{1,0:T(8,128)(2,1)} %get-tuple-element.170.refs_0_, bf16[96,2048]{1,0:T(8,128)(2,1)} %copy-done.25, bf16[96,2048]{1,0:T(8,128)(2,1)} %copy-done.26, bf16[96,2176]{1,0:T(8,128)(2,1)} %get-tuple-element.173.refs_3_, ...), custom_call_target="tpu_custom_call" | custom-call | flops 301989888 | bytes 4194304 | tf_op jit(solution)/shard_map/pack_rows/pallas_call | solution.py:417
  203.4 5.1 %collective-permute-start.20 = (f32[1,4096]{1,0:T(1,128)S(1)}, f32[1,4096]{1,0:T(1,128)S(1)}, u32[]{:S(2)}, u32[]{:S(2)}) collective-permute-start(f32[1,4096]{1,0:T(1,128)S(1)} %add_divide_fusion), channel_id=1, source_target_pairs={{0,8},{8,0},{16,24},{24,16},{32,40},{40,32},{48,56},{56,48},{64,72... | collective-permute-start | bytes 49160 | tf_op jit(solution)/shard_map/ppermute | solution.py:196
  211.0 5.2 %expert_weights.4.refs_10_ = bf16[192,4096]{1,0:T(8,128)(2,1)} custom-call(s32[1]{0:T(128)} %bitcast.2.own_ref, bf16[192,4096]{1,0:T(8,128)(2,1)} %sort_rows.3.refs_0_.refs_4_.refs_8_, bf16[192,4096]{1,0:T(8,128)(2,1)} %copy-done.1, bf16[192,4096]{1,0:T(8,128)(2,1)} %copy-done, bf16[192,4096]{1,0:T(8,128)(2,1)} %copy-done.2, ...), custom_call_target="tpu_custom_call" | custom-call | flops 1207959552 | bytes 6291456 | tf_op jit(solution)/shard_map/expert_weights/pallas_call | solution.py:366
  221.9 5.3 %expert_weights.5 = bf16[192,4096]{1,0:T(8,128)(2,1)} custom-call(s32[1]{0:T(128)} %bitcast.2.own_ref, bf16[192,4096]{1,0:T(8,128)(2,1)} %sort_rows.3.refs_0_.refs_4_.refs_8_, bf16[192,4096]{1,0:T(8,128)(2,1)} %copy-done.1, bf16[192,4096]{1,0:T(8,128)(2,1)} %copy-done, bf16[192,4096]{1,0:T(8,128)(2,1)} %copy-done.2, ...), custom_call_target="tpu_custom_call" | custom-call | flops 1207959552 | bytes 6291456 | tf_op jit(solution)/shard_map/expert_weights/pallas_call | solution.py:366
  229.4 5.9 %collective-permute-done.25.refs_1_ = bf16[96,2048]{1,0:T(8,128)(2,1)S(1)} collective-permute-done((bf16[96,2048]{1,0:T(8,128)(2,1)S(1)}, bf16[96,2048]{1,0:T(8,128)(2,1)S(1)}, u32[]{:S(2)}, u32[]{:S(2)}) %collective-permute-start.25) | collective-permute-done | bytes 393248 | tf_op jit(solution)/shard_map/ppermute | solution.py:80
  235.6 3.1 collective-permute-start.28
  241.1 7.4 %all-to-all-start.2 = ((bf16[16,24,1152]{2,1,0:T(8,128)(2,1)}), bf16[16,24,1152]{2,1,0:T(8,128)(2,1)S(1)}, u32[]{:S(2)}, u32[]{:S(2)}) async-start(bf16[16,24,1152]{2,1,0:T(8,128)(2,1)} %bitcast.37), calls=%async_computation.2 | async-start | bytes 1769472 | tf_op jit(solution)/shard_map/all_to_all | solution.py:462
  249.8 8.7 %expert_weights.6 = (bf16[2,192,4096]{2,1,0:T(8,128)(2,1)}, bf16[2,192,4096]{2,1,0:T(8,128)(2,1)}, bf16[2,192,4096]{2,1,0:T(8,128)(2,1)}) custom-call(s32[1]{0:T(128)} %bitcast.2.own_ref, bf16[192,4096]{1,0:T(8,128)(2,1)} %sort_rows.3.refs_0_.refs_4_.refs_8_, bf16[192,4096]{1,0:T(8,128)(2,1)} %copy-done.1, bf16[192,4096]{1,0:T(8,128)(2,1)} %copy-done, ...), custom_call_target="tpu_custom_call" | custom-call | flops 3623878656 | bytes 18874368 | tf_op jit(solution)/shard_map/expert_weights/pallas_call | solution.py:366
  259.3 4.9 %expert_weights.7 = bf16[192,4096]{1,0:T(8,128)(2,1)} custom-call(s32[1]{0:T(128)} %bitcast.2.own_ref, bf16[192,4096]{1,0:T(8,128)(2,1)} %sort_rows.3.refs_0_.refs_4_.refs_8_, bf16[192,4096]{1,0:T(8,128)(2,1)} %copy-done.1, bf16[192,4096]{1,0:T(8,128)(2,1)} %copy-done, bf16[192,4096]{1,0:T(8,128)(2,1)} %copy-done.2, ...), custom_call_target="tpu_custom_call" | custom-call | flops 1207959552 | bytes 6291456 | tf_op jit(solution)/shard_map/expert_weights/pallas_call | solution.py:366
  266.2 5.4 %collective-permute-done.30 = f32[8,4096]{1,0:T(8,128)S(1)} collective-permute-done((f32[8,4096]{1,0:T(8,128)S(1)}, f32[8,4096]{1,0:T(8,128)S(1)}, u32[]{:S(2)}, u32[]{:S(2)}) %collective-permute-start.30) | collective-permute-done | bytes 131104 | tf_op jit(solution)/shard_map/ppermute | solution.py:76
  274.4 3.3 %pack_rows.3 = bf16[384,1152]{1,0:T(8,128)(2,1)} custom-call(bf16[384,384]{1,0:T(8,128)(2,1)} %constant.39.clone.m_ref, bf16[96,2048]{1,0:T(8,128)(2,1)} %get-tuple-element.205.refs_10_.refs_0_, bf16[96,2048]{1,0:T(8,128)(2,1)} %copy-done.24, bf16[96,2048]{1,0:T(8,128)(2,1)} %collective-permute-done.31.refs_2_, bf16[96,2176]{1,0:T(8,128)(2,1)} %get-tuple-element.208.refs_3_, ...), custom_call_target="tpu_custom_call" | custom-call | flops 301989888 | bytes 4194304 | tf_op jit(solution)/shard_map/pack_rows/pallas_call | solution.py:417
  278.3 6.5 %all-to-all-start.3 = ((bf16[16,24,1152]{2,1,0:T(8,128)(2,1)}), bf16[16,24,1152]{2,1,0:T(8,128)(2,1)S(1)}, u32[]{:S(2)}, u32[]{:S(2)}) async-start(bf16[16,24,1152]{2,1,0:T(8,128)(2,1)} %bitcast.34), calls=%async_computation.3 | async-start | bytes 1769472 | tf_op jit(solution)/shard_map/all_to_all | solution.py:462
  287.5 12.6 %all-to-all-done.3 = bf16[16,24,1152]{2,1,0:T(8,128)(2,1)S(1)} async-done(((bf16[16,24,1152]{2,1,0:T(8,128)(2,1)}), bf16[16,24,1152]{2,1,0:T(8,128)(2,1)S(1)}, u32[]{:S(2)}, u32[]{:S(2)}) %all-to-all-start.3) | async-done | bytes 884768 | tf_op jit(solution)/shard_map/all_to_all | solution.py:462
  301.0 5.5 %combine.1 = (bf16[128,4096]{1,0:T(8,128)(2,1)}, f32[1,128]{1,0:T(1,128)}) custom-call(s32[2]{0:T(128)} %pad_add_fusion.own_ref, bf16[384,1152]{1,0:T(8,128)(2,1)} %bitcast.36, bf16[384,1152]{1,0:T(8,128)(2,1)} %bitcast.35, bf16[128,4096]{1,0:T(8,128)(2,1)} %h_ref.4, bf16[128,4096]{1,0:T(8,128)(2,1)} %c_ref.5, f32[1,4096]{1,0:T(1,128)} %bitcast.40, ...), custom_call_target="tpu_custom_call" | custom-call | flops 805306368 | bytes 5242880 | tf_op jit(solution)/shard_map/combine/pallas_call | solution.py:447
  (169 shorter events, 64.8 us)
Async XLA Ops:
  3.4 43.3 %collective-permute-start = (bf16[192,4096]{1,0:T(8,128)(2,1)}, bf16[192,4096]{1,0:T(8,128)(2,1)}, u32[]{:S(2)}, u32[]{:S(2)}) collective-permute-start(bf16[192,4096]{1,0:T(8,128)(2,1)} %dynamic-slice_bitcast_fusion.2), channel_id=1, source_target_pairs={{0,1},{1,0},{2,3},{3,2},{4,5},{5,4},{6,7},{7,6},{8,11},{9,10},{10,... | collective-permute-start | bytes 4718600 | tf_op jit(solution)/shard_map/ppermute | solution.py:68
  15.7 31.0 %all-to-all-start = ((bf16[16,24,2048]{2,1,0:T(8,128)(2,1)}), bf16[16,24,2048]{2,1,0:T(8,128)(2,1)}, u32[]{:S(2)}, u32[]{:S(2)}) async-start(bf16[16,24,2048]{2,1,0:T(8,128)(2,1)} %bitcast.32), calls=%async_computation | async-start | bytes 3145728 | tf_op jit(solution)/shard_map/all_to_all | solution.py:462
  23.7 20.4 %collective-permute-start.2 = (bf16[192,2048]{1,0:T(8,128)(2,1)}, bf16[192,2048]{1,0:T(8,128)(2,1)}, u32[]{:S(2)}, u32[]{:S(2)}) collective-permute-start(bf16[192,2048]{1,0:T(8,128)(2,1)} %get-tuple-element.116), channel_id=1, source_target_pairs={{0,3},{1,2},{2,1},{3,0},{4,7},{5,6},{6,5},{7,4},{8,11},{9,10},{10,... | collective-permute-start | bytes 2359304 | tf_op jit(solution)/shard_map/ppermute | solution.py:72
  25.0 19.2 %collective-permute-start.1 = (bf16[192,2048]{1,0:T(8,128)(2,1)}, bf16[192,2048]{1,0:T(8,128)(2,1)}, u32[]{:S(2)}, u32[]{:S(2)}) collective-permute-start(bf16[192,2048]{1,0:T(8,128)(2,1)} %get-tuple-element.115), channel_id=1, source_target_pairs={{0,1},{1,0},{2,3},{3,2},{4,5},{5,4},{6,7},{7,6},{8,9},{9,8},{10,11... | collective-permute-start | bytes 2359304 | tf_op jit(solution)/shard_map/ppermute | solution.py:72
  46.6 31.8 %collective-permute-start.3 = (bf16[192,4096]{1,0:T(8,128)(2,1)}, bf16[192,4096]{1,0:T(8,128)(2,1)S(1)}, u32[]{:S(2)}, u32[]{:S(2)}) collective-permute-start(bf16[192,4096]{1,0:T(8,128)(2,1)} %get-tuple-element.120), channel_id=1, source_target_pairs={{0,1},{1,0},{2,3},{3,2},{4,5},{5,4},{6,7},{7,6},{8,11},{9,10},{10,... | collective-permute-start | bytes 4718600 | tf_op jit(solution)/shard_map/ppermute | solution.py:68
  50.7 27.7 %all-to-all-start.1 = ((bf16[16,24,2048]{2,1,0:T(8,128)(2,1)}), bf16[16,24,2048]{2,1,0:T(8,128)(2,1)S(1)}, u32[]{:S(2)}, u32[]{:S(2)}) async-start(bf16[16,24,2048]{2,1,0:T(8,128)(2,1)} %bitcast.15), calls=%async_computation.1 | async-start | bytes 3145728 | tf_op jit(solution)/shard_map/all_to_all | solution.py:462
  55.5 30.1 %collective-permute-start.6 = (bf16[192,4096]{1,0:T(8,128)(2,1)}, bf16[192,4096]{1,0:T(8,128)(2,1)}, u32[]{:S(2)}, u32[]{:S(2)}) collective-permute-start(bf16[192,4096]{1,0:T(8,128)(2,1)} %get-tuple-element.127), channel_id=1, source_target_pairs={{0,1},{1,0},{2,3},{3,2},{4,5},{5,4},{6,7},{7,6},{8,11},{9,10},{10,... | collective-permute-start | bytes 4718600 | tf_op jit(solution)/shard_map/ppermute | solution.py:68
  83.8 35.3 %collective-permute-start.4 = (bf16[192,4096]{1,0:T(8,128)(2,1)}, bf16[192,4096]{1,0:T(8,128)(2,1)S(1)}, u32[]{:S(2)}, u32[]{:S(2)}) collective-permute-start(bf16[192,4096]{1,0:T(8,128)(2,1)} %sort_rows.3.refs_0_.refs_4_.refs_8_), channel_id=1, source_target_pairs={{0,4},{1,5},{2,6},{3,7},{4,0},{5,1},{6,2},{7,3},{8,12},{9,13},{10,... | collective-permute-start | bytes 4718600 | tf_op jit(solution)/shard_map/ppermute | solution.py:80
  84.6 34.5 %collective-permute-start.5 = (bf16[192,4096]{1,0:T(8,128)(2,1)}, bf16[192,4096]{1,0:T(8,128)(2,1)S(1)}, u32[]{:S(2)}, u32[]{:S(2)}) collective-permute-start(bf16[192,4096]{1,0:T(8,128)(2,1)} %sort_rows.3.refs_0_.refs_4_.refs_8_), channel_id=1, source_target_pairs={{0,3},{1,2},{2,1},{3,0},{4,7},{5,6},{6,5},{7,4},{8,9},{9,8},{10,11... | collective-permute-start | bytes 4718600 | tf_op jit(solution)/shard_map/ppermute | solution.py:76
  119.1 19.6 %collective-permute-start.11 = (bf16[192,4096]{1,0:T(8,128)(2,1)S(1)}, bf16[192,4096]{1,0:T(8,128)(2,1)S(1)}, u32[]{:S(2)}, u32[]{:S(2)}) collective-permute-start(bf16[192,4096]{1,0:T(8,128)(2,1)S(1)} %collective-permute-done.4.refs_2_.refs_6_.refs_10_), channel_id=1, source_target_pairs={{0,3},{1,2},{2,1},{3,0},{4,7},{5,6},{6,5},{7,4},{8,9},{9,8},{10,11... | collective-permute-start | bytes 4718600 | tf_op jit(solution)/shard_map/ppermute | solution.py:76
  120.2 30.4 %collective-permute-start.10 = (bf16[96,4096]{1,0:T(8,128)(2,1)S(1)}, bf16[96,4096]{1,0:T(8,128)(2,1)}, u32[]{:S(2)}, u32[]{:S(2)}) collective-permute-start(bf16[96,4096]{1,0:T(8,128)(2,1)S(1)} %copy-done.9), channel_id=1, source_target_pairs={{0,3},{1,2},{2,1},{3,0},{4,7},{5,6},{6,5},{7,4},{8,9},{9,8},{10,11... | collective-permute-start | bytes 2359304 | tf_op jit(solution)/shard_map/ppermute | solution.py:76
  120.6 30.0 %collective-permute-start.7 = (bf16[96,4096]{1,0:T(8,128)(2,1)S(1)}, bf16[96,4096]{1,0:T(8,128)(2,1)S(1)}, u32[]{:S(2)}, u32[]{:S(2)}) collective-permute-start(bf16[96,4096]{1,0:T(8,128)(2,1)S(1)} %copy-done.5), channel_id=1, source_target_pairs={{0,4},{1,5},{2,6},{3,7},{4,0},{5,1},{6,2},{7,3},{8,12},{9,13},{10,... | collective-permute-start | bytes 2359304 | tf_op jit(solution)/shard_map/ppermute | solution.py:80
  121.4 31.7 %collective-permute-start.8 = (bf16[96,4096]{1,0:T(8,128)(2,1)S(1)}, bf16[96,4096]{1,0:T(8,128)(2,1)}, u32[]{:S(2)}, u32[]{:S(2)}) collective-permute-start(bf16[96,4096]{1,0:T(8,128)(2,1)S(1)} %copy-done.9), channel_id=1, source_target_pairs={{0,4},{1,5},{2,6},{3,7},{4,0},{5,1},{6,2},{7,3},{8,12},{9,13},{10,... | collective-permute-start | bytes 2359304 | tf_op jit(solution)/shard_map/ppermute | solution.py:80
  122.1 33.6 %collective-permute-start.9 = (bf16[96,4096]{1,0:T(8,128)(2,1)S(1)}, bf16[96,4096]{1,0:T(8,128)(2,1)S(1)}, u32[]{:S(2)}, u32[]{:S(2)}) collective-permute-start(bf16[96,4096]{1,0:T(8,128)(2,1)S(1)} %copy-done.5), channel_id=1, source_target_pairs={{0,3},{1,2},{2,1},{3,0},{4,7},{5,6},{6,5},{7,4},{8,9},{9,8},{10,11... | collective-permute-start | bytes 2359304 | tf_op jit(solution)/shard_map/ppermute | solution.py:76
  155.7 11.7 %collective-permute-start.12 = (bf16[96,4096]{1,0:T(8,128)(2,1)S(1)}, bf16[96,4096]{1,0:T(8,128)(2,1)S(1)}, u32[]{:S(2)}, u32[]{:S(2)}) collective-permute-start(bf16[96,4096]{1,0:T(8,128)(2,1)S(1)} %collective-permute-done.7.refs_2_.refs_6_), channel_id=1, source_target_pairs={{0,3},{1,2},{2,1},{3,0},{4,7},{5,6},{6,5},{7,4},{8,9},{9,8},{10,11... | collective-permute-start | bytes 2359304 | tf_op jit(solution)/shard_map/ppermute | solution.py:76
  156.8 18.5 %collective-permute-start.13 = (bf16[96,4096]{1,0:T(8,128)(2,1)}, bf16[96,4096]{1,0:T(8,128)(2,1)S(1)}, u32[]{:S(2)}, u32[]{:S(2)}) collective-permute-start(bf16[96,4096]{1,0:T(8,128)(2,1)} %collective-permute-done.8.refs_6_.refs_14_), channel_id=1, source_target_pairs={{0,3},{1,2},{2,1},{3,0},{4,7},{5,6},{6,5},{7,4},{8,9},{9,8},{10,11... | collective-permute-start | bytes 2359304 | tf_op jit(solution)/shard_map/ppermute | solution.py:76
  165.1 21.8 %collective-permute-start.16 = (bf16[96,2176]{1,0:T(8,128)(2,1)}, bf16[96,2176]{1,0:T(8,128)(2,1)S(1)}, u32[]{:S(2)}, u32[]{:S(2)}) collective-permute-start(bf16[96,2176]{1,0:T(8,128)(2,1)} %get-tuple-element.146), channel_id=1, source_target_pairs={{0,3},{1,2},{2,1},{3,0},{4,7},{5,6},{6,5},{7,4},{8,9},{9,8},{10,11... | collective-permute-start | bytes 1253384 | tf_op jit(solution)/shard_map/ppermute | solution.py:76
  166.3 20.6 %collective-permute-start.17 = (bf16[96,2176]{1,0:T(8,128)(2,1)}, bf16[96,2176]{1,0:T(8,128)(2,1)S(1)}, u32[]{:S(2)}, u32[]{:S(2)}) collective-permute-start(bf16[96,2176]{1,0:T(8,128)(2,1)} %get-tuple-element.147), channel_id=1, source_target_pairs={{0,3},{1,2},{2,1},{3,0},{4,7},{5,6},{6,5},{7,4},{8,9},{9,8},{10,11... | collective-permute-start | bytes 1253384 | tf_op jit(solution)/shard_map/ppermute | solution.py:76
  166.6 20.2 %collective-permute-start.14 = (bf16[96,2048]{1,0:T(8,128)(2,1)}, bf16[96,2048]{1,0:T(8,128)(2,1)S(1)}, u32[]{:S(2)}, u32[]{:S(2)}) collective-permute-start(bf16[96,2048]{1,0:T(8,128)(2,1)} %get-tuple-element.143), channel_id=1, source_target_pairs={{0,4},{1,5},{2,6},{3,7},{4,0},{5,1},{6,2},{7,3},{8,12},{9,13},{10,... | collective-permute-start | bytes 1179656 | tf_op jit(solution)/shard_map/ppermute | solution.py:80
  167.4 19.4 %collective-permute-start.15 = (bf16[96,2048]{1,0:T(8,128)(2,1)}, bf16[96,2048]{1,0:T(8,128)(2,1)S(1)}, u32[]{:S(2)}, u32[]{:S(2)}) collective-permute-start(bf16[96,2048]{1,0:T(8,128)(2,1)} %get-tuple-element.144), channel_id=1, source_target_pairs={{0,4},{1,5},{2,6},{3,7},{4,0},{5,1},{6,2},{7,3},{8,12},{9,13},{10,... | collective-permute-start | bytes 1179656 | tf_op jit(solution)/shard_map/ppermute | solution.py:80
  202.1 33.3 %collective-permute-start.23 = (bf16[384,1152]{1,0:T(8,128)(2,1)}, bf16[384,1152]{1,0:T(8,128)(2,1)S(1)}, u32[]{:S(2)}, u32[]{:S(2)}) collective-permute-start(bf16[384,1152]{1,0:T(8,128)(2,1)} %pack_rows.2.refs_11_), channel_id=1, source_target_pairs={{0,1},{1,0},{2,3},{3,2},{4,5},{5,4},{6,7},{7,6},{8,11},{9,10},{10,... | collective-permute-start | bytes 2654216 | tf_op jit(solution)/shard_map/ppermute | solution.py:68
  208.6 26.8 %collective-permute-start.26 = (bf16[96,2176]{1,0:T(8,128)(2,1)S(1)}, bf16[96,2176]{1,0:T(8,128)(2,1)S(1)}, u32[]{:S(2)}, u32[]{:S(2)}) collective-permute-start(bf16[96,2176]{1,0:T(8,128)(2,1)S(1)} %copy-done.38), channel_id=1, source_target_pairs={{0,3},{1,2},{2,1},{3,0},{4,7},{5,6},{6,5},{7,4},{8,9},{9,8},{10,11... | collective-permute-start | bytes 1253384 | tf_op jit(solution)/shard_map/ppermute | solution.py:76
  210.3 25.0 %collective-permute-start.27 = (bf16[96,2176]{1,0:T(8,128)(2,1)S(1)}, bf16[96,2176]{1,0:T(8,128)(2,1)S(1)}, u32[]{:S(2)}, u32[]{:S(2)}) collective-permute-start(bf16[96,2176]{1,0:T(8,128)(2,1)S(1)} %copy-done.37), channel_id=1, source_target_pairs={{0,3},{1,2},{2,1},{3,0},{4,7},{5,6},{6,5},{7,4},{8,9},{9,8},{10,11... | collective-permute-start | bytes 1253384 | tf_op jit(solution)/shard_map/ppermute | solution.py:76
  221.1 14.2 %collective-permute-start.25 = (bf16[96,2048]{1,0:T(8,128)(2,1)S(1)}, bf16[96,2048]{1,0:T(8,128)(2,1)S(1)}, u32[]{:S(2)}, u32[]{:S(2)}) collective-permute-start(bf16[96,2048]{1,0:T(8,128)(2,1)S(1)} %copy-done.39), channel_id=1, source_target_pairs={{0,4},{1,5},{2,6},{3,7},{4,0},{5,1},{6,2},{7,3},{8,12},{9,13},{10,... | collective-permute-start | bytes 1179656 | tf_op jit(solution)/shard_map/ppermute | solution.py:80
  227.9 50.4 %collective-permute-start.33 = (bf16[192,4096]{1,0:T(8,128)(2,1)S(1)}, bf16[192,4096]{1,0:T(8,128)(2,1)}, u32[]{:S(2)}, u32[]{:S(2)}) collective-permute-start(bf16[192,4096]{1,0:T(8,128)(2,1)S(1)} %copy-done.12), channel_id=1, source_target_pairs={{0,1},{1,0},{2,3},{3,2},{4,5},{5,4},{6,7},{7,6},{8,11},{9,10},{10,... | collective-permute-start | bytes 4718600 | tf_op jit(solution)/shard_map/ppermute | solution.py:68
  235.6 22.9 %collective-permute-start.28 = (f32[1,4096]{1,0:T(1,128)S(1)}, f32[1,4096]{1,0:T(1,128)S(1)}, u32[]{:S(2)}, u32[]{:S(2)}) collective-permute-start(f32[1,4096]{1,0:T(1,128)S(1)} %add.53), channel_id=1, source_target_pairs={{0,16},{8,24},{16,0},{24,8},{32,48},{40,56},{48,32},{56,40},{64,80... | collective-permute-start | bytes 49160 | tf_op jit(solution)/shard_map/ppermute | solution.py:196
  238.7 33.0 %collective-permute-start.32 = (bf16[96,2176]{1,0:T(8,128)(2,1)S(1)}, bf16[96,2176]{1,0:T(8,128)(2,1)}, u32[]{:S(2)}, u32[]{:S(2)}) collective-permute-start(bf16[96,2176]{1,0:T(8,128)(2,1)S(1)} %add_convert_fusion.refs_21_), channel_id=1, source_target_pairs={{0,4},{1,5},{2,6},{3,7},{4,0},{5,1},{6,2},{7,3},{8,12},{9,13},{10,... | collective-permute-start | bytes 1253384 | tf_op jit(solution)/shard_map/ppermute | solution.py:80
  238.7 33.0 %collective-permute-start.31 = (bf16[96,2048]{1,0:T(8,128)(2,1)S(1)}, bf16[96,2048]{1,0:T(8,128)(2,1)}, u32[]{:S(2)}, u32[]{:S(2)}) collective-permute-start(bf16[96,2048]{1,0:T(8,128)(2,1)S(1)} %add_convert_fusion.2.refs_20_), channel_id=1, source_target_pairs={{0,3},{1,2},{2,1},{3,0},{4,7},{5,6},{6,5},{7,4},{8,9},{9,8},{10,11... | collective-permute-start | bytes 1179656 | tf_op jit(solution)/shard_map/ppermute | solution.py:76
  241.1 37.2 %all-to-all-start.2 = ((bf16[16,24,1152]{2,1,0:T(8,128)(2,1)}), bf16[16,24,1152]{2,1,0:T(8,128)(2,1)S(1)}, u32[]{:S(2)}, u32[]{:S(2)}) async-start(bf16[16,24,1152]{2,1,0:T(8,128)(2,1)} %bitcast.37), calls=%async_computation.2 | async-start | bytes 1769472 | tf_op jit(solution)/shard_map/all_to_all | solution.py:462
  248.6 38.9 %collective-permute-start.34 = (bf16[192,4096]{1,0:T(8,128)(2,1)}, bf16[192,4096]{1,0:T(8,128)(2,1)}, u32[]{:S(2)}, u32[]{:S(2)}) collective-permute-start(bf16[192,4096]{1,0:T(8,128)(2,1)} %expert_weights.5), channel_id=1, source_target_pairs={{0,1},{1,0},{2,3},{3,2},{4,5},{5,4},{6,7},{7,6},{8,11},{9,10},{10,... | collective-permute-start | bytes 4718600 | tf_op jit(solution)/shard_map/ppermute | solution.py:68
  273.0 35.2 %collective-permute-start.36 = (bf16[192,4096]{1,0:T(8,128)(2,1)}, bf16[192,4096]{1,0:T(8,128)(2,1)}, u32[]{:S(2)}, u32[]{:S(2)}) collective-permute-start(bf16[192,4096]{1,0:T(8,128)(2,1)} %expert_weights.7), channel_id=1, source_target_pairs={{0,1},{1,0},{2,3},{3,2},{4,5},{5,4},{6,7},{7,6},{8,11},{9,10},{10,... | collective-permute-start | bytes 4718600 | tf_op jit(solution)/shard_map/ppermute | solution.py:68
  278.3 21.8 %all-to-all-start.3 = ((bf16[16,24,1152]{2,1,0:T(8,128)(2,1)}), bf16[16,24,1152]{2,1,0:T(8,128)(2,1)S(1)}, u32[]{:S(2)}, u32[]{:S(2)}) async-start(bf16[16,24,1152]{2,1,0:T(8,128)(2,1)} %bitcast.34), calls=%async_computation.3 | async-start | bytes 1769472 | tf_op jit(solution)/shard_map/all_to_all | solution.py:462
  (50 other events, 451.1 us)

commit v4 on v3

--- a/solution.py
+++ b/solution.py
@@ -533,12 +533,13 @@
     take_d = trade(give_d)
     r_b, take_u = barrier(r_b, take_u)
     norm = jnp.sum(norm, axis=0)
-    out, grad_routes = combine(owns, r_b, r_a, h, c, gain, rrow, wrow)
-    grad_routes = grad_routes.reshape(TOK, 1)
     grads = [
         lax.dynamic_update_index_in_dim(x, t, 1 - mine, 0)
         for x, t in zip(mine_gud, (take_g, take_u, take_d))
     ]
+    r_b, *grads = barrier(r_b, *grads)
+    out, grad_routes = combine(owns, r_b, r_a, h, c, gain, rrow, wrow)
+    grad_routes = grad_routes.reshape(TOK, 1)
     return out, norm, grad_routes, *grads
 
 

time: 314 us -> 312 us (level)
    unnamed x82 -> x78, local copies, waits for them, and re-layouts: 8.97 us -> 5.74 us
  transfers between devices with their start and end apart: 41 -> 41, of which waited for: 13 -> 13; matrix products, arithmetic and copies ran while one was open for 5% -> 5% of each run, Pallas kernels for 27% -> 26%
where the time goes in v4:
time: 312 us; the launch traced here: 311 us
  waiting for transfers between devices  123 us (39%)
  Pallas kernels  89.7 us (29%)
  starting transfers between devices  70 us (22%)
  local copies, waits for them, and re-layouts  20.4 us (7%)
  other arithmetic  6.5 us (2%)
    ppermute x10, waiting for transfers between devices, over_z(): return lax.ppermute(x, AXES, PERMS['z'])  42.5 us
    all_to_all x4, waiting for transfers between devices, exchange(): got = lax.all_to_all(shaped, 'dp', split_axis=0, concat_axis=0, tiled=True)  32.9 us
    ppermute x13, waiting for transfers between devices, over_y(): return lax.ppermute(x, AXES, PERMS['y'])  30.6 us
    all_to_all x4, starting transfers between devices, exchange(): got = lax.all_to_all(shaped, 'dp', split_axis=0, concat_axis=0, tiled=True)  26.8 us
    pallas_call x4, Pallas kernels, expert_weights(): pl.pallas_call(functools.partial(weights_kernel, part, kinds), grid_spec=...  24 us
    pallas_call x2, Pallas kernels, forward(): pl.pallas_call(forward_kernel, grid_spec=pltpu.PrefetchScalarGridSpec(num...  21.3 us
    pallas_call x2, Pallas kernels, expert_rows(): pl.pallas_call(rows_kernel, grid_spec=pltpu.PrefetchScalarGridSpec(num_sc...  15.8 us
    ppermute x2, waiting for transfers between devices, trade_for(): lax.ppermute(x, 'tensor', [(t, move(core * 8 + t, 'trade') % 8) for t in...  15.4 us
  transfers between devices with their start and end apart: 41, of which 13 were waited for; matrix products, arithmetic and copies ran while one was open for 5% of the time, Pallas kernels for 26%

profile of v4, /device:TPU:1, one launch (start us, length us, event | category | flops | bytes accessed | tf_op | source)
XLA Modules:
  0.0 311.2 jit_solution(8220962059633673414)
XLA Ops:
  3.4 3.6 %collective-permute-start = (bf16[192,4096]{1,0:T(8,128)(2,1)}, bf16[192,4096]{1,0:T(8,128)(2,1)}, u32[]{:S(2)}, u32[]{:S(2)}) collective-permute-start(bf16[192,4096]{1,0:T(8,128)(2,1)} %dynamic-slice_bitcast_fusion.2), channel_id=1, source_target_pairs={{0,1},{1,0},{2,3},{3,2},{4,5},{5,4},{6,7},{7,6},{8,11},{9,10},{10,... | collective-permute-start | bytes 4718600 | tf_op jit(solution)/shard_map/ppermute | solution.py:68
  7.6 4.0 %dispatch.2 = (bf16[192,2048]{1,0:T(8,128)(2,1)}, bf16[192,2048]{1,0:T(8,128)(2,1)}) custom-call(s32[2]{0:T(128)} %pad_add_fusion.own_ref, bf16[128,4096]{1,0:T(8,128)(2,1)} %h_ref.4, bf16[128,4096]{1,0:T(8,128)(2,1)} %c_ref.5, f32[1,4096]{1,0:T(1,128)} %bitcast.38, s32[1,128]{1,0:T(1,128)} %bitcast.43, bf16[1,128]{1,0:T(2,128)(2,1)} %bitcast.46), custom_call_target="tpu_custom_call" | custom-call | flops 805306368 | bytes 4194304 | tf_op jit(solution)/shard_map/dispatch/pallas_call | solution.py:137
  11.6 4.1 %dispatch.3 = bf16[384,2048]{1,0:T(8,128)(2,1)} custom-call(s32[2]{0:T(128)} %pad_add_fusion.own_ref, bf16[128,4096]{1,0:T(8,128)(2,1)} %h_ref.4, bf16[128,4096]{1,0:T(8,128)(2,1)} %c_ref.5, f32[1,4096]{1,0:T(1,128)} %bitcast.39, s32[1,128]{1,0:T(1,128)} %bitcast.44, bf16[1,128]{1,0:T(2,128)(2,1)} %bitcast.47), custom_call_target="tpu_custom_call" | custom-call | flops 805306368 | bytes 4194304 | tf_op jit(solution)/shard_map/dispatch/pallas_call | solution.py:137
  15.6 8.0 %all-to-all-start = ((bf16[16,24,2048]{2,1,0:T(8,128)(2,1)}), bf16[16,24,2048]{2,1,0:T(8,128)(2,1)}, u32[]{:S(2)}, u32[]{:S(2)}) async-start(bf16[16,24,2048]{2,1,0:T(8,128)(2,1)} %bitcast.32), calls=%async_computation | async-start | bytes 3145728 | tf_op jit(solution)/shard_map/all_to_all | solution.py:462
  25.3 3.3 %dynamic-slice_bitcast_fusion = (bf16[192,4096]{1,0:T(8,128)(2,1)}, bf16[192,4096]{1,0:T(8,128)(2,1)}) fusion(bf16[2,192,4096]{2,1,0:T(8,128)(2,1)} %refs_10_.3, s32[]{:T(128)S(6)} %select_n.24, bf16[2,192,4096]{2,1,0:T(8,128)(2,1)S(1)} %copy-done.3), kind=kLoop, calls=%fused_computation.4 | loop fusion | bytes 6291460 | tf_op jit(solution)/shard_map/jit(dynamic_index_in_dim)/squeeze | solution.py:479
  28.7 15.4 %collective-permute-done.2 = bf16[192,2048]{1,0:T(8,128)(2,1)} collective-permute-done((bf16[192,2048]{1,0:T(8,128)(2,1)}, bf16[192,2048]{1,0:T(8,128)(2,1)}, u32[]{:S(2)}, u32[]{:S(2)}) %collective-permute-start.2) | collective-permute-done | bytes 786464 | tf_op jit(solution)/shard_map/ppermute | solution.py:72
  50.6 4.9 %all-to-all-start.1 = ((bf16[16,24,2048]{2,1,0:T(8,128)(2,1)}), bf16[16,24,2048]{2,1,0:T(8,128)(2,1)S(1)}, u32[]{:S(2)}, u32[]{:S(2)}) async-start(bf16[16,24,2048]{2,1,0:T(8,128)(2,1)} %bitcast.15), calls=%async_computation.1 | async-start | bytes 3145728 | tf_op jit(solution)/shard_map/all_to_all | solution.py:462
  56.8 3.7 %sort_rows.2 = (bf16[96,4096]{1,0:T(8,128)(2,1)}, bf16[96,4096]{1,0:T(8,128)(2,1)}) custom-call(bf16[384,384]{1,0:T(8,128)(2,1)} %constant.38.clone.m_ref, bf16[384,2048]{1,0:T(8,128)(2,1)} %bitcast.7.x_ref), custom_call_target="tpu_custom_call" | custom-call | flops 603979776 | bytes 4194304 | tf_op jit(solution)/shard_map/sort_rows/pallas_call | solution.py:165
  60.5 17.8 %all-to-all-done.1 = bf16[16,24,2048]{2,1,0:T(8,128)(2,1)S(1)} async-done(((bf16[16,24,2048]{2,1,0:T(8,128)(2,1)}), bf16[16,24,2048]{2,1,0:T(8,128)(2,1)S(1)}, u32[]{:S(2)}, u32[]{:S(2)}) %all-to-all-start.1) | async-done | bytes 1572896 | tf_op jit(solution)/shard_map/all_to_all | solution.py:462
  80.0 3.7 %sort_rows.3.refs_0_.refs_4_.refs_8_ = bf16[192,4096]{1,0:T(8,128)(2,1)} custom-call(bf16[384,384]{1,0:T(8,128)(2,1)} %constant.38.clone.m_ref, bf16[384,2048]{1,0:T(8,128)(2,1)} %bitcast.33), custom_call_target="tpu_custom_call" | custom-call | flops 603979776 | bytes 4194304 | tf_op jit(solution)/shard_map/sort_rows/pallas_call | solution.py:165
  85.6 33.4 %collective-permute-done.4.refs_2_.refs_6_.refs_10_ = bf16[192,4096]{1,0:T(8,128)(2,1)S(1)} collective-permute-done((bf16[192,4096]{1,0:T(8,128)(2,1)}, bf16[192,4096]{1,0:T(8,128)(2,1)S(1)}, u32[]{:S(2)}, u32[]{:S(2)}) %collective-permute-start.4) | collective-permute-done | bytes 1572896 | tf_op jit(solution)/shard_map/ppermute | solution.py:80
  123.1 15.5 %collective-permute-done.11.refs_3_.refs_7_.refs_11_ = bf16[192,4096]{1,0:T(8,128)(2,1)S(1)} collective-permute-done((bf16[192,4096]{1,0:T(8,128)(2,1)S(1)}, bf16[192,4096]{1,0:T(8,128)(2,1)S(1)}, u32[]{:S(2)}, u32[]{:S(2)}) %collective-permute-start.11) | collective-permute-done | bytes 1572896 | tf_op jit(solution)/shard_map/ppermute | solution.py:76
  139.8 10.6 %expert_forward.2 = (bf16[384,768]{1,0:T(8,128)(2,1)}, bf16[768,384]{1,0:T(8,128)(2,1)}, bf16[384,384]{1,0:T(8,128)(2,1)}, bf16[384,128]{1,0:T(8,128)(2,1)}) custom-call(s32[1]{0:T(128)} %bitcast.2.own_ref, bf16[192,4096]{1,0:T(8,128)(2,1)} %sort_rows.3.refs_0_.refs_4_.refs_8_, bf16[192,4096]{1,0:T(8,128)(2,1)} %copy-done.1, bf16[192,4096]{1,0:T(8,128)(2,1)} %copy-done, ...), custom_call_target="tpu_custom_call" | custom-call | flops 3623878656 | bytes 16777216 | tf_op jit(solution)/shard_map/expert_forward/pallas_call | solution.py:268
  157.1 7.9 %expert_rows.2 = (bf16[96,2048]{1,0:T(8,128)(2,1)}, bf16[96,2048]{1,0:T(8,128)(2,1)}, bf16[96,2048]{1,0:T(8,128)(2,1)}, bf16[96,2048]{1,0:T(8,128)(2,1)}, bf16[9...) custom-call(s32[1]{0:T(128)} %bitcast.2.own_ref, ...), custom_call_target="tpu_custom_call" | custom-call | flops 2415919104 | bytes 10485760 | tf_op jit(solution)/shard_map/expert_rows/pallas_call | solution.py:313
  168.1 7.1 %collective-permute-done.13.refs_7_.refs_15_ = bf16[96,4096]{1,0:T(8,128)(2,1)S(1)} collective-permute-done((bf16[96,4096]{1,0:T(8,128)(2,1)}, bf16[96,4096]{1,0:T(8,128)(2,1)S(1)}, u32[]{:S(2)}, u32[]{:S(2)}) %collective-permute-start.13) | collective-permute-done | bytes 786464 | tf_op jit(solution)/shard_map/ppermute | solution.py:76
  176.1 10.6 %expert_forward.3 = (bf16[384,768]{1,0:T(8,128)(2,1)}, bf16[768,384]{1,0:T(8,128)(2,1)}, bf16[384,384]{1,0:T(8,128)(2,1)}, bf16[384,128]{1,0:T(8,128)(2,1)}) custom-call(s32[1]{0:T(128)} %bitcast.2.own_ref, bf16[96,4096]{1,0:T(8,128)(2,1)} %get-tuple-element.132.refs_0_.refs_4_, bf16[96,4096]{1,0:T(8,128)(2,1)} %copy-done.7, bf16[96,4096]{1,0:T(8,128)(2,1)} %copy-done.6, ...), custom_call_target="tpu_custom_call" | custom-call | flops 3623878656 | bytes 16777216 | tf_op jit(solution)/shard_map/expert_forward/pallas_call | solution.py:268
  189.0 7.9 %expert_rows.3 = (bf16[96,2048]{1,0:T(8,128)(2,1)}, bf16[96,2048]{1,0:T(8,128)(2,1)}, bf16[96,2048]{1,0:T(8,128)(2,1)}, bf16[96,2048]{1,0:T(8,128)(2,1)}, bf16[9...) custom-call(s32[1]{0:T(128)} %bitcast.2.own_ref, ...), custom_call_target="tpu_custom_call" | custom-call | flops 2415919104 | bytes 10485760 | tf_op jit(solution)/shard_map/expert_rows/pallas_call | solution.py:313
  198.6 3.3 %pack_rows.2.refs_11_ = bf16[384,1152]{1,0:T(8,128)(2,1)} custom-call(bf16[384,384]{1,0:T(8,128)(2,1)} %constant.39.clone.m_ref, bf16[96,2048]{1,0:T(8,128)(2,1)} %get-tuple-element.174.refs_0_, bf16[96,2048]{1,0:T(8,128)(2,1)} %copy-done.25, bf16[96,2048]{1,0:T(8,128)(2,1)} %copy-done.26, bf16[96,2176]{1,0:T(8,128)(2,1)} %get-tuple-element.177.refs_3_, ...), custom_call_target="tpu_custom_call" | custom-call | flops 301989888 | bytes 4194304 | tf_op jit(solution)/shard_map/pack_rows/pallas_call | solution.py:417
  203.4 5.2 %collective-permute-start.20 = (f32[1,4096]{1,0:T(1,128)S(1)}, f32[1,4096]{1,0:T(1,128)S(1)}, u32[]{:S(2)}, u32[]{:S(2)}) collective-permute-start(f32[1,4096]{1,0:T(1,128)S(1)} %add_divide_fusion), channel_id=1, source_target_pairs={{0,8},{8,0},{16,24},{24,16},{32,40},{40,32},{48,56},{56,48},{64,72... | collective-permute-start | bytes 49160 | tf_op jit(solution)/shard_map/ppermute | solution.py:196
  211.0 5.1 %expert_weights.4.refs_10_ = bf16[192,4096]{1,0:T(8,128)(2,1)} custom-call(s32[1]{0:T(128)} %bitcast.2.own_ref, bf16[192,4096]{1,0:T(8,128)(2,1)} %sort_rows.3.refs_0_.refs_4_.refs_8_, bf16[192,4096]{1,0:T(8,128)(2,1)} %copy-done.1, bf16[192,4096]{1,0:T(8,128)(2,1)} %copy-done, bf16[192,4096]{1,0:T(8,128)(2,1)} %copy-done.2, ...), custom_call_target="tpu_custom_call" | custom-call | flops 1207959552 | bytes 6291456 | tf_op jit(solution)/shard_map/expert_weights/pallas_call | solution.py:366
  221.9 5.3 %expert_weights.5 = bf16[192,4096]{1,0:T(8,128)(2,1)} custom-call(s32[1]{0:T(128)} %bitcast.2.own_ref, bf16[192,4096]{1,0:T(8,128)(2,1)} %sort_rows.3.refs_0_.refs_4_.refs_8_, bf16[192,4096]{1,0:T(8,128)(2,1)} %copy-done.1, bf16[192,4096]{1,0:T(8,128)(2,1)} %copy-done, bf16[192,4096]{1,0:T(8,128)(2,1)} %copy-done.2, ...), custom_call_target="tpu_custom_call" | custom-call | flops 1207959552 | bytes 6291456 | tf_op jit(solution)/shard_map/expert_weights/pallas_call | solution.py:366
  229.5 5.9 %collective-permute-done.25.refs_1_ = bf16[96,2048]{1,0:T(8,128)(2,1)S(1)} collective-permute-done((bf16[96,2048]{1,0:T(8,128)(2,1)S(1)}, bf16[96,2048]{1,0:T(8,128)(2,1)S(1)}, u32[]{:S(2)}, u32[]{:S(2)}) %collective-permute-start.25) | collective-permute-done | bytes 393248 | tf_op jit(solution)/shard_map/ppermute | solution.py:80
  235.6 3.1 collective-permute-start.28
  241.1 7.4 %all-to-all-start.2 = ((bf16[16,24,1152]{2,1,0:T(8,128)(2,1)}), bf16[16,24,1152]{2,1,0:T(8,128)(2,1)S(1)}, u32[]{:S(2)}, u32[]{:S(2)}) async-start(bf16[16,24,1152]{2,1,0:T(8,128)(2,1)} %bitcast.37), calls=%async_computation.2 | async-start | bytes 1769472 | tf_op jit(solution)/shard_map/all_to_all | solution.py:462
  249.8 8.5 %expert_weights.6 = (bf16[2,192,4096]{2,1,0:T(8,128)(2,1)}, bf16[2,192,4096]{2,1,0:T(8,128)(2,1)}, bf16[2,192,4096]{2,1,0:T(8,128)(2,1)}) custom-call(s32[1]{0:T(128)} %bitcast.2.own_ref, bf16[192,4096]{1,0:T(8,128)(2,1)} %sort_rows.3.refs_0_.refs_4_.refs_8_, bf16[192,4096]{1,0:T(8,128)(2,1)} %copy-done.1, bf16[192,4096]{1,0:T(8,128)(2,1)} %copy-done, ...), custom_call_target="tpu_custom_call" | custom-call | flops 3623878656 | bytes 18874368 | tf_op jit(solution)/shard_map/expert_weights/pallas_call | solution.py:366
  259.1 5.0 %expert_weights.7 = bf16[192,4096]{1,0:T(8,128)(2,1)} custom-call(s32[1]{0:T(128)} %bitcast.2.own_ref, bf16[192,4096]{1,0:T(8,128)(2,1)} %sort_rows.3.refs_0_.refs_4_.refs_8_, bf16[192,4096]{1,0:T(8,128)(2,1)} %copy-done.1, bf16[192,4096]{1,0:T(8,128)(2,1)} %copy-done, bf16[192,4096]{1,0:T(8,128)(2,1)} %copy-done.2, ...), custom_call_target="tpu_custom_call" | custom-call | flops 1207959552 | bytes 6291456 | tf_op jit(solution)/shard_map/expert_weights/pallas_call | solution.py:366
  266.1 5.4 %collective-permute-done.30 = f32[8,4096]{1,0:T(8,128)S(1)} collective-permute-done((f32[8,4096]{1,0:T(8,128)S(1)}, f32[8,4096]{1,0:T(8,128)S(1)}, u32[]{:S(2)}, u32[]{:S(2)}) %collective-permute-start.30) | collective-permute-done | bytes 131104 | tf_op jit(solution)/shard_map/ppermute | solution.py:76
  274.3 3.3 %pack_rows.3 = bf16[384,1152]{1,0:T(8,128)(2,1)} custom-call(bf16[384,384]{1,0:T(8,128)(2,1)} %constant.39.clone.m_ref, bf16[96,2048]{1,0:T(8,128)(2,1)} %get-tuple-element.209.refs_10_.refs_0_, bf16[96,2048]{1,0:T(8,128)(2,1)} %copy-done.24, bf16[96,2048]{1,0:T(8,128)(2,1)} %collective-permute-done.31.refs_2_, bf16[96,2176]{1,0:T(8,128)(2,1)} %get-tuple-element.212.refs_3_, ...), custom_call_target="tpu_custom_call" | custom-call | flops 301989888 | bytes 4194304 | tf_op jit(solution)/shard_map/pack_rows/pallas_call | solution.py:417
  278.2 6.5 %all-to-all-start.3 = ((bf16[16,24,1152]{2,1,0:T(8,128)(2,1)}), bf16[16,24,1152]{2,1,0:T(8,128)(2,1)S(1)}, u32[]{:S(2)}, u32[]{:S(2)}) async-start(bf16[16,24,1152]{2,1,0:T(8,128)(2,1)} %bitcast.34), calls=%async_computation.3 | async-start | bytes 1769472 | tf_op jit(solution)/shard_map/all_to_all | solution.py:462
  287.4 12.6 %all-to-all-done.3 = bf16[16,24,1152]{2,1,0:T(8,128)(2,1)S(1)} async-done(((bf16[16,24,1152]{2,1,0:T(8,128)(2,1)}), bf16[16,24,1152]{2,1,0:T(8,128)(2,1)S(1)}, u32[]{:S(2)}, u32[]{:S(2)}) %all-to-all-start.3) | async-done | bytes 884768 | tf_op jit(solution)/shard_map/all_to_all | solution.py:462
  300.0 3.1 bitcast_dynamic-update-slice_fusion.1
  304.7 6.5 %combine.1 = (bf16[128,4096]{1,0:T(8,128)(2,1)}, f32[1,128]{1,0:T(1,128)}) custom-call(s32[2]{0:T(128)} %pad_add_fusion.own_ref, bf16[384,1152]{1,0:T(8,128)(2,1)} %bitcast.36, bf16[384,1152]{1,0:T(8,128)(2,1)} %bitcast.35, bf16[128,4096]{1,0:T(8,128)(2,1)} %h_ref.4, bf16[128,4096]{1,0:T(8,128)(2,1)} %c_ref.5, f32[1,4096]{1,0:T(1,128)} %bitcast.40, ...), custom_call_target="tpu_custom_call" | custom-call | flops 805306368 | bytes 5242880 | tf_op jit(solution)/shard_map/combine/pallas_call | solution.py:447
  (165 shorter events, 62.2 us)
Async XLA Ops:
  3.4 43.2 %collective-permute-start = (bf16[192,4096]{1,0:T(8,128)(2,1)}, bf16[192,4096]{1,0:T(8,128)(2,1)}, u32[]{:S(2)}, u32[]{:S(2)}) collective-permute-start(bf16[192,4096]{1,0:T(8,128)(2,1)} %dynamic-slice_bitcast_fusion.2), channel_id=1, source_target_pairs={{0,1},{1,0},{2,3},{3,2},{4,5},{5,4},{6,7},{7,6},{8,11},{9,10},{10,... | collective-permute-start | bytes 4718600 | tf_op jit(solution)/shard_map/ppermute | solution.py:68
  15.6 30.9 %all-to-all-start = ((bf16[16,24,2048]{2,1,0:T(8,128)(2,1)}), bf16[16,24,2048]{2,1,0:T(8,128)(2,1)}, u32[]{:S(2)}, u32[]{:S(2)}) async-start(bf16[16,24,2048]{2,1,0:T(8,128)(2,1)} %bitcast.32), calls=%async_computation | async-start | bytes 3145728 | tf_op jit(solution)/shard_map/all_to_all | solution.py:462
  23.6 20.4 %collective-permute-start.2 = (bf16[192,2048]{1,0:T(8,128)(2,1)}, bf16[192,2048]{1,0:T(8,128)(2,1)}, u32[]{:S(2)}, u32[]{:S(2)}) collective-permute-start(bf16[192,2048]{1,0:T(8,128)(2,1)} %get-tuple-element.120), channel_id=1, source_target_pairs={{0,3},{1,2},{2,1},{3,0},{4,7},{5,6},{6,5},{7,4},{8,11},{9,10},{10,... | collective-permute-start | bytes 2359304 | tf_op jit(solution)/shard_map/ppermute | solution.py:72
  24.9 19.2 %collective-permute-start.1 = (bf16[192,2048]{1,0:T(8,128)(2,1)}, bf16[192,2048]{1,0:T(8,128)(2,1)}, u32[]{:S(2)}, u32[]{:S(2)}) collective-permute-start(bf16[192,2048]{1,0:T(8,128)(2,1)} %get-tuple-element.119), channel_id=1, source_target_pairs={{0,1},{1,0},{2,3},{3,2},{4,5},{5,4},{6,7},{7,6},{8,9},{9,8},{10,11... | collective-permute-start | bytes 2359304 | tf_op jit(solution)/shard_map/ppermute | solution.py:72
  46.6 31.8 %collective-permute-start.3 = (bf16[192,4096]{1,0:T(8,128)(2,1)}, bf16[192,4096]{1,0:T(8,128)(2,1)S(1)}, u32[]{:S(2)}, u32[]{:S(2)}) collective-permute-start(bf16[192,4096]{1,0:T(8,128)(2,1)} %get-tuple-element.124), channel_id=1, source_target_pairs={{0,1},{1,0},{2,3},{3,2},{4,5},{5,4},{6,7},{7,6},{8,11},{9,10},{10,... | collective-permute-start | bytes 4718600 | tf_op jit(solution)/shard_map/ppermute | solution.py:68
  50.6 27.7 %all-to-all-start.1 = ((bf16[16,24,2048]{2,1,0:T(8,128)(2,1)}), bf16[16,24,2048]{2,1,0:T(8,128)(2,1)S(1)}, u32[]{:S(2)}, u32[]{:S(2)}) async-start(bf16[16,24,2048]{2,1,0:T(8,128)(2,1)} %bitcast.15), calls=%async_computation.1 | async-start | bytes 3145728 | tf_op jit(solution)/shard_map/all_to_all | solution.py:462
  55.5 30.1 %collective-permute-start.6 = (bf16[192,4096]{1,0:T(8,128)(2,1)}, bf16[192,4096]{1,0:T(8,128)(2,1)}, u32[]{:S(2)}, u32[]{:S(2)}) collective-permute-start(bf16[192,4096]{1,0:T(8,128)(2,1)} %get-tuple-element.131), channel_id=1, source_target_pairs={{0,1},{1,0},{2,3},{3,2},{4,5},{5,4},{6,7},{7,6},{8,11},{9,10},{10,... | collective-permute-start | bytes 4718600 | tf_op jit(solution)/shard_map/ppermute | solution.py:68
  83.8 35.3 %collective-permute-start.4 = (bf16[192,4096]{1,0:T(8,128)(2,1)}, bf16[192,4096]{1,0:T(8,128)(2,1)S(1)}, u32[]{:S(2)}, u32[]{:S(2)}) collective-permute-start(bf16[192,4096]{1,0:T(8,128)(2,1)} %sort_rows.3.refs_0_.refs_4_.refs_8_), channel_id=1, source_target_pairs={{0,4},{1,5},{2,6},{3,7},{4,0},{5,1},{6,2},{7,3},{8,12},{9,13},{10,... | collective-permute-start | bytes 4718600 | tf_op jit(solution)/shard_map/ppermute | solution.py:80
  84.5 34.5 %collective-permute-start.5 = (bf16[192,4096]{1,0:T(8,128)(2,1)}, bf16[192,4096]{1,0:T(8,128)(2,1)S(1)}, u32[]{:S(2)}, u32[]{:S(2)}) collective-permute-start(bf16[192,4096]{1,0:T(8,128)(2,1)} %sort_rows.3.refs_0_.refs_4_.refs_8_), channel_id=1, source_target_pairs={{0,3},{1,2},{2,1},{3,0},{4,7},{5,6},{6,5},{7,4},{8,9},{9,8},{10,11... | collective-permute-start | bytes 4718600 | tf_op jit(solution)/shard_map/ppermute | solution.py:76
  119.0 19.6 %collective-permute-start.11 = (bf16[192,4096]{1,0:T(8,128)(2,1)S(1)}, bf16[192,4096]{1,0:T(8,128)(2,1)S(1)}, u32[]{:S(2)}, u32[]{:S(2)}) collective-permute-start(bf16[192,4096]{1,0:T(8,128)(2,1)S(1)} %collective-permute-done.4.refs_2_.refs_6_.refs_10_), channel_id=1, source_target_pairs={{0,3},{1,2},{2,1},{3,0},{4,7},{5,6},{6,5},{7,4},{8,9},{9,8},{10,11... | collective-permute-start | bytes 4718600 | tf_op jit(solution)/shard_map/ppermute | solution.py:76
  120.2 30.3 %collective-permute-start.10 = (bf16[96,4096]{1,0:T(8,128)(2,1)S(1)}, bf16[96,4096]{1,0:T(8,128)(2,1)}, u32[]{:S(2)}, u32[]{:S(2)}) collective-permute-start(bf16[96,4096]{1,0:T(8,128)(2,1)S(1)} %copy-done.9), channel_id=1, source_target_pairs={{0,3},{1,2},{2,1},{3,0},{4,7},{5,6},{6,5},{7,4},{8,9},{9,8},{10,11... | collective-permute-start | bytes 2359304 | tf_op jit(solution)/shard_map/ppermute | solution.py:76
  120.6 29.9 %collective-permute-start.7 = (bf16[96,4096]{1,0:T(8,128)(2,1)S(1)}, bf16[96,4096]{1,0:T(8,128)(2,1)S(1)}, u32[]{:S(2)}, u32[]{:S(2)}) collective-permute-start(bf16[96,4096]{1,0:T(8,128)(2,1)S(1)} %copy-done.5), channel_id=1, source_target_pairs={{0,4},{1,5},{2,6},{3,7},{4,0},{5,1},{6,2},{7,3},{8,12},{9,13},{10,... | collective-permute-start | bytes 2359304 | tf_op jit(solution)/shard_map/ppermute | solution.py:80
  121.3 31.8 %collective-permute-start.8 = (bf16[96,4096]{1,0:T(8,128)(2,1)S(1)}, bf16[96,4096]{1,0:T(8,128)(2,1)}, u32[]{:S(2)}, u32[]{:S(2)}) collective-permute-start(bf16[96,4096]{1,0:T(8,128)(2,1)S(1)} %copy-done.9), channel_id=1, source_target_pairs={{0,4},{1,5},{2,6},{3,7},{4,0},{5,1},{6,2},{7,3},{8,12},{9,13},{10,... | collective-permute-start | bytes 2359304 | tf_op jit(solution)/shard_map/ppermute | solution.py:80
  122.0 33.6 %collective-permute-start.9 = (bf16[96,4096]{1,0:T(8,128)(2,1)S(1)}, bf16[96,4096]{1,0:T(8,128)(2,1)S(1)}, u32[]{:S(2)}, u32[]{:S(2)}) collective-permute-start(bf16[96,4096]{1,0:T(8,128)(2,1)S(1)} %copy-done.5), channel_id=1, source_target_pairs={{0,3},{1,2},{2,1},{3,0},{4,7},{5,6},{6,5},{7,4},{8,9},{9,8},{10,11... | collective-permute-start | bytes 2359304 | tf_op jit(solution)/shard_map/ppermute | solution.py:76
  155.6 11.7 %collective-permute-start.12 = (bf16[96,4096]{1,0:T(8,128)(2,1)S(1)}, bf16[96,4096]{1,0:T(8,128)(2,1)S(1)}, u32[]{:S(2)}, u32[]{:S(2)}) collective-permute-start(bf16[96,4096]{1,0:T(8,128)(2,1)S(1)} %collective-permute-done.7.refs_2_.refs_6_), channel_id=1, source_target_pairs={{0,3},{1,2},{2,1},{3,0},{4,7},{5,6},{6,5},{7,4},{8,9},{9,8},{10,11... | collective-permute-start | bytes 2359304 | tf_op jit(solution)/shard_map/ppermute | solution.py:76
  156.7 18.5 %collective-permute-start.13 = (bf16[96,4096]{1,0:T(8,128)(2,1)}, bf16[96,4096]{1,0:T(8,128)(2,1)S(1)}, u32[]{:S(2)}, u32[]{:S(2)}) collective-permute-start(bf16[96,4096]{1,0:T(8,128)(2,1)} %collective-permute-done.8.refs_6_.refs_14_), channel_id=1, source_target_pairs={{0,3},{1,2},{2,1},{3,0},{4,7},{5,6},{6,5},{7,4},{8,9},{9,8},{10,11... | collective-permute-start | bytes 2359304 | tf_op jit(solution)/shard_map/ppermute | solution.py:76
  165.0 21.7 %collective-permute-start.16 = (bf16[96,2176]{1,0:T(8,128)(2,1)}, bf16[96,2176]{1,0:T(8,128)(2,1)S(1)}, u32[]{:S(2)}, u32[]{:S(2)}) collective-permute-start(bf16[96,2176]{1,0:T(8,128)(2,1)} %get-tuple-element.150), channel_id=1, source_target_pairs={{0,3},{1,2},{2,1},{3,0},{4,7},{5,6},{6,5},{7,4},{8,9},{9,8},{10,11... | collective-permute-start | bytes 1253384 | tf_op jit(solution)/shard_map/ppermute | solution.py:76
  166.2 20.6 %collective-permute-start.17 = (bf16[96,2176]{1,0:T(8,128)(2,1)}, bf16[96,2176]{1,0:T(8,128)(2,1)S(1)}, u32[]{:S(2)}, u32[]{:S(2)}) collective-permute-start(bf16[96,2176]{1,0:T(8,128)(2,1)} %get-tuple-element.151), channel_id=1, source_target_pairs={{0,3},{1,2},{2,1},{3,0},{4,7},{5,6},{6,5},{7,4},{8,9},{9,8},{10,11... | collective-permute-start | bytes 1253384 | tf_op jit(solution)/shard_map/ppermute | solution.py:76
  166.6 20.2 %collective-permute-start.14 = (bf16[96,2048]{1,0:T(8,128)(2,1)}, bf16[96,2048]{1,0:T(8,128)(2,1)S(1)}, u32[]{:S(2)}, u32[]{:S(2)}) collective-permute-start(bf16[96,2048]{1,0:T(8,128)(2,1)} %get-tuple-element.147), channel_id=1, source_target_pairs={{0,4},{1,5},{2,6},{3,7},{4,0},{5,1},{6,2},{7,3},{8,12},{9,13},{10,... | collective-permute-start | bytes 1179656 | tf_op jit(solution)/shard_map/ppermute | solution.py:80
  167.3 19.5 %collective-permute-start.15 = (bf16[96,2048]{1,0:T(8,128)(2,1)}, bf16[96,2048]{1,0:T(8,128)(2,1)S(1)}, u32[]{:S(2)}, u32[]{:S(2)}) collective-permute-start(bf16[96,2048]{1,0:T(8,128)(2,1)} %get-tuple-element.148), channel_id=1, source_target_pairs={{0,4},{1,5},{2,6},{3,7},{4,0},{5,1},{6,2},{7,3},{8,12},{9,13},{10,... | collective-permute-start | bytes 1179656 | tf_op jit(solution)/shard_map/ppermute | solution.py:80
  201.9 33.4 %collective-permute-start.23 = (bf16[384,1152]{1,0:T(8,128)(2,1)}, bf16[384,1152]{1,0:T(8,128)(2,1)S(1)}, u32[]{:S(2)}, u32[]{:S(2)}) collective-permute-start(bf16[384,1152]{1,0:T(8,128)(2,1)} %pack_rows.2.refs_11_), channel_id=1, source_target_pairs={{0,1},{1,0},{2,3},{3,2},{4,5},{5,4},{6,7},{7,6},{8,11},{9,10},{10,... | collective-permute-start | bytes 2654216 | tf_op jit(solution)/shard_map/ppermute | solution.py:68
  208.6 26.8 %collective-permute-start.26 = (bf16[96,2176]{1,0:T(8,128)(2,1)S(1)}, bf16[96,2176]{1,0:T(8,128)(2,1)S(1)}, u32[]{:S(2)}, u32[]{:S(2)}) collective-permute-start(bf16[96,2176]{1,0:T(8,128)(2,1)S(1)} %copy-done.36), channel_id=1, source_target_pairs={{0,3},{1,2},{2,1},{3,0},{4,7},{5,6},{6,5},{7,4},{8,9},{9,8},{10,11... | collective-permute-start | bytes 1253384 | tf_op jit(solution)/shard_map/ppermute | solution.py:76
  210.3 25.0 %collective-permute-start.27 = (bf16[96,2176]{1,0:T(8,128)(2,1)S(1)}, bf16[96,2176]{1,0:T(8,128)(2,1)S(1)}, u32[]{:S(2)}, u32[]{:S(2)}) collective-permute-start(bf16[96,2176]{1,0:T(8,128)(2,1)S(1)} %copy-done.35), channel_id=1, source_target_pairs={{0,3},{1,2},{2,1},{3,0},{4,7},{5,6},{6,5},{7,4},{8,9},{9,8},{10,11... | collective-permute-start | bytes 1253384 | tf_op jit(solution)/shard_map/ppermute | solution.py:76
  221.1 14.2 %collective-permute-start.25 = (bf16[96,2048]{1,0:T(8,128)(2,1)S(1)}, bf16[96,2048]{1,0:T(8,128)(2,1)S(1)}, u32[]{:S(2)}, u32[]{:S(2)}) collective-permute-start(bf16[96,2048]{1,0:T(8,128)(2,1)S(1)} %copy-done.37), channel_id=1, source_target_pairs={{0,4},{1,5},{2,6},{3,7},{4,0},{5,1},{6,2},{7,3},{8,12},{9,13},{10,... | collective-permute-start | bytes 1179656 | tf_op jit(solution)/shard_map/ppermute | solution.py:80
  227.9 50.3 %collective-permute-start.33 = (bf16[192,4096]{1,0:T(8,128)(2,1)S(1)}, bf16[192,4096]{1,0:T(8,128)(2,1)}, u32[]{:S(2)}, u32[]{:S(2)}) collective-permute-start(bf16[192,4096]{1,0:T(8,128)(2,1)S(1)} %copy-done.12), channel_id=1, source_target_pairs={{0,1},{1,0},{2,3},{3,2},{4,5},{5,4},{6,7},{7,6},{8,11},{9,10},{10,... | collective-permute-start | bytes 4718600 | tf_op jit(solution)/shard_map/ppermute | solution.py:68
  235.6 22.7 %collective-permute-start.28 = (f32[1,4096]{1,0:T(1,128)S(1)}, f32[1,4096]{1,0:T(1,128)S(1)}, u32[]{:S(2)}, u32[]{:S(2)}) collective-permute-start(f32[1,4096]{1,0:T(1,128)S(1)} %add.53), channel_id=1, source_target_pairs={{0,16},{8,24},{16,0},{24,8},{32,48},{40,56},{48,32},{56,40},{64,80... | collective-permute-start | bytes 49160 | tf_op jit(solution)/shard_map/ppermute | solution.py:196
  238.7 32.9 %collective-permute-start.32 = (bf16[96,2176]{1,0:T(8,128)(2,1)S(1)}, bf16[96,2176]{1,0:T(8,128)(2,1)}, u32[]{:S(2)}, u32[]{:S(2)}) collective-permute-start(bf16[96,2176]{1,0:T(8,128)(2,1)S(1)} %add_convert_fusion.refs_21_), channel_id=1, source_target_pairs={{0,4},{1,5},{2,6},{3,7},{4,0},{5,1},{6,2},{7,3},{8,12},{9,13},{10,... | collective-permute-start | bytes 1253384 | tf_op jit(solution)/shard_map/ppermute | solution.py:80
  238.7 32.8 %collective-permute-start.31 = (bf16[96,2048]{1,0:T(8,128)(2,1)S(1)}, bf16[96,2048]{1,0:T(8,128)(2,1)}, u32[]{:S(2)}, u32[]{:S(2)}) collective-permute-start(bf16[96,2048]{1,0:T(8,128)(2,1)S(1)} %add_convert_fusion.2.refs_20_), channel_id=1, source_target_pairs={{0,3},{1,2},{2,1},{3,0},{4,7},{5,6},{6,5},{7,4},{8,9},{9,8},{10,11... | collective-permute-start | bytes 1179656 | tf_op jit(solution)/shard_map/ppermute | solution.py:76
  241.1 37.1 %all-to-all-start.2 = ((bf16[16,24,1152]{2,1,0:T(8,128)(2,1)}), bf16[16,24,1152]{2,1,0:T(8,128)(2,1)S(1)}, u32[]{:S(2)}, u32[]{:S(2)}) async-start(bf16[16,24,1152]{2,1,0:T(8,128)(2,1)} %bitcast.37), calls=%async_computation.2 | async-start | bytes 1769472 | tf_op jit(solution)/shard_map/all_to_all | solution.py:462
  248.6 38.8 %collective-permute-start.34 = (bf16[192,4096]{1,0:T(8,128)(2,1)}, bf16[192,4096]{1,0:T(8,128)(2,1)}, u32[]{:S(2)}, u32[]{:S(2)}) collective-permute-start(bf16[192,4096]{1,0:T(8,128)(2,1)} %expert_weights.5), channel_id=1, source_target_pairs={{0,1},{1,0},{2,3},{3,2},{4,5},{5,4},{6,7},{7,6},{8,11},{9,10},{10,... | collective-permute-start | bytes 4718600 | tf_op jit(solution)/shard_map/ppermute | solution.py:68
  273.0 30.1 %collective-permute-start.35 = (bf16[192,4096]{1,0:T(8,128)(2,1)}, bf16[192,4096]{1,0:T(8,128)(2,1)}, u32[]{:S(2)}, u32[]{:S(2)}) collective-permute-start(bf16[192,4096]{1,0:T(8,128)(2,1)} %expert_weights.7), channel_id=1, source_target_pairs={{0,1},{1,0},{2,3},{3,2},{4,5},{5,4},{6,7},{7,6},{8,11},{9,10},{10,... | collective-permute-start | bytes 4718600 | tf_op jit(solution)/shard_map/ppermute | solution.py:68
  278.2 21.8 %all-to-all-start.3 = ((bf16[16,24,1152]{2,1,0:T(8,128)(2,1)}), bf16[16,24,1152]{2,1,0:T(8,128)(2,1)S(1)}, u32[]{:S(2)}, u32[]{:S(2)}) async-start(bf16[16,24,1152]{2,1,0:T(8,128)(2,1)} %bitcast.34), calls=%async_computation.3 | async-start | bytes 1769472 | tf_op jit(solution)/shard_map/all_to_all | solution.py:462
  (48 other events, 450.8 us)
